TPU v7x, 32 devices: a whole 2x2x4 slice. The times are simulated.
32 devices in a mesh: dp: 8 (over z, x), fsdp: 4 (over y, core).
Axes of the slice: x: 2, y: 2, z: 4, core: 2. Of those that a mesh axis runs over, the one named last changes fastest.
Arguments:
- embed_table: float32 [768, 32128], P(('dp', 'fsdp')), may hold values from -6 to 6
- square_weights: float32 [5, 768, 768], P(None, 'dp', 'fsdp'), may hold values from -0.21875 to 0.21875
- expand_weight: float32 [768, 3072], P('dp', 'fsdp'), may hold values from -0.21875 to 0.21875
- reduce_weight: float32 [3072, 768], P('dp', 'fsdp'), may hold values from -0.109375 to 0.109375
- norm_gains: float32 [3, 768], P(None, ('dp', 'fsdp')), as said below
- position_bias: float32 [32, 12], replicated, may hold values from -6 to 6
- log_scale: float32 [1], replicated, may hold values from 3 to 3.4
- table_moment: float32 [768, 32128], P(('dp', 'fsdp')), may hold values from -3.8146973e-06 to 3.8146973e-06
- table_second: float32 [768, 32128], P(('dp', 'fsdp')), may hold values from 9.275199e-15 to 3.7100795e-14
- square_moment: float32 [5, 768, 768], P(None, 'dp', 'fsdp'), may hold values from -6.1035156e-05 to 6.1035156e-05
- square_second: float32 [5, 768, 768], P(None, 'dp', 'fsdp'), may hold values from 3.8646664e-12 to 6.183466e-11
- expand_moment: float32 [768, 3072], P('dp', 'fsdp'), may hold values from -6.1035156e-05 to 6.1035156e-05
- expand_second: float32 [768, 3072], P('dp', 'fsdp'), may hold values from 3.8646664e-12 to 6.183466e-11
- reduce_moment: float32 [3072, 768], P('dp', 'fsdp'), may hold values from -6.1035156e-05 to 6.1035156e-05
- reduce_second: float32 [3072, 768], P('dp', 'fsdp'), may hold values from 3.8646664e-12 to 6.183466e-11
- gains_moment: float32 [3, 768], P(None, ('dp', 'fsdp')), may hold values from -0.00030517578 to 0.00030517578
- gains_second: float32 [3, 768], P(None, ('dp', 'fsdp')), may hold values from 9.661665e-11 to 1.5458664e-09
- position_moment: float32 [32, 12], replicated, may hold values from -0.00030517578 to 0.00030517578
- position_second: float32 [32, 12], replicated, may hold values from 9.6616656e-12 to 1.5458665e-10
- scale_moment: float32 [1], replicated, may hold values from -0.00030517578 to 0.00030517578
- scale_second: float32 [1], replicated, may hold values from 9.661665e-11 to 1.5458664e-09
- query_tokens: int32 [128, 64], P(('dp', 'fsdp')), may hold values from 0 to 32127
- answer_tokens: int32 [128, 128], P(('dp', 'fsdp')), may hold values from 0 to 32127
- query_length: int32 [128], P(('dp', 'fsdp')), may hold values from 1 to 64, as said below
- answer_length: int32 [128], P(('dp', 'fsdp')), may hold values from 1 to 128, as said below
- premise_tokens: int32 [64, 64], P(('dp', 'fsdp')), may hold values from 0 to 32127
- hypothesis_tokens: int32 [64, 64], P(('dp', 'fsdp')), may hold values from 0 to 32127
- hard_negative: int32 [64], P(('dp', 'fsdp')), may hold values from 0 to 63
Outputs:
- moment_table: float32 [768, 32128], P(('dp', 'fsdp'))
- second_table: float32 [768, 32128], P(('dp', 'fsdp'))
- updated_table: float32 [768, 32128], P(('dp', 'fsdp'))
- moment_square: float32 [5, 768, 768], P(None, 'dp', 'fsdp')
- second_square: float32 [5, 768, 768], P(None, 'dp', 'fsdp')
- updated_square: float32 [5, 768, 768], P(None, 'dp', 'fsdp')
- moment_expand: float32 [768, 3072], P('dp', 'fsdp')
- second_expand: float32 [768, 3072], P('dp', 'fsdp')
- updated_expand: float32 [768, 3072], P('dp', 'fsdp')
- moment_reduce: float32 [3072, 768], P('dp', 'fsdp')
- second_reduce: float32 [3072, 768], P('dp', 'fsdp')
- updated_reduce: float32 [3072, 768], P('dp', 'fsdp')
- moment_gains: float32 [3, 768], P(None, ('dp', 'fsdp'))
- second_gains: float32 [3, 768], P(None, ('dp', 'fsdp'))
- updated_gains: float32 [3, 768], P(None, ('dp', 'fsdp'))
- moment_position: float32 [32, 12], replicated
- second_position: float32 [32, 12], replicated
- updated_position: float32 [32, 12], replicated
- moment_scale: float32 [1], replicated
- second_scale: float32 [1], replicated
- updated_scale: float32 [1], replicated
- losses: float32 [2], replicated
- gradient_norm: float32 [], replicated
Inputs may be any that keep to these rules, and one draw needn't show every extreme that they name: `query_length`: each query has 1 to 64 tokens; some query has all 64. `answer_length`: each answer has 1 to 128 tokens; some answer has all 128. `norm_gains`: gains positive.
All inputs are finite; a program needn't handle non-finite values.
Results may differ from a plain program's by a relative error of at most 0.013.
Values may be sent and summed in bfloat16 or wider, within the bound.
A program may use at most 576 MiB of HBM per device.

v0:
```python
import jax
import jax.numpy as jnp
import numpy as np
from jax import lax
from jax.sharding import PartitionSpec as P

D = 768
HEADS = 12
HEAD = 64
BUCKETS = 32
MAXDIST = 128
STEP = 10


HIGHEST = lax.Precision.HIGHEST
NORM_EPS = 1e-06
LEARN_RATE = 0.03
TABLE_RATE = 0.4
SMALL_RATE = 0.5
BETA_ONE = 0.9
BETA_TWO = 0.999
ADAM_EPS = 1e-08
WEIGHT_DECAY = 0.01
CLIP_NORM = 0.5


def bucket_table(length):
    places = np.arange(length)
    offset = places[None, :] - places[:, None]
    half_count = BUCKETS // 2
    exact_count = half_count // 2
    upper = (offset > 0).astype(np.int64) * half_count
    distance = np.abs(offset)
    far_bucket = exact_count + (
        np.log(np.maximum(distance, 1) / exact_count)
        / np.log(MAXDIST / exact_count)
        * (half_count - exact_count)
    ).astype(np.int64)
    far_bucket = np.minimum(far_bucket, half_count - 1)
    return (upper + np.where(distance < exact_count, distance, far_bucket)).astype(np.int32)


def bucket_onehot(length):
    flat_table = bucket_table(length).reshape(-1)
    return jnp.asarray((flat_table[:, None] == np.arange(BUCKETS)[None, :]).astype(np.float32))


def product(left, right):
    return jnp.dot(left, right, preferred_element_type=jnp.float32)


def product_left(left, right):
    return lax.dot_general(
        left, right, (((0,), (0,)), ((), ())), preferred_element_type=jnp.float32
    )


def product_right(left, right):
    return lax.dot_general(
        left, right, (((1,), (1,)), ((), ())), preferred_element_type=jnp.float32
    )


def norm_scale(values):
    return lax.rsqrt(jnp.mean(values * values, axis=-1, keepdims=True) + NORM_EPS)


def norm_back(values, scale, gain, grad):
    weighted = grad * gain
    inner = jnp.mean(weighted * values, axis=-1, keepdims=True)
    return (scale * weighted - values * scale**3 * inner, jnp.sum(grad * values * scale, axis=0))


def attention_bias(position_bias, length):
    onehot = bucket_onehot(length)
    flat_bias = jnp.dot(onehot, position_bias, precision=HIGHEST)
    return (jnp.transpose(flat_bias.reshape(length, length, HEADS), (2, 0, 1)), onehot)


def attention_scores(queries, keys_here, bias_table, key_mask):
    scores = (
        jnp.einsum("bqhe,bkhe->bhqk", queries, keys_here, preferred_element_type=jnp.float32)
        * HEAD ** (-0.5)
        + bias_table[None]
    )
    return jnp.where(key_mask[:, None, None, :], scores, -1e30)


def layer_forward(start_rows, key_mask, layer, length):
    square_low, expand_low, reduce_low, gain_rows, position_bias = layer
    head_shape = (key_mask.shape[0], length, HEADS, HEAD)
    scale_one = norm_scale(start_rows)
    normed_one = (start_rows * scale_one * gain_rows[0]).astype(jnp.bfloat16)
    queries = product(normed_one, square_low[0]).astype(jnp.bfloat16)
    keys_here = product(normed_one, square_low[1]).astype(jnp.bfloat16)
    values_here = product(normed_one, square_low[2]).astype(jnp.bfloat16)
    bias_table, onehot = attention_bias(position_bias, length)
    scores = attention_scores(
        queries.reshape(head_shape), keys_here.reshape(head_shape), bias_table, key_mask
    )
    row_top = jnp.max(scores, axis=-1, keepdims=True)
    raised = jnp.exp(scores - row_top)
    row_total = jnp.sum(raised, axis=-1, keepdims=True)
    log_total = row_top + jnp.log(row_total)
    attend = (raised / row_total).astype(jnp.bfloat16)
    mixed_heads = (
        jnp.einsum(
            "bhqk,bkhe->bqhe",
            attend,
            values_here.reshape(head_shape),
            preferred_element_type=jnp.float32,
        )
        .reshape(-1, D)
        .astype(jnp.bfloat16)
    )
    middle = start_rows + product(mixed_heads, square_low[3])
    scale_two = norm_scale(middle)
    normed_two = (middle * scale_two * gain_rows[1]).astype(jnp.bfloat16)
    hidden_pre = product(normed_two, expand_low)
    hidden_act = jax.nn.gelu(hidden_pre).astype(jnp.bfloat16)
    ending = middle + product(hidden_act, reduce_low)
    scale_three = norm_scale(ending)
    output = ending * scale_three * gain_rows[2]
    stored = (
        start_rows,
        scale_one,
        normed_one,
        queries,
        keys_here,
        values_here,
        log_total,
        mixed_heads,
        middle,
        scale_two,
        normed_two,
        hidden_pre,
        hidden_act,
        ending,
        scale_three,
    )
    return (output, stored)


def layer_backward(grad_out, key_mask, layer, stored, length):
    square_low, expand_low, reduce_low, gain_rows, position_bias = layer
    (
        start_rows,
        scale_one,
        normed_one,
        queries,
        keys_here,
        values_here,
        log_total,
        mixed_heads,
        middle,
        scale_two,
        normed_two,
        hidden_pre,
        hidden_act,
        ending,
        scale_three,
    ) = stored
    head_shape = (key_mask.shape[0], length, HEADS, HEAD)
    grad_end, gain_three = norm_back(ending, scale_three, gain_rows[2], grad_out)
    grad_end_low = grad_end.astype(jnp.bfloat16)
    grad_reduce = product_left(hidden_act, grad_end_low)
    grad_act = product_right(grad_end_low, reduce_low)
    grad_pre = jax.vjp(jax.nn.gelu, hidden_pre)[1](grad_act)[0].astype(jnp.bfloat16)
    grad_expand = product_left(normed_two, grad_pre)
    grad_normed_two = product_right(grad_pre, expand_low)
    grad_mid_norm, gain_two = norm_back(middle, scale_two, gain_rows[1], grad_normed_two)
    grad_middle = grad_end + grad_mid_norm
    grad_mid_low = grad_middle.astype(jnp.bfloat16)
    grad_output_proj = product_left(mixed_heads, grad_mid_low)
    grad_mixed = product_right(grad_mid_low, square_low[3]).astype(jnp.bfloat16).reshape(head_shape)
    bias_table, onehot = attention_bias(position_bias, length)
    query_heads = queries.reshape(head_shape)
    key_heads = keys_here.reshape(head_shape)
    value_heads = values_here.reshape(head_shape)
    scores = attention_scores(query_heads, key_heads, bias_table, key_mask)
    attend_full = jnp.exp(scores - log_total)
    attend = attend_full.astype(jnp.bfloat16)
    grad_attend = jnp.einsum(
        "bqhe,bkhe->bhqk", grad_mixed, value_heads, preferred_element_type=jnp.float32
    )
    grad_values = (
        jnp.einsum("bhqk,bqhe->bkhe", attend, grad_mixed, preferred_element_type=jnp.float32)
        .astype(jnp.bfloat16)
        .reshape(-1, D)
    )
    grad_scores = attend_full * (
        grad_attend - jnp.sum(grad_attend * attend_full, axis=-1, keepdims=True)
    )
    grad_scores_low = grad_scores.astype(jnp.bfloat16)
    grad_queries = (
        (
            jnp.einsum(
                "bhqk,bkhe->bqhe", grad_scores_low, key_heads, preferred_element_type=jnp.float32
            )
            * HEAD ** (-0.5)
        )
        .astype(jnp.bfloat16)
        .reshape(-1, D)
    )
    grad_keys = (
        (
            jnp.einsum(
                "bhqk,bqhe->bkhe", grad_scores_low, query_heads, preferred_element_type=jnp.float32
            )
            * HEAD ** (-0.5)
        )
        .astype(jnp.bfloat16)
        .reshape(-1, D)
    )
    summed_scores = jnp.sum(grad_scores_low.astype(jnp.float32), axis=0).reshape(
        HEADS, length * length
    )
    grad_position = lax.dot_general(
        onehot, summed_scores, (((0,), (1,)), ((), ())), precision=HIGHEST
    )
    grad_normed_one = (
        product_right(grad_queries, square_low[0])
        + product_right(grad_keys, square_low[1])
        + product_right(grad_values, square_low[2])
    )
    grad_start_norm, gain_one = norm_back(start_rows, scale_one, gain_rows[0], grad_normed_one)
    grad_start = grad_middle + grad_start_norm
    grad_squares = jnp.stack(
        [
            product_left(normed_one, grad_queries),
            product_left(normed_one, grad_keys),
            product_left(normed_one, grad_values),
            grad_output_proj,
        ]
    )
    return (
        grad_start,
        (
            grad_squares,
            grad_expand,
            grad_reduce,
            jnp.stack([gain_one, gain_two, gain_three]),
            grad_position,
        ),
    )


def contrast_local(left_low, right_low, scale, extra, target):
    sims = product_right(left_low, right_low)
    logits = scale * sims
    row_top = jnp.max(logits, axis=1, keepdims=True)
    raised = (1.0 + extra) * jnp.exp(logits - row_top)
    row_total = jnp.sum(raised, axis=1, keepdims=True)
    spread = row_top[:, 0] + jnp.log(row_total[:, 0])
    target_hit = jnp.arange(right_low.shape[0])[None, :] == target[:, None]
    loss_sum = jnp.sum(spread - jnp.sum(jnp.where(target_hit, logits, 0.0), axis=1))
    grad_logits = raised / row_total - target_hit.astype(jnp.float32)
    grad_scale = jnp.sum(grad_logits * sims)
    grad_sims = (scale * grad_logits).astype(jnp.bfloat16)
    return (loss_sum, grad_scale, product(grad_sims, right_low), product_left(grad_sims, left_low))


def pool_rows(output, key_mask, lengths, length):
    shaped = output.reshape(key_mask.shape[0], length, D)
    return jnp.sum(jnp.where(key_mask[:, :, None], shaped, 0.0), axis=1) / lengths[:, None].astype(
        jnp.float32
    )


def spread_rows(grad_rows, key_mask, lengths):
    spread = jnp.where(key_mask[:, :, None], grad_rows[:, None, :], 0.0) / lengths[
        :, None, None
    ].astype(jnp.float32)
    return spread.reshape(-1, D)


def adam_update(weight, moment, second, grad, factor, rate):
    clipped = grad * factor
    moment_new = BETA_ONE * moment + (1 - BETA_ONE) * clipped
    second_new = BETA_TWO * second + (1 - BETA_TWO) * clipped * clipped
    moment_hat = moment_new / (1 - BETA_ONE**STEP)
    second_hat = second_new / (1 - BETA_TWO**STEP)
    updated = weight - rate * (
        moment_hat / (jnp.sqrt(second_hat) + ADAM_EPS) + WEIGHT_DECAY * weight
    )
    return (moment_new, second_new, updated)


def shards(
    embed_table,
    square_weights,
    expand_weight,
    reduce_weight,
    norm_gains,
    position_bias,
    log_scale,
    table_moment,
    table_second,
    square_moment,
    square_second,
    expand_moment,
    expand_second,
    reduce_moment,
    reduce_second,
    gains_moment,
    gains_second,
    position_moment,
    position_second,
    scale_moment,
    scale_second,
    query_tokens,
    answer_tokens,
    query_length,
    answer_length,
    premise_tokens,
    hypothesis_tokens,
    hard_negative,
):

    def gather_layer():
        wide_parts = (
            lax.all_gather(square_weights.astype(jnp.bfloat16), "fsdp", axis=2, tiled=True),
            lax.all_gather(expand_weight.astype(jnp.bfloat16), "fsdp", axis=1, tiled=True),
            lax.all_gather(reduce_weight.astype(jnp.bfloat16), "fsdp", axis=1, tiled=True),
            lax.all_gather(norm_gains.astype(jnp.bfloat16), "fsdp", axis=1, tiled=True),
        )
        full_parts = (
            lax.all_gather(wide_parts[0], "dp", axis=1, tiled=True),
            lax.all_gather(wide_parts[1], "dp", axis=0, tiled=True),
            lax.all_gather(wide_parts[2], "dp", axis=0, tiled=True),
            lax.all_gather(wide_parts[3], "dp", axis=1, tiled=True),
        )
        return (
            full_parts[0],
            full_parts[1],
            full_parts[2],
            full_parts[3].astype(jnp.float32),
            position_bias,
        )

    layer = gather_layer()
    query_rows = query_tokens.shape[0]
    nli_rows = premise_tokens.shape[0]
    short_length = query_tokens.shape[1]
    long_length = answer_tokens.shape[1]
    vocab_size = embed_table.shape[1]
    count_rows = lax.axis_size("dp")
    count_cols = lax.axis_size("fsdp")
    short_tokens = jnp.concatenate([query_tokens, premise_tokens, hypothesis_tokens], axis=0)
    short_lengths = jnp.concatenate(
        [query_length, jnp.full((2 * nli_rows,), short_length, jnp.int32)]
    )
    all_tokens = jnp.concatenate([short_tokens.reshape(-1), answer_tokens.reshape(-1)])
    table_low = embed_table.astype(jnp.bfloat16)
    chosen = jnp.take(
        lax.all_gather(table_low, ("dp", "fsdp"), axis=0, tiled=True), all_tokens, axis=1
    ).astype(jnp.float32)
    embedded = chosen.T
    split_at = short_tokens.shape[0] * short_length
    short_mask = jnp.arange(short_length)[None, :] < short_lengths[:, None]
    long_mask = jnp.arange(long_length)[None, :] < answer_length[:, None]
    short_out, short_stored = layer_forward(embedded[:split_at], short_mask, layer, short_length)
    long_out, long_stored = layer_forward(embedded[split_at:], long_mask, layer, long_length)
    pooled = jnp.concatenate(
        [
            pool_rows(short_out, short_mask, short_lengths, short_length),
            pool_rows(long_out, long_mask, answer_length, long_length),
        ],
        axis=0,
    )
    pooled_low = pooled.astype(jnp.bfloat16)
    projected = product(pooled_low, layer[0][4])
    inverse = lax.rsqrt(jnp.sum(projected * projected, axis=-1, keepdims=True) + NORM_EPS)
    embeds = projected * inverse
    embeds_low = embeds.astype(jnp.bfloat16)
    hypo_start = query_rows + nli_rows
    answer_start = query_rows + 2 * nli_rows
    gathered = (
        lax.all_gather(embeds_low[answer_start:], ("dp", "fsdp"), axis=0, tiled=True),
        lax.all_gather(embeds_low[hypo_start:answer_start], ("dp", "fsdp"), axis=0, tiled=True),
    )
    scale = jnp.exp(log_scale[0])
    position = lax.axis_index(("dp", "fsdp"))
    first_loss, first_dscale, grad_queries, grad_answers = contrast_local(
        embeds_low[:query_rows],
        gathered[0],
        scale,
        0.0,
        position * query_rows + jnp.arange(query_rows),
    )
    negatives = (jnp.arange(gathered[1].shape[0])[None, :] == hard_negative[:, None]).astype(
        jnp.float32
    )
    second_loss, second_dscale, grad_premises, grad_hypotheses = contrast_local(
        embeds_low[query_rows:hypo_start],
        gathered[1],
        scale,
        negatives,
        position * nli_rows + jnp.arange(nli_rows),
    )
    back_parts = (
        lax.psum_scatter(grad_answers, ("dp", "fsdp"), scatter_dimension=0, tiled=True),
        lax.psum_scatter(grad_hypotheses, ("dp", "fsdp"), scatter_dimension=0, tiled=True),
    )
    grad_embeds = jnp.concatenate(
        [grad_queries, grad_premises, back_parts[1], back_parts[0]], axis=0
    )
    grad_projected = (
        inverse * (grad_embeds - embeds * jnp.sum(grad_embeds * embeds, axis=-1, keepdims=True))
    ).astype(jnp.bfloat16)
    grad_proj_weight = product_left(pooled_low, grad_projected)
    grad_pooled = product_right(grad_projected, layer[0][4])
    short_rows = short_tokens.shape[0]
    back_layer = gather_layer()
    grad_short_start, short_grads = layer_backward(
        spread_rows(grad_pooled[:short_rows], short_mask, short_lengths),
        short_mask,
        back_layer,
        short_stored,
        short_length,
    )
    grad_long_start, long_grads = layer_backward(
        spread_rows(grad_pooled[short_rows:], long_mask, answer_length),
        long_mask,
        back_layer,
        long_stored,
        long_length,
    )
    grad_squares = jnp.concatenate([short_grads[0] + long_grads[0], grad_proj_weight[None]], axis=0)
    grad_expand = short_grads[1] + long_grads[1]
    grad_reduce = short_grads[2] + long_grads[2]
    grad_gains = short_grads[3] + long_grads[3]
    grad_position = short_grads[4] + long_grads[4]
    grad_scale = ((first_dscale + second_dscale) * scale).reshape(1)
    grad_tokens = jnp.concatenate([grad_short_start, grad_long_start], axis=0)
    grad_table = lax.psum_scatter(
        jax.ops.segment_sum(grad_tokens, all_tokens, num_segments=vocab_size).T,
        ("dp", "fsdp"),
        scatter_dimension=0,
        tiled=True,
    )
    gains_four = grad_gains.reshape(3, count_rows, count_cols, -1)
    rows_part = (
        lax.psum_scatter(grad_squares, "dp", scatter_dimension=1, tiled=True),
        lax.psum_scatter(grad_expand, "dp", scatter_dimension=0, tiled=True),
        lax.psum_scatter(grad_reduce, "dp", scatter_dimension=0, tiled=True),
        lax.psum_scatter(gains_four, "dp", scatter_dimension=1, tiled=True),
    )
    reduced = (
        lax.psum_scatter(rows_part[0], "fsdp", scatter_dimension=2, tiled=True),
        lax.psum_scatter(rows_part[1], "fsdp", scatter_dimension=1, tiled=True),
        lax.psum_scatter(rows_part[2], "fsdp", scatter_dimension=1, tiled=True),
        lax.psum_scatter(rows_part[3], "fsdp", scatter_dimension=2, tiled=True),
    )
    grad_gain_shard = reduced[3].reshape(3, -1)
    local_square = (
        jnp.sum(reduced[0] * reduced[0])
        + jnp.sum(reduced[1] * reduced[1])
        + jnp.sum(reduced[2] * reduced[2])
        + jnp.sum(grad_gain_shard * grad_gain_shard)
        + jnp.sum(grad_table * grad_table)
    )
    summed = lax.psum(
        (grad_position, grad_scale, jnp.stack([first_loss, second_loss]), local_square),
        ("dp", "fsdp"),
    )
    position_total, scale_total, losses, square_total = summed
    gradient_norm = jnp.sqrt(
        square_total + jnp.sum(position_total * position_total) + jnp.sum(scale_total * scale_total)
    )
    factor = jnp.minimum(1.0, CLIP_NORM / gradient_norm)
    table_out = adam_update(embed_table, table_moment, table_second, grad_table, factor, TABLE_RATE)
    square_out = adam_update(
        square_weights, square_moment, square_second, reduced[0], factor, LEARN_RATE
    )
    expand_out = adam_update(
        expand_weight, expand_moment, expand_second, reduced[1], factor, LEARN_RATE
    )
    reduce_out = adam_update(
        reduce_weight, reduce_moment, reduce_second, reduced[2], factor, LEARN_RATE
    )
    gains_out = adam_update(
        norm_gains, gains_moment, gains_second, grad_gain_shard, factor, SMALL_RATE
    )
    position_out = adam_update(
        position_bias, position_moment, position_second, position_total, factor, SMALL_RATE
    )
    scale_out = adam_update(log_scale, scale_moment, scale_second, scale_total, factor, SMALL_RATE)
    return (
        table_out[0],
        table_out[1],
        table_out[2],
        square_out[0],
        square_out[1],
        square_out[2],
        expand_out[0],
        expand_out[1],
        expand_out[2],
        reduce_out[0],
        reduce_out[1],
        reduce_out[2],
        gains_out[0],
        gains_out[1],
        gains_out[2],
        position_out[0],
        position_out[1],
        position_out[2],
        scale_out[0],
        scale_out[1],
        scale_out[2],
        losses,
        gradient_norm,
    )


def solution(mesh):
    return jax.shard_map(
        shards,
        mesh=mesh,
        in_specs=(
            P(("dp", "fsdp"), None),
            P(None, "dp", "fsdp"),
            P("dp", "fsdp"),
            P("dp", "fsdp"),
            P(None, ("dp", "fsdp")),
            P(),
            P(),
            P(("dp", "fsdp"), None),
            P(("dp", "fsdp"), None),
            P(None, "dp", "fsdp"),
            P(None, "dp", "fsdp"),
            P("dp", "fsdp"),
            P("dp", "fsdp"),
            P("dp", "fsdp"),
            P("dp", "fsdp"),
            P(None, ("dp", "fsdp")),
            P(None, ("dp", "fsdp")),
            P(),
            P(),
            P(),
            P(),
            P(("dp", "fsdp"), None),
            P(("dp", "fsdp"), None),
            P(("dp", "fsdp")),
            P(("dp", "fsdp")),
            P(("dp", "fsdp"), None),
            P(("dp", "fsdp"), None),
            P(("dp", "fsdp")),
        ),
        out_specs=(
            P(("dp", "fsdp"), None),
            P(("dp", "fsdp"), None),
            P(("dp", "fsdp"), None),
            P(None, "dp", "fsdp"),
            P(None, "dp", "fsdp"),
            P(None, "dp", "fsdp"),
            P("dp", "fsdp"),
            P("dp", "fsdp"),
            P("dp", "fsdp"),
            P("dp", "fsdp"),
            P("dp", "fsdp"),
            P("dp", "fsdp"),
            P(None, ("dp", "fsdp")),
            P(None, ("dp", "fsdp")),
            P(None, ("dp", "fsdp")),
            P(),
            P(),
            P(),
            P(),
            P(),
            P(),
            P(),
            P(),
        ),
        check_vma=False,
    )
```

profile of v0, /device:TPU:15, one launch (start us, length us, event | category | flops | bytes accessed | tf_op | source)
XLA Modules:
  0.0 3017.8 jit_solution(3374028535371128900)
XLA Ops:
  10.8 13.1 all_gather.44
  25.6 11.8 all_gather.46
  37.5 8.1 all_gather.48
  51.0 11.3 all-gather.1
  70.5 210.5 %all-gather.9.cloned.1.call-done = bf16[768,32128]{1,0:T(8,128)(2,1)} async-done(((bf16[24,32128]{1,0:T(8,128)(2,1)}), bf16[768,32128]{1,0:T(8,128)(2,1)}) %all-gather.9.cloned.1.call-update) | async-done | bytes 49348624 | tf_op jit(solution)/shard_map/all_gather | solution.py:356
  281.0 62.2 %copy.473 = bf16[768,32128]{0,1:T(8,128)(2,1)} copy(bf16[768,32128]{1,0:T(8,128)(2,1)} %all-gather.9.cloned.1.call-done) | data formatting | bytes 98697216 | tf_op jit(solution)/shard_map/all_gather | solution.py:356
  343.2 18.2 gather_fusion
  366.3 9.0 all-gather.11.cloned.1.call-done
  409.2 46.7 %all-gather.13.cloned.1.call-done = bf16[768,3072]{1,0:T(8,128)(2,1)} async-done(((bf16[96,3072]{1,0:T(8,128)(2,1)}), bf16[768,3072]{1,0:T(8,128)(2,1)}) %all-gather.13.cloned.1.call-update) | async-done | bytes 4718608 | tf_op jit(solution)/shard_map/all_gather | solution.py:329
  455.9 8.2 fusion.118
  464.1 72.6 %all-gather.15.cloned.1.call-done = bf16[3072,768]{0,1:T(8,128)(2,1)} async-done(((bf16[384,768]{0,1:T(8,128)(2,1)}), bf16[3072,768]{0,1:T(8,128)(2,1)}) %all-gather.15.cloned.1.call-update) | async-done | bytes 4718608 | tf_op jit(solution)/shard_map/all_gather | solution.py:330
  536.7 9.2 multiply_reduce_fusion.15
  597.3 34.8 %all-gather.2 = bf16[32,4,768]{2,1,0:T(4,128)(2,1)} all-gather(bf16[1,4,768]{2,1,0:T(4,128)(2,1)S(1)} %slice_bitcast_fusion.24), channel_id=1, replica_groups=mesh['dp'=8,'fsdp'=4] {'dp','fsdp'}, dimensions={0}, use_global_device_ids=true | all-gather | bytes 202752 | tf_op jit(solution)/shard_map/all_gather | solution.py:379
  633.0 40.6 %all-gather.3 = bf16[32,2,768]{2,1,0:T(2,128)(2,1)} all-gather(bf16[1,2,768]{2,1,0:T(2,128)(2,1)S(1)} %slice_bitcast_fusion.25), channel_id=1, replica_groups=mesh['dp'=8,'fsdp'=4] {'dp','fsdp'}, dimensions={0}, use_global_device_ids=true | all-gather | bytes 101376 | tf_op jit(solution)/shard_map/all_gather | solution.py:380
  683.0 131.7 %all-reduce.13.cloned.1.call-done = (f32[128,768]{1,0:T(8,128)}, f32[64,768]{1,0:T(8,128)}) async-done(((f32[128,768]{1,0:T(8,128)}, f32[64,768]{1,0:T(8,128)}), (f32[128,768]{1,0:T(8,128)}, f32[64,768]{1,0:T(8,128)})) %all-reduce.13.cloned.1.call-update) | async-done | bytes 589840
  823.7 6.8 fusion.89
  836.5 9.2 fusion.6
  848.6 9.3 fusion.13
  872.6 6.2 multiply_reduce_fusion.7
  956.7 6.7 pad_maximum_fusion
  963.5 36.1 %reduce-scatter.18.cloned.1.call-done = f32[384,768]{1,0:T(8,128)} async-done(((f32[3072,768]{1,0:T(8,128)}), f32[384,768]{1,0:T(8,128)}) %reduce-scatter.18.cloned.1.call-update) | async-done | bytes 1179664 | tf_op jit(solution)/shard_map/reduce_scatter | solution.py:446
  1002.4 163.8 %reduce-scatter.14.cloned.1.call-done = f32[96,3072]{1,0:T(8,128)} async-done(((f32[768,3072]{1,0:T(8,128)}), f32[96,3072]{1,0:T(8,128)}) %reduce-scatter.14.cloned.1.call-update) | async-done | bytes 1179664 | tf_op jit(solution)/shard_map/reduce_scatter | solution.py:445
  1169.6 195.9 %reduce-scatter.12.cloned.1.call-done = f32[5,96,768]{2,1,0:T(8,128)} async-done(((f32[5,768,768]{2,1,0:T(8,128)}), f32[5,96,768]{2,1,0:T(8,128)}) %reduce-scatter.12.cloned.1.call-update) | async-done | bytes 1474576 | tf_op jit(solution)/shard_map/reduce_scatter | solution.py:444
  1383.9 31.4 %broadcast_in_dim.122 = f32[32128,768]{1,0:T(8,128)} broadcast(f32[]{:T(128)} %constant.44.clone.1), dimensions={} | broadcast | bytes 98697216 | tf_op jit(solution)/shard_map/broadcast_in_dim | solution.py:437
  1415.3 130.6 %scatter_fusion = f32[32128,768]{1,0:T(8,128)} fusion(f32[32128,768]{1,0:T(8,128)} %broadcast_in_dim.122, s32[1024]{0:T(1024)S(1)} %pad_add_fusion.1, f32[1024,768]{1,0:T(8,128)S(1)} %pad_maximum_fusion.1), kind=kCustom, calls=%fused_computation.1 | custom fusion | flops 786432 | bytes 9441280 | tf_op jit(solution)/shard_map/scatter-add | solution.py:437
  1556.1 27.1 all-reduce.4
  1583.9 11.5 all-reduce.5
  1608.5 1311.7 %all-reduce.11.cloned.1.call-done = f32[768,32128]{0,1:T(8,128)} async-done(((f32[768,32128]{0,1:T(8,128)}), f32[768,32128]{0,1:T(8,128)}) %all-reduce.11.cloned.1.call-update) | async-done | bytes 98697232
  2920.1 17.1 multiply_reduce_fusion
  2937.9 40.2 %all-reduce.6 = (f32[]{:T(128)}, f32[32,12]{0,1:T(8,128)S(1)}, f32[1]{0:T(128)}, f32[2]{0:T(128)}) all-reduce(f32[]{:T(128)S(6)} %add.459, f32[32,12]{0,1:T(8,128)S(1)} %fusion.47, f32[1]{0:T(128)} %bitcast.41, f32[2]{0:T(128)S(1)} %copy-done.159), channel_id=1, replica_groups=mesh['dp'=8,'fsdp'=4] {'dp','fsdp'}, use_global_device_ids=true, to_apply=%region_49.50 | all-reduce | flops 388 | bytes 3104 | tf_op jit(solution)/shard_map/psum | solution.py:463
  2982.9 9.8 copy.525
  2997.2 6.9 multiply_subtract_fusion
  (564 shorter events, 278.1 us)
Async XLA Ops:
  7.2 273.8 %all-gather.9.cloned.1.call-start = ((), (), s32[]{:S(2)}) async-start(), calls=%async_computation.6 | async-start | bytes 50890752 | tf_op jit(solution)/shard_map/all_gather | solution.py:356
  10.5 364.8 %all-gather.11.cloned.1.call-start = ((), (), s32[]{:S(2)}) async-start(), calls=%async_computation.7 | async-start | bytes 6635520 | tf_op jit(solution)/shard_map/all_gather | solution.py:328
  25.6 430.4 %all-gather.13.cloned.1.call-start = ((), (), s32[]{:S(2)}) async-start(), calls=%async_computation.8 | async-start | bytes 5308416 | tf_op jit(solution)/shard_map/all_gather | solution.py:329
  37.4 499.3 %all-gather.15.cloned.1.call-start = ((), (), s32[]{:S(2)}) async-start(), calls=%async_computation.9 | async-start | bytes 5308416 | tf_op jit(solution)/shard_map/all_gather | solution.py:330
  45.6 769.1 %all-reduce.13.cloned.1.call-start = ((), (), s32[]{:S(2)}) async-start(), calls=%async_computation.17 | async-start | bytes 1179648
  65.9 277.3 %copy-start.147 = (f32[4]{0:T(128)}, f32[4]{0:T(128)S(1)}, u32[]{:S(2)}) copy-start(f32[4]{0:T(128)S(1)} %convert_element_type.235) | copy-start | bytes 52
  66.7 276.5 %copy-start.143 = (f32[8]{0:T(128)}, f32[8]{0:T(128)S(1)}, u32[]{:S(2)}) copy-start(f32[8]{0:T(128)S(1)} %get-tuple-element.268) | copy-start | bytes 100
  69.3 294.9 %copy-start.87 = (f32[768]{0:T(1024)}, f32[768]{0:T(1024)S(1)}, u32[]{:S(2)}) copy-start(f32[768]{0:T(1024)S(1)} %get-tuple-element.202) | copy-start | bytes 9220
  69.3 523.7 %copy-start.89 = (f32[768]{0:T(1024)}, f32[768]{0:T(1024)S(1)}, u32[]{:S(2)}) copy-start(f32[768]{0:T(1024)S(1)} %get-tuple-element.200) | copy-start | bytes 9220
  455.9 80.8 %copy-start.4 = (f32[512,768]{1,0:T(8,128)S(1)}, f32[512,768]{1,0:T(8,128)}, u32[]{:S(2)}) copy-start(f32[512,768]{1,0:T(8,128)} %get-tuple-element.279) | copy-start | bytes 4718596
  464.1 82.4 %copy-start.25 = (bf16[512,768]{1,0:T(8,128)(2,1)S(1)}, bf16[512,768]{1,0:T(8,128)(2,1)}, u32[]{:S(2)}) copy-start(bf16[512,768]{1,0:T(8,128)(2,1)} %get-tuple-element.242) | copy-start | bytes 2359300
  546.6 46.4 %copy-start.105 = (f32[512]{0:T(512)}, f32[512]{0:T(512)S(1)}, u32[]{:S(2)}) copy-start(f32[512]{0:T(512)S(1)} %get-tuple-element.265) | copy-start | bytes 6148
  596.5 226.0 %copy-start.68 = (f32[12,768]{1,0:T(8,128)}, f32[12,768]{1,0:T(8,128)S(1)}, u32[]{:S(2)}) copy-start(f32[12,768]{1,0:T(8,128)S(1)} %get-tuple-element.283) | copy-start | bytes 110596
  596.5 222.6 %copy-start.90 = (f32[768]{0:T(1024)S(1)}, f32[768]{0:T(1024)}, u32[]{:S(2)}) copy-start(f32[768]{0:T(1024)} %copy-done.89) | copy-start | bytes 9220
  596.6 222.6 %copy-start.106 = (f32[512]{0:T(512)S(1)}, f32[512]{0:T(512)}, u32[]{:S(2)}) copy-start(f32[512]{0:T(512)} %copy-done.105) | copy-start | bytes 6148
  674.9 140.6 %copy-start.103 = (f32[4,128]{1,0:T(4,128)}, f32[4,128]{1,0:T(4,128)S(1)}, u32[]{:S(2)}) copy-start(f32[4,128]{1,0:T(4,128)S(1)} %get-tuple-element.285) | copy-start | bytes 6148
  674.9 140.6 %copy-start.117 = (f32[4]{0:T(128)}, f32[4]{0:T(128)S(1)}, u32[]{:S(2)}) copy-start(f32[4]{0:T(128)S(1)} %get-tuple-element.284) | copy-start | bytes 52
  681.3 318.3 %reduce-scatter.18.cloned.1.call-start = ((), (), s32[]{:S(2)}) async-start(), calls=%async_computation.13 | async-start | bytes 10616832 | tf_op jit(solution)/shard_map/reduce_scatter | solution.py:446
  682.2 136.9 %copy-start.93 = (f32[2,768]{1,0:T(2,128)}, f32[2,768]{1,0:T(2,128)S(1)}, u32[]{:S(2)}) copy-start(f32[2,768]{1,0:T(2,128)S(1)} %fusion.114) | copy-start | bytes 18436
  683.0 134.3 %copy-start.97 = (f32[4,768]{1,0:T(4,128)}, f32[4,768]{1,0:T(4,128)S(1)}, u32[]{:S(2)}) copy-start(f32[4,768]{1,0:T(4,128)S(1)} %fusion.111) | copy-start | bytes 36868
  836.4 329.8 %reduce-scatter.14.cloned.1.call-start = ((), (), s32[]{:S(2)}) async-start(), calls=%async_computation.11 | async-start | bytes 10616832 | tf_op jit(solution)/shard_map/reduce_scatter | solution.py:445
  864.9 500.5 %reduce-scatter.12.cloned.1.call-start = ((), (), s32[]{:S(2)}) async-start(), calls=%async_computation.10 | async-start | bytes 13271040 | tf_op jit(solution)/shard_map/reduce_scatter | solution.py:444
  963.4 202.8 %copy-start.110 = (s32[512]{0:T(512)S(1)}, s32[512]{0:T(512)}, u32[]{:S(2)}) copy-start(s32[512]{0:T(512)} %copy-done.109) | copy-start | bytes 6148
  963.4 202.8 %copy-start.112 = (s32[4,128]{1,0:T(4,128)S(1)}, s32[4,128]{1,0:T(4,128)}, u32[]{:S(2)}) copy-start(s32[4,128]{1,0:T(4,128)} %param.54) | copy-start | bytes 6148
  963.5 202.9 %copy-start.55 = (bf16[512,768]{0,1:T(8,128)(2,1)S(1)}, bf16[512,768]{0,1:T(8,128)(2,1)}, u32[]{:S(2)}) copy-start(bf16[512,768]{0,1:T(8,128)(2,1)} %reshape.515) | copy-start | bytes 2359300
  963.5 636.6 %reduce-scatter.22.cloned.1.call-start = ((), (), s32[]{:S(2)}) async-start(), calls=%async_computation.15 | async-start | bytes 1474560
  1002.3 598.9 %reduce-scatter.16.cloned.1.call-start = ((), (), s32[]{:S(2)}) async-start(), calls=%async_computation.12 | async-start | bytes 1474560 | tf_op jit(solution)/shard_map/reduce_scatter | solution.py:451
  1166.2 437.4 %reduce-scatter.20.cloned.1.call-start = ((), (), s32[]{:S(2)}) async-start(), calls=%async_computation.14 | async-start | bytes 1966080
  1369.4 1550.8 %all-reduce.11.cloned.1.call-start = ((), (), s32[]{:S(2)}) async-start(), calls=%async_computation.16 | async-start | bytes 197394432
  1554.8 43.5 %copy-start.29 = (f32[16384,32]{0,1:T(8,128)S(1)}, f32[16384,32]{0,1:T(8,128)}, u32[]{:S(2)}) copy-start(f32[16384,32]{0,1:T(8,128)} %constant.85.clone) | copy-start | bytes 6291460
  1605.1 1332.1 %copy-start.39 = (f32[5,96,192]{2,1,0:T(8,128)}, f32[5,96,192]{2,1,0:T(8,128)S(1)}, u32[]{:S(2)}) copy-start(f32[5,96,192]{2,1,0:T(8,128)S(1)} %copy.540) | copy-start | bytes 1105924
  1608.5 1329.5 %copy-start.159 = (f32[2]{0:T(128)S(1)}, f32[2]{0:T(128)}, u32[]{:S(2)}) copy-start(f32[2]{0:T(128)} %pad_maximum_fusion.6) | copy-start | bytes 28
  (148 other events, 798.3 us)
Sparse Core Ops, SparseCore 0:
  11.4 269.4 all-gather.8
  283.7 91.5 all-gather.10
  377.5 78.3 all-gather.12
  457.8 78.8 all-gather.14
  681.4 133.2 all-reduce.12
  836.5 163.0 reduce-scatter.17
  1003.7 162.4 reduce-scatter.13
  1170.3 195.1 reduce-scatter.11
  1368.6 25.5 reduce-scatter.21
  1396.8 25.6 reduce-scatter.15
  1425.7 28.1 reduce-scatter.19
  1546.1 1374.0 all-reduce.10
where the time goes:
time: 3030 us; the launch traced here: 3020 us
  waiting for transfers between devices  2180 us (72%)
  local copies, waits for them, and re-layouts  227 us (7%)
  other arithmetic  209 us (7%)
  blocking collectives  204 us (7%)
  matrix products  168 us (6%)
  between operations  31.4 us (1%)
    unnamed x16, waiting for transfers between devices  1440 us
    all_gather x1, waiting for transfers between devices, shards(): lax.all_gather(table_low, ('dp', 'fsdp'), axis=0, tiled=True)  210 us
    reduce_scatter x1, waiting for transfers between devices, shards(): lax.psum_scatter(grad_squares, 'dp', scatter_dimension=1, tiled=True)  196 us
    reduce_scatter x1, waiting for transfers between devices, shards(): lax.psum_scatter(grad_expand, 'dp', scatter_dimension=0, tiled=True)  164 us
    scatter-add x1, other arithmetic, shards(): jax.ops.segment_sum(grad_tokens, all_tokens, num_segments=vocab_size)  131 us
    all_gather x1, waiting for transfers between devices, gather_layer(): lax.all_gather(wide_parts[2], 'dp', axis=0, tiled=True)  72.6 us
    all_gather x1, local copies, waits for them, and re-layouts, shards(): lax.all_gather(table_low, ('dp', 'fsdp'), axis=0, tiled=True)  62.2 us
  transfers between devices with their start and end apart: 12, of which 9 were waited for; matrix products, arithmetic and copies ran while one was open for 15% of the time, Pallas kernels for 0%

commit v1 on v0

--- a/solution.py
+++ b/solution.py
@@ -1,7 +1,11 @@
+import functools
+
 import jax
 import jax.numpy as jnp
 import numpy as np
 from jax import lax
+from jax.experimental import pallas as pl
+from jax.experimental.pallas import tpu as pltpu
 from jax.sharding import PartitionSpec as P
 
 D = 768
@@ -286,6 +290,210 @@
     return (moment_new, second_new, updated)
 
 
+LANES = 128
+GROUPS = 4
+SLOT = LANES // GROUPS
+VMEM_CAP = 48 * 1024 * 1024
+
+def fold_rows(vocab):
+    per = -(-vocab // GROUPS)
+    return -(-per // LANES) * LANES
+
+def up8(n):
+    return -(-n // 8) * 8
+
+def eye():
+    r = lax.broadcasted_iota(jnp.int32, (LANES, LANES), 0)
+    c = lax.broadcasted_iota(jnp.int32, (LANES, LANES), 1)
+    return (r == c).astype(jnp.float32).astype(jnp.bfloat16)
+
+def lookup_kernel(fold, row_ref, group_ref, table_ref, out_ref, turned, rows):
+    feats, vocab = table_ref.shape
+    tokens = rows.shape[0]
+    @pl.when(pl.program_id(0) == 0)
+    def _():
+        pad = jnp.zeros((SLOT - feats, LANES), jnp.float32)
+        def build(b, _):
+            parts = []
+            for j in range(GROUPS):
+                start = jnp.minimum(j * fold + b * LANES, vocab - LANES)
+                start = pl.multiple_of(start, LANES)
+                parts += [table_ref[:, pl.ds(start, LANES)], pad]
+            tile = jnp.concatenate(parts, axis=0)
+            turned[pl.ds(pl.multiple_of(b * LANES, LANES), LANES), :] = tile.T
+            return 0
+        lax.fori_loop(0, fold // LANES, build, 0)
+        turned[pl.ds(fold, 8), :] = jnp.zeros((8, LANES), jnp.float32)
+    UN = 32
+    def fetch(b, _):
+        for k in range(UN):
+            t = b * UN + k
+            rows[pl.ds(t, 1), :] = turned[pl.ds(row_ref[0, 0, t], 1), :]
+        return 0
+    lax.fori_loop(0, tokens // UN, fetch, 0)
+    wide = lax.dot_general(eye(), rows[...].astype(jnp.bfloat16), (((1,), (1,)), ((), ())), preferred_element_type=jnp.float32)
+    group = group_ref[0]
+    total = jnp.where(group == 0, wide[:SLOT], 0.0)
+    for j in range(1, GROUPS):
+        total = total + jnp.where(group == j, wide[j * SLOT:(j + 1) * SLOT], 0.0)
+    half = tokens // 2
+    out_ref[0] = jnp.concatenate([total[:feats, :half], total[:feats, half:]], axis=0).astype(jnp.bfloat16)
+
+def lookup(table, rows_idx, groups_idx):
+    feats, vocab = table.shape
+    n, tokens = rows_idx.shape[0], rows_idx.shape[2]
+    fold = fold_rows(vocab)
+    return pl.pallas_call(
+        functools.partial(lookup_kernel, fold),
+        grid=(n,),
+        out_shape=jax.ShapeDtypeStruct((n, 2 * feats, tokens // 2), jnp.bfloat16),
+        in_specs=[
+            pl.BlockSpec((1, 1, tokens), lambda s: (s, 0, 0), memory_space=pltpu.SMEM),
+            pl.BlockSpec((1, 1, tokens), lambda s: (s, 0, 0)),
+            pl.BlockSpec((feats, vocab), lambda s: (0, 0)),
+        ],
+        out_specs=pl.BlockSpec((1, 2 * feats, tokens // 2), lambda s: (s, 0, 0)),
+        scratch_shapes=[pltpu.VMEM((fold + 8, LANES), jnp.float32), pltpu.VMEM((tokens, LANES), jnp.float32)],
+        compiler_params=pltpu.CompilerParams(vmem_limit_bytes=VMEM_CAP),
+        name="lookup",
+    )(rows_idx, groups_idx, table)
+
+def scatter_kernel(fold, row_ref, group_ref, grad_ref, out_ref, total, rows):
+    feats, vocab = out_ref.shape
+    tokens = rows.shape[0]
+    step = pl.program_id(0)
+    @pl.when(step == 0)
+    def _():
+        def clear(b, _):
+            total[pl.ds(pl.multiple_of(b * LANES, LANES), LANES), :] = jnp.zeros((LANES, LANES), jnp.float32)
+            return 0
+        lax.fori_loop(0, fold // LANES, clear, 0)
+        total[pl.ds(fold, 8), :] = jnp.zeros((8, LANES), jnp.float32)
+    block = grad_ref[0].astype(jnp.float32)
+    flat = jnp.concatenate([block[:feats], block[feats:]], axis=1)
+    group = group_ref[0]
+    pad = jnp.zeros((SLOT - feats, tokens), jnp.float32)
+    parts = []
+    for j in range(GROUPS):
+        parts += [jnp.where(group == j, flat, 0.0), pad]
+    spread = jnp.concatenate(parts, axis=0).astype(jnp.bfloat16)
+    rows[...] = lax.dot_general(spread, eye(), (((0,), (0,)), ((), ())), preferred_element_type=jnp.float32)
+    LN = 16
+    stride = tokens // LN
+    def add(i, _):
+        at = [row_ref[0, 0, i + stride * k] for k in range(LN)]
+        new = [total[pl.ds(at[k], 1), :] + rows[pl.ds(i + stride * k, 1), :] for k in range(LN)]
+        for k in range(LN):
+            total[pl.ds(at[k], 1), :] = new[k]
+        return 0
+    lax.fori_loop(0, stride, add, 0, unroll=2)
+    @pl.when(step == pl.num_programs(0) - 1)
+    def _():
+        whole = (vocab - (GROUPS - 1) * fold) // LANES
+        def turn(b, _):
+            tile = total[pl.ds(pl.multiple_of(b * LANES, LANES), LANES), :].T
+            for j in range(GROUPS):
+                out_ref[:, pl.ds(pl.multiple_of(j * fold + b * LANES, LANES), LANES)] = tile[j * SLOT:j * SLOT + feats]
+            return 0
+        lax.fori_loop(0, whole, turn, 0)
+        for b in range(whole, fold // LANES):
+            tile = total[pl.ds(b * LANES, LANES), :].T
+            for j in range(GROUPS - 1):
+                out_ref[:, pl.ds(j * fold + b * LANES, LANES)] = tile[j * SLOT:j * SLOT + feats]
+
+def scatter(grads, rows_idx, groups_idx, vocab):
+    n, tokens = rows_idx.shape[0], rows_idx.shape[2]
+    feats = grads.shape[1] // 2
+    fold = fold_rows(vocab)
+    return pl.pallas_call(
+        functools.partial(scatter_kernel, fold),
+        grid=(n,),
+        out_shape=jax.ShapeDtypeStruct((feats, vocab), jnp.float32),
+        in_specs=[
+            pl.BlockSpec((1, 1, tokens), lambda s: (s, 0, 0), memory_space=pltpu.SMEM),
+            pl.BlockSpec((1, 1, tokens), lambda s: (s, 0, 0)),
+            pl.BlockSpec((1, 2 * feats, tokens // 2), lambda s: (s, 0, 0)),
+        ],
+        out_specs=pl.BlockSpec((feats, vocab), lambda s: (0, 0)),
+        scratch_shapes=[pltpu.VMEM((fold + 8, LANES), jnp.float32), pltpu.VMEM((tokens, LANES), jnp.float32)],
+        compiler_params=pltpu.CompilerParams(vmem_limit_bytes=VMEM_CAP),
+        name="scatter",
+    )(rows_idx, groups_idx, grads)
+
+def token_keys(tokens, fold):
+    count = tokens.shape[0]
+    key = (tokens % fold) * GROUPS + tokens // fold
+    places = jnp.arange(count, dtype=jnp.int32)
+    same_before = (key[:, None] == key[None, :]) & (places[:, None] < places[None, :])
+    first = ~jnp.any(same_before, axis=0)
+    rank = jnp.sum(((key[None, :] < key[:, None]) & first[None, :]).astype(jnp.int32), axis=1)
+    hit = rank[:, None] == places[None, :]
+    packed = GROUPS * fold + jnp.sum(jnp.where(hit & first[:, None], key[:, None] - GROUPS * fold, 0), axis=0)
+    return packed, hit.astype(jnp.bfloat16)
+
+
+MESH = pl.DeviceIdType.MESH
+
+
+def exchange_kernel(same, src, dst, send_sem, recv_sem, own_sem):
+    rows, cols = lax.axis_size("dp"), lax.axis_size("fsdp")
+    count = rows * cols
+    me = lax.axis_index("dp") * cols + lax.axis_index("fsdp")
+    barrier = pltpu.get_barrier_semaphore()
+
+    def device(k):
+        to = lax.rem(me + k, count)
+        return (to // cols, lax.rem(to, cols))
+
+    def greet(k, carry):
+        pl.semaphore_signal(barrier, inc=1, device_id=device(k), device_id_type=MESH)
+        return carry
+
+    def copy(k):
+        to = lax.rem(me + k, count)
+        return pltpu.make_async_remote_copy(
+            src_ref=src.at[0 if same else to],
+            dst_ref=dst.at[me],
+            send_sem=send_sem.at[k],
+            recv_sem=recv_sem.at[k],
+            device_id=device(k),
+            device_id_type=MESH,
+        )
+
+    def start(k, carry):
+        copy(k).start()
+        return carry
+
+    def end(k, carry):
+        copy(k).wait()
+        return carry
+
+    lax.fori_loop(1, count, greet, 0)
+    own = pltpu.make_async_copy(src.at[0 if same else me], dst.at[me], own_sem)
+    own.start()
+    pl.semaphore_wait(barrier, count - 1)
+    lax.fori_loop(1, count, start, 0)
+    own.wait()
+    lax.fori_loop(1, count, end, 0)
+
+
+def exchange(blocks, same, call_id, name):
+    count = lax.axis_size("dp") * lax.axis_size("fsdp")
+    return pl.pallas_call(
+        functools.partial(exchange_kernel, same),
+        out_shape=jax.ShapeDtypeStruct((count,) + blocks.shape[1:], blocks.dtype),
+        in_specs=[pl.BlockSpec(memory_space=pl.ANY)],
+        out_specs=pl.BlockSpec(memory_space=pl.ANY),
+        scratch_shapes=[
+            pltpu.SemaphoreType.DMA((count,)),
+            pltpu.SemaphoreType.DMA((count,)),
+            pltpu.SemaphoreType.DMA,
+        ],
+        compiler_params=pltpu.CompilerParams(collective_id=call_id, has_side_effects=True),
+        name=name,
+    )(blocks)
+
+
 def shards(
     embed_table,
     square_weights,
@@ -316,46 +524,56 @@
     hypothesis_tokens,
     hard_negative,
 ):
-
-    def gather_layer():
-        wide_parts = (
-            lax.all_gather(square_weights.astype(jnp.bfloat16), "fsdp", axis=2, tiled=True),
-            lax.all_gather(expand_weight.astype(jnp.bfloat16), "fsdp", axis=1, tiled=True),
-            lax.all_gather(reduce_weight.astype(jnp.bfloat16), "fsdp", axis=1, tiled=True),
-            lax.all_gather(norm_gains.astype(jnp.bfloat16), "fsdp", axis=1, tiled=True),
-        )
-        full_parts = (
-            lax.all_gather(wide_parts[0], "dp", axis=1, tiled=True),
-            lax.all_gather(wide_parts[1], "dp", axis=0, tiled=True),
-            lax.all_gather(wide_parts[2], "dp", axis=0, tiled=True),
-            lax.all_gather(wide_parts[3], "dp", axis=1, tiled=True),
-        )
-        return (
-            full_parts[0],
-            full_parts[1],
-            full_parts[2],
-            full_parts[3].astype(jnp.float32),
-            position_bias,
-        )
-
-    layer = gather_layer()
+    both = ("dp", "fsdp")
+    count = lax.axis_size("dp") * lax.axis_size("fsdp")
+    feats, vocab_size = embed_table.shape
+    feats_pad = up8(feats)
+    fold = fold_rows(vocab_size)
     query_rows = query_tokens.shape[0]
     nli_rows = premise_tokens.shape[0]
     short_length = query_tokens.shape[1]
     long_length = answer_tokens.shape[1]
-    vocab_size = embed_table.shape[1]
-    count_rows = lax.axis_size("dp")
-    count_cols = lax.axis_size("fsdp")
     short_tokens = jnp.concatenate([query_tokens, premise_tokens, hypothesis_tokens], axis=0)
     short_lengths = jnp.concatenate(
         [query_length, jnp.full((2 * nli_rows,), short_length, jnp.int32)]
     )
     all_tokens = jnp.concatenate([short_tokens.reshape(-1), answer_tokens.reshape(-1)])
-    table_low = embed_table.astype(jnp.bfloat16)
-    chosen = jnp.take(
-        lax.all_gather(table_low, ("dp", "fsdp"), axis=0, tiled=True), all_tokens, axis=1
-    ).astype(jnp.float32)
-    embedded = chosen.T
+    token_count = all_tokens.shape[0]
+    packed, hit = token_keys(all_tokens, fold)
+    packed_all = exchange(packed.reshape(1, -1, LANES), True, 0, "share_keys")
+    packed_all = packed_all.reshape(count, 1, token_count)
+    row_all, group_all = packed_all >> 2, packed_all & 3
+
+    def gather_layer():
+        def whole(weight, row_axis):
+            low = weight.astype(jnp.bfloat16)
+            parts = lax.all_gather(low, both, axis=0, tiled=False)
+            dp, fsdp = lax.axis_size("dp"), lax.axis_size("fsdp")
+            parts = parts.reshape((dp, fsdp) + low.shape)
+            lead = tuple(range(2, 2 + row_axis))
+            order = lead + (0, 2 + row_axis, 1, 3 + row_axis)
+            shape = low.shape[:row_axis] + (dp * low.shape[row_axis], fsdp * low.shape[row_axis + 1])
+            return parts.transpose(order).reshape(shape)
+
+        gains = exchange(jnp.pad(norm_gains, ((0, 5), (0, LANES - feats)))[None], True, 1, "share_gains")
+        gains = gains[:, :3, :feats].transpose(1, 0, 2).reshape(3, D)
+        return (
+            whole(square_weights, 1),
+            whole(expand_weight, 0),
+            whole(reduce_weight, 0),
+            gains.astype(jnp.bfloat16).astype(jnp.float32),
+            position_bias,
+        )
+
+    layer = gather_layer()
+    table_low = embed_table.astype(jnp.bfloat16).astype(jnp.float32)
+    if feats_pad > feats:
+        table_low = jnp.pad(table_low, ((0, feats_pad - feats), (0, 0)))
+    found = exchange(lookup(table_low, row_all, group_all), False, 2, "send_features")
+    half = token_count // 2
+    found = found.reshape(count, 2, feats_pad, half)[:, :, :feats]
+    found = found.transpose(0, 2, 1, 3).reshape(D, token_count)
+    embedded = product_right(hit, found)
     split_at = short_tokens.shape[0] * short_length
     short_mask = jnp.arange(short_length)[None, :] < short_lengths[:, None]
     long_mask = jnp.arange(long_length)[None, :] < answer_length[:, None]
@@ -375,35 +593,48 @@
     embeds_low = embeds.astype(jnp.bfloat16)
     hypo_start = query_rows + nli_rows
     answer_start = query_rows + 2 * nli_rows
-    gathered = (
-        lax.all_gather(embeds_low[answer_start:], ("dp", "fsdp"), axis=0, tiled=True),
-        lax.all_gather(embeds_low[hypo_start:answer_start], ("dp", "fsdp"), axis=0, tiled=True),
-    )
+    seq_count = answer_start + query_rows
+    seq_pad = -(-seq_count // 16) * 16
+    gathered = exchange(
+        jnp.pad(embeds_low, ((0, seq_pad - seq_count), (0, 0)))[None], True, 3, "share_embeds"
+    )
+    negative_all = exchange(
+        jnp.pad(hard_negative, (0, 8 * LANES - nli_rows)).reshape(1, 8, LANES), True, 4, "share_negatives"
+    ).reshape(count, -1)[:, :nli_rows].reshape(-1)
+    queries_all = gathered[:, :query_rows].reshape(-1, D)
+    premises_all = gathered[:, query_rows:hypo_start].reshape(-1, D)
+    hypotheses_all = gathered[:, hypo_start:answer_start].reshape(-1, D)
+    answers_all = gathered[:, answer_start:seq_count].reshape(-1, D)
     scale = jnp.exp(log_scale[0])
-    position = lax.axis_index(("dp", "fsdp"))
-    first_loss, first_dscale, grad_queries, grad_answers = contrast_local(
-        embeds_low[:query_rows],
-        gathered[0],
-        scale,
-        0.0,
-        position * query_rows + jnp.arange(query_rows),
-    )
-    negatives = (jnp.arange(gathered[1].shape[0])[None, :] == hard_negative[:, None]).astype(
+    position = lax.axis_index(both)
+
+    def contrast(left, right, extra, own):
+        sims = product_right(left, right)
+        logits = scale * sims
+        row_top = jnp.max(logits, axis=1, keepdims=True)
+        raised = (1.0 + extra) * jnp.exp(logits - row_top)
+        row_total = jnp.sum(raised, axis=1, keepdims=True)
+        spread = row_top[:, 0] + jnp.log(row_total[:, 0])
+        target_hit = jnp.eye(left.shape[0], dtype=jnp.float32)
+        loss_sum = jnp.sum(spread - jnp.sum(target_hit * logits, axis=1))
+        grad_logits = raised / row_total - target_hit
+        grad_scale = jnp.sum(grad_logits * sims)
+        grad_sims = (scale * grad_logits).astype(jnp.bfloat16)
+        mine_left = lax.dynamic_slice_in_dim(grad_sims, position * own, own, 0)
+        mine_right = lax.dynamic_slice_in_dim(grad_sims, position * own, own, 1)
+        return (loss_sum, grad_scale, product(mine_left, right), product_left(mine_right, left))
+
+    first_loss, first_dscale, grad_queries, grad_answers = contrast(
+        queries_all, answers_all, 0.0, query_rows
+    )
+    negatives = (jnp.arange(hypotheses_all.shape[0])[None, :] == negative_all[:, None]).astype(
         jnp.float32
     )
-    second_loss, second_dscale, grad_premises, grad_hypotheses = contrast_local(
-        embeds_low[query_rows:hypo_start],
-        gathered[1],
-        scale,
-        negatives,
-        position * nli_rows + jnp.arange(nli_rows),
-    )
-    back_parts = (
-        lax.psum_scatter(grad_answers, ("dp", "fsdp"), scatter_dimension=0, tiled=True),
-        lax.psum_scatter(grad_hypotheses, ("dp", "fsdp"), scatter_dimension=0, tiled=True),
+    second_loss, second_dscale, grad_premises, grad_hypotheses = contrast(
+        premises_all, hypotheses_all, negatives, nli_rows
     )
     grad_embeds = jnp.concatenate(
-        [grad_queries, grad_premises, back_parts[1], back_parts[0]], axis=0
+        [grad_queries, grad_premises, grad_hypotheses, grad_answers], axis=0
     )
     grad_projected = (
         inverse * (grad_embeds - embeds * jnp.sum(grad_embeds * embeds, axis=-1, keepdims=True))
@@ -411,18 +642,17 @@
     grad_proj_weight = product_left(pooled_low, grad_projected)
     grad_pooled = product_right(grad_projected, layer[0][4])
     short_rows = short_tokens.shape[0]
-    back_layer = gather_layer()
     grad_short_start, short_grads = layer_backward(
         spread_rows(grad_pooled[:short_rows], short_mask, short_lengths),
         short_mask,
-        back_layer,
+        layer,
         short_stored,
         short_length,
     )
     grad_long_start, long_grads = layer_backward(
         spread_rows(grad_pooled[short_rows:], long_mask, answer_length),
         long_mask,
-        back_layer,
+        layer,
         long_stored,
         long_length,
     )
@@ -433,40 +663,43 @@
     grad_position = short_grads[4] + long_grads[4]
     grad_scale = ((first_dscale + second_dscale) * scale).reshape(1)
     grad_tokens = jnp.concatenate([grad_short_start, grad_long_start], axis=0)
-    grad_table = lax.psum_scatter(
-        jax.ops.segment_sum(grad_tokens, all_tokens, num_segments=vocab_size).T,
-        ("dp", "fsdp"),
-        scatter_dimension=0,
-        tiled=True,
-    )
-    gains_four = grad_gains.reshape(3, count_rows, count_cols, -1)
-    rows_part = (
-        lax.psum_scatter(grad_squares, "dp", scatter_dimension=1, tiled=True),
-        lax.psum_scatter(grad_expand, "dp", scatter_dimension=0, tiled=True),
-        lax.psum_scatter(grad_reduce, "dp", scatter_dimension=0, tiled=True),
-        lax.psum_scatter(gains_four, "dp", scatter_dimension=1, tiled=True),
-    )
+    merged = product_left(grad_tokens.astype(jnp.bfloat16), hit).astype(jnp.bfloat16)
+    merged = merged.reshape(count, feats, 2, half).transpose(0, 2, 1, 3)
+    if feats_pad > feats:
+        merged = jnp.pad(merged, ((0, 0), (0, 0), (0, feats_pad - feats), (0, 0)))
+    returned = exchange(merged.reshape(count, 2 * feats_pad, half), False, 5, "send_gradients")
+    grad_table = scatter(returned, row_all, group_all, vocab_size)[:feats]
+    squares_part = lax.psum_scatter(grad_squares, "dp", scatter_dimension=1, tiled=True)
     reduced = (
-        lax.psum_scatter(rows_part[0], "fsdp", scatter_dimension=2, tiled=True),
-        lax.psum_scatter(rows_part[1], "fsdp", scatter_dimension=1, tiled=True),
-        lax.psum_scatter(rows_part[2], "fsdp", scatter_dimension=1, tiled=True),
-        lax.psum_scatter(rows_part[3], "fsdp", scatter_dimension=2, tiled=True),
-    )
-    grad_gain_shard = reduced[3].reshape(3, -1)
+        lax.psum_scatter(squares_part, "fsdp", scatter_dimension=2, tiled=True),
+        lax.psum_scatter(
+            lax.psum_scatter(grad_expand, "dp", scatter_dimension=0, tiled=True),
+            "fsdp", scatter_dimension=1, tiled=True),
+        lax.psum_scatter(
+            lax.psum_scatter(grad_reduce, "dp", scatter_dimension=0, tiled=True),
+            "fsdp", scatter_dimension=1, tiled=True),
+    )
     local_square = (
         jnp.sum(reduced[0] * reduced[0])
         + jnp.sum(reduced[1] * reduced[1])
         + jnp.sum(reduced[2] * reduced[2])
-        + jnp.sum(grad_gain_shard * grad_gain_shard)
         + jnp.sum(grad_table * grad_table)
     )
-    summed = lax.psum(
-        (grad_position, grad_scale, jnp.stack([first_loss, second_loss]), local_square),
-        ("dp", "fsdp"),
-    )
-    position_total, scale_total, losses, square_total = summed
+    small = jnp.concatenate([grad_gains.reshape(-1), grad_position.reshape(-1), local_square.reshape(1)])
+    small_rows = -(-small.shape[0] // (8 * LANES)) * 8
+    small = jnp.pad(small, (0, small_rows * LANES - small.shape[0])).reshape(1, small_rows, LANES)
+    summed = jnp.sum(exchange(small, True, 6, "share_small"), axis=0).reshape(-1)
+    gains_total = summed[: 3 * D].reshape(3, D)
+    position_total = summed[3 * D : 3 * D + BUCKETS * HEADS].reshape(BUCKETS, HEADS)
+    square_total = summed[3 * D + BUCKETS * HEADS]
+    scale_total = grad_scale
+    losses = jnp.stack([first_loss, second_loss])
+    grad_gain_shard = lax.dynamic_slice_in_dim(gains_total, position * feats, feats, 1)
     gradient_norm = jnp.sqrt(
-        square_total + jnp.sum(position_total * position_total) + jnp.sum(scale_total * scale_total)
+        square_total
+        + jnp.sum(gains_total * gains_total)
+        + jnp.sum(position_total * position_total)
+        + jnp.sum(scale_total * scale_total)
     )
     factor = jnp.minimum(1.0, CLIP_NORM / gradient_norm)
     table_out = adam_update(embed_table, table_moment, table_second, grad_table, factor, TABLE_RATE)
@@ -487,27 +720,13 @@
     )
     scale_out = adam_update(log_scale, scale_moment, scale_second, scale_total, factor, SMALL_RATE)
     return (
-        table_out[0],
-        table_out[1],
-        table_out[2],
-        square_out[0],
-        square_out[1],
-        square_out[2],
-        expand_out[0],
-        expand_out[1],
-        expand_out[2],
-        reduce_out[0],
-        reduce_out[1],
-        reduce_out[2],
-        gains_out[0],
-        gains_out[1],
-        gains_out[2],
-        position_out[0],
-        position_out[1],
-        position_out[2],
-        scale_out[0],
-        scale_out[1],
-        scale_out[2],
+        *table_out,
+        *square_out,
+        *expand_out,
+        *reduce_out,
+        *gains_out,
+        *position_out,
+        *scale_out,
         losses,
         gradient_norm,
     )

time: 3030 us -> 1160 us (0.38)
  waiting for transfers between devices: 2180 us -> 442 us
  Pallas kernels: 0 us -> 272 us
  blocking collectives: 204 us -> 0 us
  other arithmetic: 209 us -> 71.6 us
  local copies, waits for them, and re-layouts: 227 us -> 185 us
    unnamed x16 -> x11, waiting for transfers between devices: 1440 us -> 0.15 us
    all_gather x4 -> x3, waiting for transfers between devices: 339 us -> 52 us  [whole(): parts = lax.all_gather(low, both, axis=0, tiled=False)]
    pallas_call x0 -> x9, Pallas kernels: none -> 272 us  [the longest x7 161 us: exchange(): pl.pallas_call(functools.partial(exchange_kernel, same), out_shape=jax.Sh...]
    scatter-add x1 -> x0, other arithmetic: 131 us -> none  [shards(): jax.ops.segment_sum(grad_tokens, all_tokens, num_segments=vocab_size)]
    all_gather x7 -> x0, blocking collectives: 125 us -> none  [the longest x1 40.6 us: shards(): lax.all_gather(embeds_low[hypo_start:answer_start], ('dp', 'fsdp'), axis=...]
    all_gather x3 -> x0, local copies, waits for them, and re-layouts: 63.7 us -> none  [the longest x1 62.2 us: shards(): lax.all_gather(table_low, ('dp', 'fsdp'), axis=0, tiled=True)]
    psum x1 -> x0, blocking collectives: 40.2 us -> none  [shards(): lax.psum((grad_position, grad_scale, jnp.stack([first_loss, second_loss])...]
    unnamed x2 -> x0, blocking collectives: 38.6 us -> none
  transfers between devices with their start and end apart: 12 -> 9, of which waited for: 9 -> 4; matrix products, arithmetic and copies ran while one was open for 15% -> 19% of each run, Pallas kernels for 0% -> 20%
where the time goes in v1:
time: 1160 us
  waiting for transfers between devices  442 us (38%)
  Pallas kernels  272 us (23%)
  local copies, waits for them, and re-layouts  185 us (16%)
  matrix products  154 us (13%)
  other arithmetic  71.6 us (6%)
  between operations  29.3 us (3%)
    reduce_scatter x1, waiting for transfers between devices, shards(): lax.psum_scatter(grad_squares, 'dp', scatter_dimension=1, tiled=True)  189 us
    reduce_scatter x1, waiting for transfers between devices, shards(): lax.psum_scatter(grad_expand, 'dp', scatter_dimension=0, tiled=True)  163 us
    pallas_call x7, Pallas kernels, exchange(): pl.pallas_call(functools.partial(exchange_kernel, same), out_shape=jax.Sh...  161 us
    pallas_call x1, Pallas kernels, scatter(): pl.pallas_call(functools.partial(scatter_kernel, fold), grid=(n,), out_sh...  66.2 us
    dot_general x16, matrix products, product_right(): lax.dot_general(left, right, (((1,), (1,)), ((), ())), preferred_element_...  53 us
    all_gather x3, waiting for transfers between devices, whole(): parts = lax.all_gather(low, both, axis=0, tiled=False)  52 us
    pallas_call x1, Pallas kernels, lookup(): pl.pallas_call(functools.partial(lookup_kernel, fold), grid=(n,), out_sha...  45.3 us
    unnamed x375, local copies, waits for them, and re-layouts  42.9 us
  transfers between devices with their start and end apart: 9, of which 4 were waited for; matrix products, arithmetic and copies ran while one was open for 19% of the time, Pallas kernels for 20%

profile of v1, /device:TPU:15, one launch (start us, length us, event | category | flops | bytes accessed | tf_op | source)
XLA Modules:
  0.0 1155.2 jit_solution(14386926557735962224)
XLA Ops:
  15.6 11.3 share_keys.1
  30.1 45.3 %lookup.1.src = bf16[32,48,512]{2,1,0:T(8,128)(2,1)S(1)} custom-call(s32[32,1,1024]{2,1,0:T(1,128)S(1)} %bitcast.295, s32[32,1,1024]{2,1,0:T(1,128)S(1)} %bitcast.293, f32[24,32128]{1,0:T(8,128)S(1)} %convert_convert_fusion.table_ref), custom_call_target="tpu_custom_call" | custom-call | tf_op jit(solution)/shard_map/lookup/pallas_call | solution.py:346
  76.6 45.5 %send_features.1 = bf16[32,48,512]{2,1,0:T(8,128)(2,1)} custom-call(bf16[32,48,512]{2,1,0:T(8,128)(2,1)} %copy-done.1), custom_call_target="tpu_custom_call" | custom-call | tf_op jit(solution)/shard_map/send_features/pallas_call | solution.py:482
  127.2 9.9 share_gains.1
  143.8 12.0 %share_negatives.1 = s32[32,8,128]{2,1,0:T(8,128)} custom-call(s32[1,8,128]{2,1,0:T(8,128)} %pad_bitcast_fusion.1.src), custom_call_target="tpu_custom_call" | custom-call | tf_op jit(solution)/shard_map/share_negatives/pallas_call | solution.py:482
  166.5 6.0 copy.428
  175.7 8.2 reshape.662
  190.2 52.0 %all-gather.7.cloned.1.call-done = bf16[160,96,192]{2,1,0:T(8,128)(2,1)} async-done(((bf16[5,96,192]{2,1,0:T(8,128)(2,1)}), bf16[160,96,192]{2,1,0:T(8,128)(2,1)}) %all-gather.7.cloned.1.call-update) | async-done | bytes 5898256 | tf_op jit(solution)/shard_map/all_gather | solution.py:550
  242.2 11.2 copy.418
  253.5 5.6 fusion.135
  262.9 4.2 squeeze.14
  312.5 4.6 fusion.127
  317.3 5.1 multiply_reduce_fusion.15
  349.2 4.6 fusion.126
  366.6 23.2 %share_embeds.1 = bf16[32,16,768]{2,1,0:T(8,128)(2,1)} custom-call(bf16[1,16,768]{2,1,0:T(8,128)(2,1)} %pad_bitcast_fusion.src), custom_call_target="tpu_custom_call" | custom-call | tf_op jit(solution)/shard_map/share_embeds/pallas_call | solution.py:482
  407.8 7.0 fusion.96
  414.9 5.9 convolution_add_fusion
  420.8 8.9 fusion.6
  432.6 9.3 fusion.13
  443.6 5.4 convolution_add_fusion.1
  449.1 6.1 fusion.146
  455.3 6.2 multiply_reduce_fusion.7
  470.4 4.2 copy.450
  537.4 7.2 pad_maximum_fusion
  544.6 38.0 %reduce-scatter.17.cloned.1.call-done = f32[384,768]{1,0:T(8,128)} async-done(((f32[3072,768]{1,0:T(8,128)}), f32[384,768]{1,0:T(8,128)}) %reduce-scatter.17.cloned.1.call-update) | async-done | bytes 1179664 | tf_op jit(solution)/shard_map/reduce_scatter | solution.py:679
  585.4 163.3 %reduce-scatter.13.cloned.1.call-done = f32[96,3072]{1,0:T(8,128)} async-done(((f32[768,3072]{1,0:T(8,128)}), f32[96,3072]{1,0:T(8,128)}) %reduce-scatter.13.cloned.1.call-update) | async-done | bytes 1179664 | tf_op jit(solution)/shard_map/reduce_scatter | solution.py:676
  758.6 188.7 %reduce-scatter.11.cloned.1.call-done = f32[5,96,768]{2,1,0:T(8,128)} async-done(((f32[5,768,768]{2,1,0:T(8,128)}), f32[5,96,768]{2,1,0:T(8,128)}) %reduce-scatter.11.cloned.1.call-update) | async-done | bytes 1474576 | tf_op jit(solution)/shard_map/reduce_scatter | solution.py:672
  955.2 6.1 multiply_reduce_fusion.8
  980.2 44.6 %send_gradients.1.grad_ref = bf16[32,48,512]{2,1,0:T(8,128)(2,1)} custom-call(bf16[32,48,512]{2,1,0:T(8,128)(2,1)} %bitcast.314), custom_call_target="tpu_custom_call" | custom-call | tf_op jit(solution)/shard_map/send_gradients/pallas_call | solution.py:482
  1026.2 66.2 %scatter.1 = f32[24,32128]{1,0:T(8,128)S(1)} custom-call(s32[32,1,1024]{2,1,0:T(1,128)S(1)} %bitcast.296, s32[32,1,1024]{2,1,0:T(1,128)S(1)} %bitcast.294, bf16[32,48,512]{2,1,0:T(8,128)(2,1)S(1)} %copy-done), custom_call_target="tpu_custom_call" | custom-call | tf_op jit(solution)/shard_map/scatter/pallas_call | solution.py:408
  1110.9 14.3 %share_small.1 = f32[32,24,128]{2,1,0:T(8,128)} custom-call(f32[1,24,128]{2,1,0:T(8,128)} %fusion.111.src), custom_call_target="tpu_custom_call" | custom-call | tf_op jit(solution)/shard_map/share_small/pallas_call | solution.py:482
  1133.4 6.8 multiply_subtract_fusion
  (600 shorter events, 288.7 us)
Async XLA Ops:
  7.2 159.3 %all-gather.9.cloned.1.call-start = ((), (), s32[]{:S(2)}) async-start(), calls=%async_computation.11 | async-start | bytes 4866048 | tf_op jit(solution)/shard_map/all_gather | solution.py:550
  8.9 166.8 %all-gather.11.cloned.1.call-start = ((), (), s32[]{:S(2)}) async-start(), calls=%async_computation.12 | async-start | bytes 4866048 | tf_op jit(solution)/shard_map/all_gather | solution.py:550
  10.7 231.6 %all-gather.7.cloned.1.call-start = ((), (), s32[]{:S(2)}) async-start(), calls=%async_computation.10 | async-start | bytes 8110080 | tf_op jit(solution)/shard_map/all_gather | solution.py:550
  12.5 570.2 %reduce-scatter.17.cloned.1.call-start = ((), (), s32[]{:S(2)}) async-start(), calls=%async_computation.9 | async-start | bytes 10616832 | tf_op jit(solution)/shard_map/reduce_scatter | solution.py:679
  125.1 13.2 %copy-start.40 = (f32[16384,32]{0,1:T(8,128)S(1)}, f32[16384,32]{0,1:T(8,128)}, u32[]{:S(2)}) copy-start(f32[16384,32]{0,1:T(8,128)} %constant.101.clone) | copy-start | bytes 6291460
  125.1 13.2 %copy-start.103 = (f32[32,12]{0,1:T(8,128)S(1)}, f32[32,12]{0,1:T(8,128)}, u32[]{:S(2)}) copy-start(f32[32,12]{0,1:T(8,128)} %param.37) | copy-start | bytes 4612
  138.3 26.1 %copy-start.105 = (f32[768]{0:T(1024)}, f32[768]{0:T(1024)S(1)}, u32[]{:S(2)}) copy-start(f32[768]{0:T(1024)S(1)} %mul.905) | copy-start | bytes 9220
  141.0 15.8 %copy-start.170 = (s32[4]{0:T(128)S(1)}, s32[4]{0:T(128)}, u32[]{:S(2)}) copy-start(s32[4]{0:T(128)} %param.55) | copy-start | bytes 52
  141.9 216.6 %copy-start.107 = (f32[768]{0:T(1024)}, f32[768]{0:T(1024)S(1)}, u32[]{:S(2)}) copy-start(f32[768]{0:T(1024)S(1)} %mul.922) | copy-start | bytes 9220
  161.7 147.6 %copy-start.6 = (f32[1024,768]{1,0:T(8,128)}, f32[1024,768]{1,0:T(8,128)S(1)}, u32[]{:S(2)}) copy-start(f32[1024,768]{1,0:T(8,128)S(1)} %fusion.15) | copy-start | bytes 9437188
  322.9 35.6 %copy-start.111 = (f32[512]{0:T(512)}, f32[512]{0:T(512)S(1)}, u32[]{:S(2)}) copy-start(f32[512]{0:T(512)S(1)} %get-tuple-element.250) | copy-start | bytes 6148
  365.8 30.3 %copy-start.69 = (f32[12,768]{1,0:T(8,128)}, f32[12,768]{1,0:T(8,128)S(1)}, u32[]{:S(2)}) copy-start(f32[12,768]{1,0:T(8,128)S(1)} %get-tuple-element.268) | copy-start | bytes 110596
  365.9 27.2 %copy-start.139 = (f32[12]{0:T(128)}, f32[12]{0:T(128)S(1)}, u32[]{:S(2)}) copy-start(f32[12]{0:T(128)S(1)} %add_rsqrt_fusion.6) | copy-start | bytes 148
  420.8 9.0 copy-start.98
  420.8 327.9 %reduce-scatter.13.cloned.1.call-start = ((), (), s32[]{:S(2)}) async-start(), calls=%async_computation.7 | async-start | bytes 10616832 | tf_op jit(solution)/shard_map/reduce_scatter | solution.py:676
  432.6 11.0 copy-start.12
  432.6 11.0 copy-start.102
  449.0 498.3 %reduce-scatter.11.cloned.1.call-start = ((), (), s32[]{:S(2)}) async-start(), calls=%async_computation.6 | async-start | bytes 13271040 | tf_op jit(solution)/shard_map/reduce_scatter | solution.py:672
  518.4 11.5 copy-start.45
  544.6 553.7 %reduce-scatter.21.cloned.1.call-start = ((), (), s32[]{:S(2)}) async-start(), calls=%async_computation.14 | async-start | bytes 1474560
  585.3 164.7 %copy-start.62 = (bf16[512,768]{0,1:T(8,128)(2,1)S(1)}, bf16[512,768]{0,1:T(8,128)(2,1)}, u32[]{:S(2)}) copy-start(bf16[512,768]{0,1:T(8,128)(2,1)} %reshape.679) | copy-start | bytes 2359300
  585.3 164.7 %copy-start.78 = (bf16[768,768]{0,1:T(8,128)(2,1)S(1)}, bf16[768,768]{0,1:T(8,128)(2,1)}, u32[]{:S(2)}) copy-start(bf16[768,768]{0,1:T(8,128)(2,1)} %squeeze.14) | copy-start | bytes 3538948
  585.4 514.0 %reduce-scatter.15.cloned.1.call-start = ((), (), s32[]{:S(2)}) async-start(), calls=%async_computation.8 | async-start | bytes 1474560 | tf_op jit(solution)/shard_map/reduce_scatter | solution.py:675
  748.7 353.1 %reduce-scatter.19.cloned.1.call-start = ((), (), s32[]{:S(2)}) async-start(), calls=%async_computation.13 | async-start | bytes 1966080
  980.2 44.6 %copy-start.3 = (s32[32,8,128]{2,1,0:T(8,128)S(1)}, s32[32,8,128]{2,1,0:T(8,128)}, u32[]{:S(2)}) copy-start(s32[32,8,128]{2,1,0:T(8,128)} %copy-done.2) | copy-start | bytes 393220
  980.2 44.6 %copy-start.5 = (s32[32,8,128]{2,1,0:T(8,128)S(1)}, s32[32,8,128]{2,1,0:T(8,128)}, u32[]{:S(2)}) copy-start(s32[32,8,128]{2,1,0:T(8,128)} %copy-done.4) | copy-start | bytes 393220
  1026.2 67.5 %copy-start.128 = (f32[128]{0:T(128)S(1)}, f32[128]{0:T(128)}, u32[]{:S(2)}) copy-start(f32[128]{0:T(128)} %copy-done.127) | copy-start | bytes 1540
  1026.2 67.5 %copy-start.146 = (f32[128]{0:T(128)S(1)}, f32[128]{0:T(128)}, u32[]{:S(2)}) copy-start(f32[128]{0:T(128)} %copy-done.145) | copy-start | bytes 1540
  1026.2 67.6 %copy-start.156 = (f32[128]{0:T(128)S(1)}, f32[128]{0:T(128)}, u32[]{:S(2)}) copy-start(f32[128]{0:T(128)} %get-tuple-element.177) | copy-start | bytes 1540
  1026.2 68.2 %copy-start.126 = (f32[64]{0:T(128)S(1)}, f32[64]{0:T(128)}, u32[]{:S(2)}) copy-start(f32[64]{0:T(128)} %copy-done.125) | copy-start | bytes 772
  1026.2 68.2 %copy-start.144 = (f32[64]{0:T(128)S(1)}, f32[64]{0:T(128)}, u32[]{:S(2)}) copy-start(f32[64]{0:T(128)} %copy-done.143) | copy-start | bytes 772
  1026.2 68.2 %copy-start.155 = (f32[64]{0:T(128)S(1)}, f32[64]{0:T(128)}, u32[]{:S(2)}) copy-start(f32[64]{0:T(128)} %get-tuple-element.182) | copy-start | bytes 772
  (158 other events, 538.5 us)
Sparse Core Ops, SparseCore 0:
  11.6 64.5 all-gather.8
  79.7 84.9 all-gather.10
  168.1 74.0 all-gather.6
  420.9 161.7 reduce-scatter.16
  586.1 162.5 reduce-scatter.12
  752.1 195.1 reduce-scatter.10
  950.1 25.6 reduce-scatter.20
  978.3 30.0 reduce-scatter.14
  1011.1 30.3 reduce-scatter.18

commit v2 on v1

--- a/solution.py
+++ b/solution.py
@@ -65,217 +65,10 @@
     )
 
 
-def norm_scale(values):
-    return lax.rsqrt(jnp.mean(values * values, axis=-1, keepdims=True) + NORM_EPS)
-
-
-def norm_back(values, scale, gain, grad):
-    weighted = grad * gain
-    inner = jnp.mean(weighted * values, axis=-1, keepdims=True)
-    return (scale * weighted - values * scale**3 * inner, jnp.sum(grad * values * scale, axis=0))
-
-
 def attention_bias(position_bias, length):
     onehot = bucket_onehot(length)
     flat_bias = jnp.dot(onehot, position_bias, precision=HIGHEST)
     return (jnp.transpose(flat_bias.reshape(length, length, HEADS), (2, 0, 1)), onehot)
-
-
-def attention_scores(queries, keys_here, bias_table, key_mask):
-    scores = (
-        jnp.einsum("bqhe,bkhe->bhqk", queries, keys_here, preferred_element_type=jnp.float32)
-        * HEAD ** (-0.5)
-        + bias_table[None]
-    )
-    return jnp.where(key_mask[:, None, None, :], scores, -1e30)
-
-
-def layer_forward(start_rows, key_mask, layer, length):
-    square_low, expand_low, reduce_low, gain_rows, position_bias = layer
-    head_shape = (key_mask.shape[0], length, HEADS, HEAD)
-    scale_one = norm_scale(start_rows)
-    normed_one = (start_rows * scale_one * gain_rows[0]).astype(jnp.bfloat16)
-    queries = product(normed_one, square_low[0]).astype(jnp.bfloat16)
-    keys_here = product(normed_one, square_low[1]).astype(jnp.bfloat16)
-    values_here = product(normed_one, square_low[2]).astype(jnp.bfloat16)
-    bias_table, onehot = attention_bias(position_bias, length)
-    scores = attention_scores(
-        queries.reshape(head_shape), keys_here.reshape(head_shape), bias_table, key_mask
-    )
-    row_top = jnp.max(scores, axis=-1, keepdims=True)
-    raised = jnp.exp(scores - row_top)
-    row_total = jnp.sum(raised, axis=-1, keepdims=True)
-    log_total = row_top + jnp.log(row_total)
-    attend = (raised / row_total).astype(jnp.bfloat16)
-    mixed_heads = (
-        jnp.einsum(
-            "bhqk,bkhe->bqhe",
-            attend,
-            values_here.reshape(head_shape),
-            preferred_element_type=jnp.float32,
-        )
-        .reshape(-1, D)
-        .astype(jnp.bfloat16)
-    )
-    middle = start_rows + product(mixed_heads, square_low[3])
-    scale_two = norm_scale(middle)
-    normed_two = (middle * scale_two * gain_rows[1]).astype(jnp.bfloat16)
-    hidden_pre = product(normed_two, expand_low)
-    hidden_act = jax.nn.gelu(hidden_pre).astype(jnp.bfloat16)
-    ending = middle + product(hidden_act, reduce_low)
-    scale_three = norm_scale(ending)
-    output = ending * scale_three * gain_rows[2]
-    stored = (
-        start_rows,
-        scale_one,
-        normed_one,
-        queries,
-        keys_here,
-        values_here,
-        log_total,
-        mixed_heads,
-        middle,
-        scale_two,
-        normed_two,
-        hidden_pre,
-        hidden_act,
-        ending,
-        scale_three,
-    )
-    return (output, stored)
-
-
-def layer_backward(grad_out, key_mask, layer, stored, length):
-    square_low, expand_low, reduce_low, gain_rows, position_bias = layer
-    (
-        start_rows,
-        scale_one,
-        normed_one,
-        queries,
-        keys_here,
-        values_here,
-        log_total,
-        mixed_heads,
-        middle,
-        scale_two,
-        normed_two,
-        hidden_pre,
-        hidden_act,
-        ending,
-        scale_three,
-    ) = stored
-    head_shape = (key_mask.shape[0], length, HEADS, HEAD)
-    grad_end, gain_three = norm_back(ending, scale_three, gain_rows[2], grad_out)
-    grad_end_low = grad_end.astype(jnp.bfloat16)
-    grad_reduce = product_left(hidden_act, grad_end_low)
-    grad_act = product_right(grad_end_low, reduce_low)
-    grad_pre = jax.vjp(jax.nn.gelu, hidden_pre)[1](grad_act)[0].astype(jnp.bfloat16)
-    grad_expand = product_left(normed_two, grad_pre)
-    grad_normed_two = product_right(grad_pre, expand_low)
-    grad_mid_norm, gain_two = norm_back(middle, scale_two, gain_rows[1], grad_normed_two)
-    grad_middle = grad_end + grad_mid_norm
-    grad_mid_low = grad_middle.astype(jnp.bfloat16)
-    grad_output_proj = product_left(mixed_heads, grad_mid_low)
-    grad_mixed = product_right(grad_mid_low, square_low[3]).astype(jnp.bfloat16).reshape(head_shape)
-    bias_table, onehot = attention_bias(position_bias, length)
-    query_heads = queries.reshape(head_shape)
-    key_heads = keys_here.reshape(head_shape)
-    value_heads = values_here.reshape(head_shape)
-    scores = attention_scores(query_heads, key_heads, bias_table, key_mask)
-    attend_full = jnp.exp(scores - log_total)
-    attend = attend_full.astype(jnp.bfloat16)
-    grad_attend = jnp.einsum(
-        "bqhe,bkhe->bhqk", grad_mixed, value_heads, preferred_element_type=jnp.float32
-    )
-    grad_values = (
-        jnp.einsum("bhqk,bqhe->bkhe", attend, grad_mixed, preferred_element_type=jnp.float32)
-        .astype(jnp.bfloat16)
-        .reshape(-1, D)
-    )
-    grad_scores = attend_full * (
-        grad_attend - jnp.sum(grad_attend * attend_full, axis=-1, keepdims=True)
-    )
-    grad_scores_low = grad_scores.astype(jnp.bfloat16)
-    grad_queries = (
-        (
-            jnp.einsum(
-                "bhqk,bkhe->bqhe", grad_scores_low, key_heads, preferred_element_type=jnp.float32
-            )
-            * HEAD ** (-0.5)
-        )
-        .astype(jnp.bfloat16)
-        .reshape(-1, D)
-    )
-    grad_keys = (
-        (
-            jnp.einsum(
-                "bhqk,bqhe->bkhe", grad_scores_low, query_heads, preferred_element_type=jnp.float32
-            )
-            * HEAD ** (-0.5)
-        )
-        .astype(jnp.bfloat16)
-        .reshape(-1, D)
-    )
-    summed_scores = jnp.sum(grad_scores_low.astype(jnp.float32), axis=0).reshape(
-        HEADS, length * length
-    )
-    grad_position = lax.dot_general(
-        onehot, summed_scores, (((0,), (1,)), ((), ())), precision=HIGHEST
-    )
-    grad_normed_one = (
-        product_right(grad_queries, square_low[0])
-        + product_right(grad_keys, square_low[1])
-        + product_right(grad_values, square_low[2])
-    )
-    grad_start_norm, gain_one = norm_back(start_rows, scale_one, gain_rows[0], grad_normed_one)
-    grad_start = grad_middle + grad_start_norm
-    grad_squares = jnp.stack(
-        [
-            product_left(normed_one, grad_queries),
-            product_left(normed_one, grad_keys),
-            product_left(normed_one, grad_values),
-            grad_output_proj,
-        ]
-    )
-    return (
-        grad_start,
-        (
-            grad_squares,
-            grad_expand,
-            grad_reduce,
-            jnp.stack([gain_one, gain_two, gain_three]),
-            grad_position,
-        ),
-    )
-
-
-def contrast_local(left_low, right_low, scale, extra, target):
-    sims = product_right(left_low, right_low)
-    logits = scale * sims
-    row_top = jnp.max(logits, axis=1, keepdims=True)
-    raised = (1.0 + extra) * jnp.exp(logits - row_top)
-    row_total = jnp.sum(raised, axis=1, keepdims=True)
-    spread = row_top[:, 0] + jnp.log(row_total[:, 0])
-    target_hit = jnp.arange(right_low.shape[0])[None, :] == target[:, None]
-    loss_sum = jnp.sum(spread - jnp.sum(jnp.where(target_hit, logits, 0.0), axis=1))
-    grad_logits = raised / row_total - target_hit.astype(jnp.float32)
-    grad_scale = jnp.sum(grad_logits * sims)
-    grad_sims = (scale * grad_logits).astype(jnp.bfloat16)
-    return (loss_sum, grad_scale, product(grad_sims, right_low), product_left(grad_sims, left_low))
-
-
-def pool_rows(output, key_mask, lengths, length):
-    shaped = output.reshape(key_mask.shape[0], length, D)
-    return jnp.sum(jnp.where(key_mask[:, :, None], shaped, 0.0), axis=1) / lengths[:, None].astype(
-        jnp.float32
-    )
-
-
-def spread_rows(grad_rows, key_mask, lengths):
-    spread = jnp.where(key_mask[:, :, None], grad_rows[:, None, :], 0.0) / lengths[
-        :, None, None
-    ].astype(jnp.float32)
-    return spread.reshape(-1, D)
 
 
 def adam_update(weight, moment, second, grad, factor, rate):
@@ -293,7 +86,7 @@
 LANES = 128
 GROUPS = 4
 SLOT = LANES // GROUPS
-VMEM_CAP = 48 * 1024 * 1024
+VMEM_CAP = 56 * 1024 * 1024
 
 def fold_rows(vocab):
     per = -(-vocab // GROUPS)
@@ -427,9 +220,9 @@
     same_before = (key[:, None] == key[None, :]) & (places[:, None] < places[None, :])
     first = ~jnp.any(same_before, axis=0)
     rank = jnp.sum(((key[None, :] < key[:, None]) & first[None, :]).astype(jnp.int32), axis=1)
-    hit = rank[:, None] == places[None, :]
-    packed = GROUPS * fold + jnp.sum(jnp.where(hit & first[:, None], key[:, None] - GROUPS * fold, 0), axis=0)
-    return packed, hit.astype(jnp.bfloat16)
+    hit = (rank[:, None] == places[None, :]) & first[:, None]
+    packed = GROUPS * fold + jnp.sum(jnp.where(hit, key[:, None] - GROUPS * fold, 0), axis=0)
+    return packed, rank
 
 
 MESH = pl.DeviceIdType.MESH
@@ -492,6 +285,927 @@
         compiler_params=pltpu.CompilerParams(collective_id=call_id, has_side_effects=True),
         name=name,
     )(blocks)
+
+
+SQUARE, EXPAND, REDUCE = range(3)
+KINDS = 3
+STEPS = (5, 6, 4)
+FIRST = (3, 3, 2)
+
+
+def spot(refs, kind, z, x, y, core):
+    dp = z * 2 + x
+    column = y * 2 + core
+    if kind == SQUARE:
+        return refs[kind].at[
+            :,
+            pl.ds(pl.multiple_of(dp * 96 + core * 48, 16), 48),
+            pl.ds(pl.multiple_of(y * 384, 128), 384),
+        ]
+    if kind == EXPAND:
+        return refs[kind].at[
+            pl.ds(pl.multiple_of(dp * 96, 16), 96), pl.ds(pl.multiple_of(column * 768, 128), 768)
+        ]
+    return refs[kind].at[
+        pl.ds(pl.multiple_of(column * 192, 16), 192), pl.ds(pl.multiple_of(dp * 384, 128), 384)
+    ]
+
+
+def spot_part(refs, kind, z, x, y, core, part):
+    dp = z * 2 + x
+    column = y * 2 + core
+    if kind == SQUARE:
+        return refs[kind].at[
+            pl.ds(0, 3) if part == 0 else pl.ds(3, 2),
+            pl.ds(pl.multiple_of(dp * 96 + core * 48, 16), 48),
+            pl.ds(pl.multiple_of(y * 384, 128), 384),
+        ]
+    if kind == EXPAND:
+        return refs[kind].at[
+            pl.ds(pl.multiple_of(dp * 96 + part * 48, 16), 48),
+            pl.ds(pl.multiple_of(column * 768, 128), 768),
+        ]
+    return refs[kind].at[
+        pl.ds(pl.multiple_of(column * 192 + part * 96, 16), 96),
+        pl.ds(pl.multiple_of(dp * 384, 128), 384),
+    ]
+
+
+def block_part(ref, kind, part):
+    if kind == SQUARE:
+        return ref.at[pl.ds(0, 3) if part == 0 else pl.ds(3, 2)]
+    half = 48 if kind == EXPAND else 96
+    return ref.at[pl.ds(part * half, half)]
+
+
+def block_step(ref, kind, k):
+    if kind == SQUARE:
+        return ref.at[k]
+    rows = 16 if kind == EXPAND else 48
+    return ref.at[pl.ds(pl.multiple_of(k * rows, 16), rows)]
+
+
+BLOCKS = ((5, 48, 384), (96, 768), (192, 384))
+
+
+def place():
+    dp, fsdp = lax.axis_index("dp"), lax.axis_index("fsdp")
+    return dp // 2, lax.rem(dp, 2), fsdp // 2, lax.rem(fsdp, 2)
+
+
+def device_at(z, x, y, core):
+    return (z * 2 + x, y * 2 + core)
+
+
+def greet_neighbours(depth):
+    z, x, y, core = place()
+    barrier = pltpu.get_barrier_semaphore()
+
+    def hello(target):
+        pl.semaphore_signal(barrier, inc=1, device_id=target, device_id_type=MESH)
+
+    hello(device_at(z, x, y, 1 - core))
+    hello(device_at(z, 1 - x, y, core))
+    hello(device_at(z, x, 1 - y, core))
+
+    @pl.when(z > 0)
+    def _():
+        hello(device_at(z - 1, x, y, core))
+
+    @pl.when(z < depth - 1)
+    def _():
+        hello(device_at(z + 1, x, y, core))
+
+    above = jnp.where(z < depth - 1, 1, 0)
+    below = jnp.where(z > 0, 1, 0)
+    pl.semaphore_wait(barrier, 3 + above + below)
+
+
+def remote(src, dst, send_sem, recv_sem, target):
+    return pltpu.make_async_remote_copy(
+        src_ref=src, dst_ref=dst, send_sem=send_sem, recv_sem=recv_sem,
+        device_id=target, device_id_type=MESH)
+
+
+def gather_kernel(depth, *refs):
+    mine, outs = refs[:KINDS], refs[KINDS : 2 * KINDS]
+    theirs, own = refs[2 * KINDS : 2 * KINDS + 2]
+    pair_send, pair_recv, own_sem, send, got, sib_send, sib_got, diag_got = refs[2 * KINDS + 2 :]
+    z, x, y, core = place()
+    sibling = device_at(z, x, y, 1 - core)
+    x_next, y_next = device_at(z, 1 - x, y, core), device_at(z, x, 1 - y, core)
+    greet_neighbours(depth)
+    pair = remote(mine[SQUARE].at[1 - core], theirs, pair_send, pair_recv, sibling)
+    pair.start()
+
+    def number(z_at, x_at, y_at):
+        return (z_at * 2 + x_at) * 2 + y_at
+
+    def to(way, a, z_at, x_at, y_at, target, part=None, src=None):
+        k = number(z_at, x_at, y_at)
+        if part is None:
+            spot_at, recv = spot(outs, a, z_at, x_at, y_at, core), got.at[a, k]
+        else:
+            spot_at = spot_part(outs, a, z_at, x_at, y_at, core, part)
+            recv = diag_got.at[a, z_at, part]
+        return remote(spot_at if src is None else src, spot_at, send.at[way, a, k], recv, target)
+
+    def to_sibling(a, z_at, x_at, y_at, src=None):
+        spot_at = spot(outs, a, z_at, x_at, y_at, core)
+        k = number(z_at, x_at, y_at)
+        return remote(spot_at if src is None else src, spot_at, sib_send.at[a, k], sib_got.at[a, k], sibling)
+
+    def from_sibling(a, z_at, x_at, y_at):
+        spot_at = spot(outs, a, z_at, x_at, y_at, 1 - core)
+        k = number(z_at, x_at, y_at)
+        return remote(spot_at, spot_at, sib_send.at[a, k], sib_got.at[a, k], sibling)
+
+    UP, DOWN, ACROSS_X, ACROSS_Y = range(4)
+    sources = [own, mine[EXPAND], mine[REDUCE]]
+    for a in (EXPAND, REDUCE, SQUARE):
+        if a == SQUARE:
+            row = lax.broadcasted_iota(jnp.int32, (192, 384), 0)
+            col = lax.broadcasted_iota(jnp.int32, (192, 384), 1)
+            here = (row + core * 192 == col).astype(jnp.float32).astype(jnp.bfloat16)
+            there = (row + (1 - core) * 192 == col).astype(jnp.float32).astype(jnp.bfloat16)
+            pair.wait_recv()
+            for k in range(5):
+                block = jnp.dot(mine[a][core, k], here, preferred_element_type=jnp.float32) + jnp.dot(
+                    theirs[k], there, preferred_element_type=jnp.float32
+                )
+                own[k] = block.astype(jnp.bfloat16)
+        pltpu.make_async_copy(sources[a], spot(outs, a, z, x, y, core), own_sem.at[a]).start()
+
+        @pl.when(z < depth - 1)
+        def _():
+            to(UP, a, z, x, y, device_at(z + 1, x, y, core), src=sources[a]).start()
+
+        @pl.when(z > 0)
+        def _():
+            to(DOWN, a, z, x, y, device_at(z - 1, x, y, core), src=sources[a]).start()
+
+        to(ACROSS_X, a, z, x, y, x_next, src=sources[a]).start()
+        to(ACROSS_Y, a, z, x, y, y_next, src=sources[a]).start()
+        to_sibling(a, z, x, y, src=sources[a]).start()
+
+    def sides(step, act):
+        if step == 0:
+            act(z)
+            return
+        for sign in (1, -1):
+            z_at = z + sign * step
+
+            @pl.when((z_at >= 0) & (z_at < depth))
+            def _():
+                act(z_at)
+
+    def first(step):
+        def act(z_at):
+            for a in range(KINDS):
+                to(UP, a, z_at, x, y, sibling).wait_recv()
+
+                @pl.when((z_at < z) & (z < depth - 1))
+                def _():
+                    to(UP, a, z_at, x, y, device_at(z + 1, x, y, core)).start()
+
+                @pl.when((z_at > z) & (z > 0))
+                def _():
+                    to(DOWN, a, z_at, x, y, device_at(z - 1, x, y, core)).start()
+
+                to(ACROSS_X, a, z_at, x, y, x_next).start()
+                to(ACROSS_Y, a, z_at, x, y, y_next).start()
+                to_sibling(a, z_at, x, y).start()
+
+        sides(step, act)
+
+    def second(step):
+        def act(z_at):
+            for a in range(KINDS):
+                to(UP, a, z_at, 1 - x, y, sibling).wait_recv()
+                to(ACROSS_Y, a, z_at, 1 - x, y, y_next, 0).start()
+                to_sibling(a, z_at, 1 - x, y).start()
+                to(UP, a, z_at, x, 1 - y, sibling).wait_recv()
+                to(ACROSS_X, a, z_at, x, 1 - y, x_next, 1).start()
+                to_sibling(a, z_at, x, 1 - y).start()
+
+        sides(step, act)
+
+    def third(step):
+        def act(z_at):
+            for a in range(KINDS):
+                for part in range(2):
+                    to(UP, a, z_at, 1 - x, 1 - y, sibling, part).wait_recv()
+                to_sibling(a, z_at, 1 - x, 1 - y).start()
+
+        sides(step, act)
+
+    for step in range(1, depth + 2):
+        if step < depth:
+            first(step)
+        if 0 <= step - 1 < depth:
+            second(step - 1)
+        if 0 <= step - 2 < depth:
+            third(step - 2)
+
+    pair.wait_send()
+    for a in range(KINDS):
+        pltpu.make_async_copy(sources[a], spot(outs, a, z, x, y, core), own_sem.at[a]).wait()
+
+    def finish(z_at, carry):
+        for a in range(KINDS):
+
+            @pl.when((z_at <= z) & (z < depth - 1))
+            def _():
+                to(UP, a, z_at, x, y, x_next).wait_send()
+
+            @pl.when((z_at >= z) & (z > 0))
+            def _():
+                to(DOWN, a, z_at, x, y, x_next).wait_send()
+
+            to(ACROSS_X, a, z_at, x, y, x_next).wait_send()
+            to(ACROSS_Y, a, z_at, x, y, y_next).wait_send()
+            to(ACROSS_Y, a, z_at, 1 - x, y, y_next, 0).wait_send()
+            to(ACROSS_X, a, z_at, x, 1 - y, x_next, 1).wait_send()
+            for x_at in range(2):
+                for y_at in range(2):
+                    to_sibling(a, z_at, x_at, y_at).wait_send()
+                    from_sibling(a, z_at, x_at, y_at).wait_recv()
+        return carry
+
+    lax.fori_loop(0, depth, finish, 0)
+
+
+def gather_blocks(square, expand, reduce_turned, call_id):
+    depth = lax.axis_size("dp") // 2
+    count = 4 * depth
+    return pl.pallas_call(
+        functools.partial(gather_kernel, depth),
+        out_shape=[
+            jax.ShapeDtypeStruct((5, 768, 768), jnp.bfloat16),
+            jax.ShapeDtypeStruct((768, 3072), jnp.bfloat16),
+            jax.ShapeDtypeStruct((768, 3072), jnp.bfloat16),
+        ],
+        in_specs=[pl.BlockSpec(memory_space=pltpu.VMEM)] * KINDS,
+        out_specs=[pl.BlockSpec(memory_space=pltpu.VMEM)] * KINDS,
+        scratch_shapes=[
+            pltpu.VMEM((5, 48, 192), jnp.bfloat16),
+            pltpu.VMEM((5, 48, 384), jnp.bfloat16),
+            pltpu.SemaphoreType.DMA,
+            pltpu.SemaphoreType.DMA,
+            pltpu.SemaphoreType.DMA((KINDS,)),
+            pltpu.SemaphoreType.DMA((4, KINDS, count)),
+            pltpu.SemaphoreType.DMA((KINDS, count)),
+            pltpu.SemaphoreType.DMA((KINDS, count)),
+            pltpu.SemaphoreType.DMA((KINDS, count)),
+            pltpu.SemaphoreType.DMA((KINDS, depth, 2)),
+        ],
+        compiler_params=pltpu.CompilerParams(
+            collective_id=call_id, has_side_effects=True, vmem_limit_bytes=VMEM_CAP
+        ),
+        name="gather_layer",
+    )(square, expand, reduce_turned)
+
+
+def reduce_kernel(depth, *refs):
+    count = KINDS
+    grads, outs = refs[:count], refs[count : 2 * count]
+    work, paired, step_one, from_x, from_y, from_z = [
+        refs[(2 + k) * count : (3 + k) * count] for k in range(6)
+    ]
+    spare = refs[8 * count]
+    load_sem, pair_send, pair_got, send, one_got, x_got, y_got, z_got, end_send, end_got = refs[8 * count + 1 :]
+    z, x, y, core = place()
+    sibling = device_at(z, x, y, 1 - core)
+    x_next, y_next = device_at(z, 1 - x, y, core), device_at(z, x, 1 - y, core)
+    greet_neighbours(depth)
+
+    def index(z_at, x_at):
+        return z_at * 2 + x_at
+
+    def load(a, z_at, x_at, y_at):
+        i = index(z_at, x_at)
+        return pltpu.make_async_copy(
+            spot(grads, a, z_at, x_at, y_at, core), work[a].at[i, y_at], load_sem.at[a, i, y_at]
+        )
+
+    def pair(a, z_at, x_at, y_at):
+        i = index(z_at, x_at)
+        return remote(
+            spot(grads, a, z_at, x_at, y_at, 1 - core),
+            paired[a].at[i, y_at],
+            pair_send.at[a, i, y_at],
+            pair_got.at[a, i, y_at],
+            sibling,
+        )
+
+    rounds = list(range(depth - 1, -1, -1))
+
+    def sides(step, act):
+        if step == 0:
+            act(z)
+            return
+        for sign in (1, -1):
+            z_at = z + sign * step
+
+            @pl.when((z_at >= 0) & (z_at < depth))
+            def _():
+                act(z_at)
+
+    for x_at, y_at in ((1 - x, 1 - y), (1 - x, y), (x, 1 - y), (x, y)):
+        for step in rounds:
+
+            def begin(z_at):
+                for a in range(count):
+                    load(a, z_at, x_at, y_at).start()
+                    pair(a, z_at, x_at, y_at).start()
+
+            sides(step, begin)
+
+    def ready(a, z_at, x_at, y_at):
+        load(a, z_at, x_at, y_at).wait()
+        pair(a, z_at, x_at, y_at).wait_recv()
+
+    def total(a, z_at, x_at, y_at, first, last, extra=()):
+        i = index(z_at, x_at)
+
+        def add(k, carry):
+            here = block_step(work[a].at[i, y_at], a, k)
+            value = here[...].astype(jnp.float32)
+            value = value + block_step(paired[a].at[i, y_at], a, k)[...].astype(jnp.float32)
+            for buffer in extra:
+                value = value + block_step(buffer, a, k)[...].astype(jnp.float32)
+            here[...] = value.astype(jnp.bfloat16)
+            return carry
+
+        lax.fori_loop(first, last, add, 0)
+
+    def diag_copy(a, z_at, part):
+        return remote(
+            block_part(work[a].at[index(z_at, 1 - x), 1 - y], a, part),
+            block_part(step_one[a].at[z_at], a, part),
+            send.at[part, a, z_at],
+            one_got.at[a, part, z_at],
+            y_next if part == 0 else x_next,
+        )
+
+    def diag(z_at):
+        for a in range(count):
+            ready(a, z_at, 1 - x, 1 - y)
+            total(a, z_at, 1 - x, 1 - y, 0, STEPS[a])
+            for part in range(2):
+                diag_copy(a, z_at, part).start()
+
+    def x_copy(a, z_at):
+        return remote(work[a].at[index(z_at, 1 - x), y], from_x[a].at[z_at], send.at[2, a, z_at], x_got.at[a, z_at], x_next)
+
+    def y_copy(a, z_at):
+        return remote(work[a].at[index(z_at, x), 1 - y], from_y[a].at[z_at], send.at[3, a, z_at], y_got.at[a, z_at], y_next)
+
+    def columns(z_at):
+        for a in range(count):
+            middle, last = FIRST[a], STEPS[a]
+            ready(a, z_at, 1 - x, y)
+            diag_copy(a, z_at, 0).wait_recv()
+            total(a, z_at, 1 - x, y, 0, middle, [step_one[a].at[z_at]])
+            total(a, z_at, 1 - x, y, middle, last)
+            x_copy(a, z_at).start()
+            ready(a, z_at, x, 1 - y)
+            diag_copy(a, z_at, 1).wait_recv()
+            total(a, z_at, x, 1 - y, 0, middle)
+            total(a, z_at, x, 1 - y, middle, last, [step_one[a].at[z_at]])
+            y_copy(a, z_at).start()
+
+    def z_copy(a, z_at, side):
+        target = device_at(z + 1, x, y, core) if side == 0 else device_at(z - 1, x, y, core)
+        return remote(work[a].at[index(z_at, x), y], from_z[a].at[side, z_at], send.at[4, a, z_at], z_got.at[a, side, z_at], target)
+
+    def line(step):
+        def act(z_at):
+            for a in range(count):
+                ready(a, z_at, x, y)
+                x_copy(a, z_at).wait_recv()
+                y_copy(a, z_at).wait_recv()
+                across = [from_x[a].at[z_at], from_y[a].at[z_at]]
+                if step > 0:
+                    upward = z_at > z
+                    before = (upward & (z > 0)) | (jnp.logical_not(upward) & (z < depth - 1))
+                    side = jnp.where(upward, 0, 1)
+
+                    @pl.when(before)
+                    def _():
+                        remote(
+                            work[a].at[index(z_at, x), y],
+                            from_z[a].at[side, z_at],
+                            send.at[4, a, z_at],
+                            z_got.at[a, side, z_at],
+                            sibling,
+                        ).wait_recv()
+                        total(a, z_at, x, y, 0, STEPS[a], across + [from_z[a].at[side, z_at]])
+
+                    @pl.when(jnp.logical_not(before))
+                    def _():
+                        total(a, z_at, x, y, 0, STEPS[a], across)
+
+                    @pl.when(upward)
+                    def _():
+                        z_copy(a, z_at, 0).start()
+
+                    @pl.when(jnp.logical_not(upward))
+                    def _():
+                        z_copy(a, z_at, 1).start()
+                else:
+                    for side in range(2):
+                        present = (z > 0) if side == 0 else (z < depth - 1)
+
+                        @pl.when(present)
+                        def _():
+                            z_copy(a, z, side).wait_recv()
+
+                        @pl.when(jnp.logical_not(present))
+                        def _():
+                            from_z[a][side, z] = jnp.zeros(BLOCKS[a], jnp.bfloat16)
+
+                    def finish(k, carry):
+                        i = index(z, x)
+                        value = block_step(work[a].at[i, y], a, k)[...].astype(jnp.float32)
+                        for buffer in [paired[a].at[i, y]] + across + [from_z[a].at[0, z], from_z[a].at[1, z]]:
+                            value = value + block_step(buffer, a, k)[...].astype(jnp.float32)
+                        if a == SQUARE:
+                            low, high = value[:, :192], pltpu.roll(value, 192, 1)[:, :192]
+                            outs[a][core, k] = jnp.where(core == 0, low, high)
+                            spare[k] = jnp.where(core == 0, high, low)
+                        else:
+                            block_step(outs[a], a, k)[...] = value
+                        return carry
+
+                    lax.fori_loop(0, STEPS[a], finish, 0)
+                    if a == SQUARE:
+                        end_copy().start()
+
+        sides(step, act)
+
+    def end_copy():
+        return remote(spare, outs[SQUARE].at[core], end_send, end_got, sibling)
+
+    for k in range(depth + 2):
+        if k < depth:
+            sides(rounds[k], diag)
+        if 0 <= k - 1 < depth:
+            sides(rounds[k - 1], columns)
+        if 0 <= k - 2 < depth:
+            line(rounds[k - 2])
+
+    def finish_all(z_at, carry):
+        for a in range(count):
+            for x_at in range(2):
+                for y_at in range(2):
+                    pair(a, z_at, x_at, y_at).wait_send()
+            for part in range(2):
+                diag_copy(a, z_at, part).wait_send()
+            x_copy(a, z_at).wait_send()
+            y_copy(a, z_at).wait_send()
+
+            @pl.when(z_at != z)
+            def _():
+                z_copy(a, z_at, 0).wait_send()
+        return carry
+
+    lax.fori_loop(0, depth, finish_all, 0)
+    end_copy().wait_send()
+    remote(spare, outs[SQUARE].at[1 - core], end_send, end_got, sibling).wait_recv()
+
+
+def reduce_blocks(square, expand, reduce_turned, call_id):
+    depth = lax.axis_size("dp") // 2
+
+    def buffers(*lead):
+        return [pltpu.VMEM(lead + block, jnp.bfloat16) for block in BLOCKS]
+
+    return pl.pallas_call(
+        functools.partial(reduce_kernel, depth),
+        out_shape=[
+            jax.ShapeDtypeStruct((2, 5, 48, 192), jnp.float32),
+            jax.ShapeDtypeStruct((96, 768), jnp.float32),
+            jax.ShapeDtypeStruct((192, 384), jnp.float32),
+        ],
+        in_specs=[pl.BlockSpec(memory_space=pl.ANY)] * KINDS,
+        out_specs=[pl.BlockSpec(memory_space=pltpu.VMEM)] * KINDS,
+        scratch_shapes=buffers(2 * depth, 2)
+        + buffers(2 * depth, 2)
+        + buffers(depth)
+        + buffers(depth)
+        + buffers(depth)
+        + buffers(2, depth)
+        + [
+            pltpu.VMEM((5, 48, 192), jnp.float32),
+            pltpu.SemaphoreType.DMA((KINDS, 2 * depth, 2)),
+            pltpu.SemaphoreType.DMA((KINDS, 2 * depth, 2)),
+            pltpu.SemaphoreType.DMA((KINDS, 2 * depth, 2)),
+            pltpu.SemaphoreType.DMA((5, KINDS, depth)),
+            pltpu.SemaphoreType.DMA((KINDS, 2, depth)),
+            pltpu.SemaphoreType.DMA((KINDS, depth)),
+            pltpu.SemaphoreType.DMA((KINDS, depth)),
+            pltpu.SemaphoreType.DMA((KINDS, 2, depth)),
+            pltpu.SemaphoreType.DMA,
+            pltpu.SemaphoreType.DMA,
+        ],
+        compiler_params=pltpu.CompilerParams(
+            collective_id=call_id, has_side_effects=True, vmem_limit_bytes=VMEM_CAP
+        ),
+        name="reduce_layer",
+    )(square, expand, reduce_turned)
+
+
+TILE = 128
+PAIRS = HEADS // 2
+GELU_IN = (2.0 / np.pi) ** 0.5
+
+
+def dot_nn(left, right):
+    return jnp.dot(left, right, preferred_element_type=jnp.float32)
+
+
+def dot_nt(left, right):
+    return lax.dot_general(left, right, (((1,), (1,)), ((), ())), preferred_element_type=jnp.float32)
+
+
+def dot_tn(left, right):
+    return lax.dot_general(left, right, (((0,), (0,)), ((), ())), preferred_element_type=jnp.float32)
+
+
+def rows_at(index, size):
+    return pl.ds(pl.multiple_of(index * size, size), size)
+
+
+def split_heads(block):
+    low = lax.broadcasted_iota(jnp.int32, block.shape, 1) < HEAD
+    wide = block.astype(jnp.float32)
+    first = jnp.where(low, wide, 0.0).astype(jnp.bfloat16)
+    second = jnp.where(low, 0.0, wide).astype(jnp.bfloat16)
+    return jnp.concatenate([first, second], axis=0)
+
+
+def join_heads(stacked):
+    return jnp.concatenate([stacked[:TILE], stacked[TILE:]], axis=1)
+
+
+def pair_probs(query, keys_here, bias, mask):
+    scores = dot_nt(split_heads(query), keys_here) * HEAD ** (-0.5) + bias
+    scores = scores + mask
+    raised = jnp.exp(scores - jnp.max(scores, axis=1, keepdims=True))
+    return raised / jnp.sum(raised, axis=1, keepdims=True)
+
+
+def pair_bias(bias_ref, pair):
+    return jnp.concatenate([bias_ref[2 * pair], bias_ref[2 * pair + 1]], axis=0)
+
+
+def tile_mask(mask_ref, tile):
+    mask = mask_ref[tile]
+    return jnp.concatenate([mask, mask], axis=0)
+
+
+def hot_rows(rank_ref, rows, tokens):
+    place = lax.broadcasted_iota(jnp.int32, (rows.size, tokens), 1)
+    return (rank_ref[rows, :1] == place).astype(jnp.float32).astype(jnp.bfloat16)
+
+
+def norm_rows(values, gain):
+    scale = lax.rsqrt(jnp.mean(values * values, axis=1, keepdims=True) + NORM_EPS)
+    return values * scale * gain
+
+
+def gelu_parts(pre):
+    inner = GELU_IN * (pre + 0.044715 * pre * pre * pre)
+    return jnp.tanh(inner)
+
+
+def forward_kernel(
+    found_ref, rank_ref, square_ref, expand_ref, reduce_ref, gains_ref, bias_ref, mask_ref, pool_ref, length_ref,
+    start_ref, query_ref, key_ref, value_ref, mixed_ref, middle_ref, ending_ref, low_ref, pooled_ref, embed_ref,
+    inverse_ref, normed, pooled_sum,
+):
+    tokens = start_ref.shape[0]
+    big = 512
+
+    def begin(r, carry):
+        rows = rows_at(r, 256)
+        start = dot_nt(hot_rows(rank_ref, rows, tokens), found_ref[...])
+        start_ref[rows, :] = start.astype(jnp.bfloat16)
+        normed[rows, :] = norm_rows(start, gains_ref[0:1]).astype(jnp.bfloat16)
+        return carry
+
+    lax.fori_loop(0, tokens // 256, begin, 0)
+    for k, target in enumerate((query_ref, key_ref, value_ref)):
+
+        def project(r, carry):
+            rows = rows_at(r, big)
+            target[rows, :] = dot_nn(normed[rows, :], square_ref[k]).astype(jnp.bfloat16)
+            return carry
+
+        lax.fori_loop(0, tokens // big, project, 0)
+
+    def attend(t, carry):
+        rows = rows_at(t, TILE)
+        mask = tile_mask(mask_ref, t)
+        for pair in range(PAIRS):
+            lanes = pl.ds(pair * TILE, TILE)
+            probs = pair_probs(query_ref[rows, lanes], key_ref[rows, lanes], pair_bias(bias_ref, pair), mask)
+            mixed = dot_nn(join_heads(probs).astype(jnp.bfloat16), split_heads(value_ref[rows, lanes]))
+            mixed_ref[rows, lanes] = mixed.astype(jnp.bfloat16)
+        return carry
+
+    lax.fori_loop(0, tokens // TILE, attend, 0)
+
+    def merge(r, carry):
+        rows = rows_at(r, big)
+        middle = start_ref[rows, :].astype(jnp.float32) + dot_nn(mixed_ref[rows, :], square_ref[3])
+        middle_ref[rows, :] = middle
+        ending_ref[rows, :] = middle
+        normed[rows, :] = norm_rows(middle, gains_ref[1:2]).astype(jnp.bfloat16)
+        return carry
+
+    lax.fori_loop(0, tokens // big, merge, 0)
+    wide = expand_ref.shape[1]
+
+    def feed(c, carry):
+        lanes = rows_at(c, D)
+
+        def rows_of(r, inner):
+            rows = rows_at(r, big)
+            pre = dot_nn(normed[rows, :], expand_ref[:, lanes])
+            act = (0.5 * pre * (1.0 + gelu_parts(pre))).astype(jnp.bfloat16)
+            ending_ref[rows, :] += dot_nt(act, reduce_ref[:, lanes])
+            return inner
+
+        return lax.fori_loop(0, tokens // big, rows_of, carry)
+
+    lax.fori_loop(0, wide // D, feed, 0)
+    pooled_sum[...] = jnp.zeros_like(pooled_sum)
+
+    def pool(r, carry):
+        rows = rows_at(r, 256)
+        output = norm_rows(ending_ref[rows, :], gains_ref[2:3])
+        pooled_sum[...] += jnp.dot(
+            pool_ref[:, rows], output, precision=HIGHEST, preferred_element_type=jnp.float32
+        )
+        return carry
+
+    lax.fori_loop(0, tokens // 256, pool, 0)
+    pooled = (pooled_sum[...] / length_ref[:, :1]).astype(jnp.bfloat16)
+    pooled_ref[...] = pooled
+    projected = dot_nn(pooled, square_ref[4])
+    inverse = lax.rsqrt(jnp.sum(projected * projected, axis=1, keepdims=True) + NORM_EPS)
+    embeds = projected * inverse
+    embed_ref[...] = embeds
+    low_ref[...] = embeds.astype(jnp.bfloat16)
+    inverse_ref[...] = jnp.broadcast_to(inverse, inverse_ref.shape)
+
+
+def run_forward(found, rank, square, expand, reduce_turned, gains, bias, mask, pool, lengths):
+    tokens = found.shape[1]
+    seqs = pool.shape[0]
+    low = jnp.bfloat16
+    flat = jax.ShapeDtypeStruct((tokens, D), low)
+    full = jax.ShapeDtypeStruct((tokens, D), jnp.float32)
+    return pl.pallas_call(
+        forward_kernel,
+        out_shape=[
+            flat, flat, flat, flat, flat, full, full,
+            jax.ShapeDtypeStruct((seqs, D), low),
+            jax.ShapeDtypeStruct((seqs, D), low),
+            jax.ShapeDtypeStruct((seqs, D), jnp.float32),
+            jax.ShapeDtypeStruct((seqs, LANES), jnp.float32),
+        ],
+        scratch_shapes=[pltpu.VMEM((tokens, D), low), pltpu.VMEM((seqs, D), jnp.float32)],
+        compiler_params=pltpu.CompilerParams(vmem_limit_bytes=VMEM_CAP),
+        name="layer_forward",
+    )(found, rank, square, expand, reduce_turned, gains, bias, mask, pool, lengths)
+
+
+def norm_back_rows(values, gain, grad):
+    scale = lax.rsqrt(jnp.mean(values * values, axis=1, keepdims=True) + NORM_EPS)
+    weighted = grad * gain
+    inner = jnp.mean(weighted * values, axis=1, keepdims=True)
+    through = scale * weighted - values * (scale * scale * scale * inner)
+    return through, jnp.sum(grad * values * scale, axis=0, keepdims=True)
+
+
+def feed_back_kernel(
+    grad_embed_ref, embed_ref, inverse_ref, pool_ref, length_ref, last_ref, middle_ref, ending_ref, expand_ref,
+    reduce_ref, gains_ref,
+    grad_expand_ref, grad_reduce_ref, grad_middle_ref, grad_low_ref, grad_proj_ref, grad_gains_ref,
+    normed, normed_turned, end_low, end_turned, back,
+):
+    tokens = middle_ref.shape[0]
+    embeds, grads = embed_ref[...], grad_embed_ref[...]
+    grad_proj = inverse_ref[:, :1] * (grads - embeds * jnp.sum(grads * embeds, axis=1, keepdims=True))
+    grad_proj = grad_proj.astype(jnp.bfloat16)
+    grad_proj_ref[...] = grad_proj
+    grad_pooled = dot_nt(grad_proj, last_ref[0]) / length_ref[:, :1]
+    grad_gains_ref[...] = jnp.zeros_like(grad_gains_ref)
+
+    def begin(r, carry):
+        rows = rows_at(r, 256)
+        grad_out = lax.dot_general(
+            pool_ref[:, rows], grad_pooled, (((0,), (0,)), ((), ())), precision=HIGHEST,
+            preferred_element_type=jnp.float32,
+        )
+        through, gain = norm_back_rows(ending_ref[rows, :], gains_ref[2:3], grad_out)
+        grad_gains_ref[2:3] += gain
+        grad_middle_ref[rows, :] = through
+        end_low[rows, :] = through.astype(jnp.bfloat16)
+        end_turned[:, rows] = through.T.astype(jnp.bfloat16)
+        middle_normed = norm_rows(middle_ref[rows, :], gains_ref[1:2])
+        normed[rows, :] = middle_normed.astype(jnp.bfloat16)
+        normed_turned[:, rows] = middle_normed.T.astype(jnp.bfloat16)
+        return carry
+
+    lax.fori_loop(0, tokens // 256, begin, 0)
+    back[...] = jnp.zeros_like(back)
+    wide = expand_ref.shape[1]
+    step = 384
+
+    def feed(c, carry):
+        lanes = rows_at(c, step)
+        pre = dot_nn(normed[...], expand_ref[:, lanes])
+        grad_act = dot_nn(end_low[...], reduce_ref[:, lanes])
+        turn = gelu_parts(pre)
+        act = (0.5 * pre * (1.0 + turn)).astype(jnp.bfloat16)
+        slope = 0.5 * (1.0 + turn) + 0.5 * pre * (1.0 - turn * turn) * GELU_IN * (1.0 + 3.0 * 0.044715 * pre * pre)
+        grad_pre = (grad_act * slope).astype(jnp.bfloat16)
+        grad_reduce_ref[:, lanes] = dot_nn(end_turned[...], act).astype(jnp.bfloat16)
+        grad_expand_ref[:, lanes] = dot_nn(normed_turned[...], grad_pre).astype(jnp.bfloat16)
+        back[...] += dot_nt(grad_pre, expand_ref[:, lanes])
+        return carry
+
+    lax.fori_loop(0, wide // step, feed, 0)
+
+    def end(r, carry):
+        rows = rows_at(r, 256)
+        through, gain = norm_back_rows(middle_ref[rows, :], gains_ref[1:2], back[rows, :])
+        grad_gains_ref[1:2] += gain
+        grad_middle = grad_middle_ref[rows, :] + through
+        grad_middle_ref[rows, :] = grad_middle
+        grad_low_ref[rows, :] = grad_middle.astype(jnp.bfloat16)
+        return carry
+
+    lax.fori_loop(0, tokens // 256, end, 0)
+
+
+def run_feed_back(grad_embed, embeds, inverse, pool, lengths, square, middle, ending, expand, reduce_turned, gains):
+    tokens = middle.shape[0]
+    seqs = pool.shape[0]
+    low = jnp.bfloat16
+    whole = pl.BlockSpec(memory_space=pltpu.VMEM)
+    return pl.pallas_call(
+        feed_back_kernel,
+        grid=(1,),
+        out_shape=[
+            jax.ShapeDtypeStruct(expand.shape, low),
+            jax.ShapeDtypeStruct(reduce_turned.shape, low),
+            jax.ShapeDtypeStruct((tokens, D), jnp.float32),
+            jax.ShapeDtypeStruct((tokens, D), low),
+            jax.ShapeDtypeStruct((seqs, D), low),
+            jax.ShapeDtypeStruct((8, D), jnp.float32),
+        ],
+        in_specs=[whole] * 5
+        + [pl.BlockSpec((1, D, D), lambda i: (4, 0, 0))]
+        + [whole] * 5,
+        out_specs=[whole] * 6,
+        scratch_shapes=[
+            pltpu.VMEM((tokens, D), low),
+            pltpu.VMEM((D, tokens), low),
+            pltpu.VMEM((tokens, D), low),
+            pltpu.VMEM((D, tokens), low),
+            pltpu.VMEM((tokens, D), jnp.float32),
+        ],
+        compiler_params=pltpu.CompilerParams(vmem_limit_bytes=VMEM_CAP),
+        name="feed_backward",
+    )(grad_embed, embeds, inverse, pool, lengths, square, middle, ending, expand, reduce_turned, gains)
+
+
+def attend_back_kernel(
+    grad_middle_ref, grad_low_ref, grad_proj_ref, pooled_ref, start_ref, query_ref, key_ref, value_ref, mixed_ref,
+    square_ref, gains_ref, bias_ref, mask_ref, rank_ref,
+    grad_square_ref, grad_score_ref, grad_gain_ref, send_ref,
+    grad_mixed, turned, grad_query, grad_key, grad_value, start_low,
+):
+    tokens = start_ref.shape[0]
+    big = 512
+    grad_square_ref[4] = dot_tn(pooled_ref[...], grad_proj_ref[...]).astype(jnp.bfloat16)
+
+    def begin(r, carry):
+        rows = rows_at(r, big)
+        grad_mixed[rows, :] = dot_nt(grad_low_ref[rows, :], square_ref[3]).astype(jnp.bfloat16)
+        turned[:, rows] = mixed_ref[rows, :].astype(jnp.float32).T.astype(jnp.bfloat16)
+        return carry
+
+    lax.fori_loop(0, tokens // big, begin, 0)
+
+    def outer(target, right_ref):
+        def part(r, carry):
+            rows = rows_at(r, 384)
+            grad_square_ref[target, rows, :] = dot_nn(turned[rows, :], right_ref[...]).astype(jnp.bfloat16)
+            return carry
+
+        lax.fori_loop(0, D // 384, part, 0)
+
+    outer(3, grad_low_ref)
+    grad_score_ref[...] = jnp.zeros_like(grad_score_ref)
+
+    def attend(t, carry):
+        rows = rows_at(t, TILE)
+        mask = tile_mask(mask_ref, t)
+        for pair in range(PAIRS):
+            lanes = pl.ds(pair * TILE, TILE)
+            query, keys_here = query_ref[rows, lanes], key_ref[rows, lanes]
+            probs = pair_probs(query, keys_here, pair_bias(bias_ref, pair), mask)
+            grads = split_heads(grad_mixed[rows, lanes])
+            grad_probs = dot_nt(grads, value_ref[rows, lanes])
+            grad_value[rows, lanes] = dot_tn(probs.astype(jnp.bfloat16), grads).astype(jnp.bfloat16)
+            inner = jnp.sum(grad_probs * probs, axis=1, keepdims=True)
+            grad_scores = (probs * (grad_probs - inner)).astype(jnp.bfloat16)
+            kept = grad_scores.astype(jnp.float32)
+            grad_score_ref[2 * pair] += kept[:TILE]
+            grad_score_ref[2 * pair + 1] += kept[TILE:]
+            grad_query[rows, lanes] = (
+                dot_nn(join_heads(grad_scores), split_heads(keys_here)) * HEAD ** (-0.5)
+            ).astype(jnp.bfloat16)
+            grad_key[rows, lanes] = (dot_tn(grad_scores, split_heads(query)) * HEAD ** (-0.5)).astype(jnp.bfloat16)
+        return carry
+
+    lax.fori_loop(0, tokens // TILE, attend, 0)
+
+    def renorm(r, carry):
+        rows = rows_at(r, 256)
+        normed = norm_rows(start_ref[rows, :].astype(jnp.float32), gains_ref[0:1])
+        turned[:, rows] = normed.T.astype(jnp.bfloat16)
+        return carry
+
+    lax.fori_loop(0, tokens // 256, renorm, 0)
+    outer(0, grad_query)
+    outer(1, grad_key)
+    outer(2, grad_value)
+    grad_gain_ref[...] = jnp.zeros_like(grad_gain_ref)
+
+    def end(r, carry):
+        rows = rows_at(r, 256)
+        grad_normed = (
+            dot_nt(grad_query[rows, :], square_ref[0])
+            + dot_nt(grad_key[rows, :], square_ref[1])
+            + dot_nt(grad_value[rows, :], square_ref[2])
+        )
+        through, gain = norm_back_rows(start_ref[rows, :].astype(jnp.float32), gains_ref[0:1], grad_normed)
+        grad_gain_ref[0:1] += gain
+        turned[:, rows] = (grad_middle_ref[rows, :] + through).T.astype(jnp.bfloat16)
+        return carry
+
+    lax.fori_loop(0, tokens // 256, end, 0)
+
+    def hot(r, carry):
+        rows = rows_at(r, 256)
+        start_low[rows, :] = hot_rows(rank_ref, rows, tokens)
+        return carry
+
+    lax.fori_loop(0, tokens // 256, hot, 0)
+
+    def gather_rows(r, carry):
+        rows = rows_at(r, 384)
+        send_ref[rows, :] = dot_nn(turned[rows, :], start_low[...]).astype(jnp.bfloat16)
+        return carry
+
+    lax.fori_loop(0, D // 384, gather_rows, 0)
+
+
+def run_attend_back(
+    grad_middle, grad_low, grad_proj, pooled, start, queries, keys_here, values_here, mixed, square, gains, bias,
+    mask, rank,
+):
+    tokens = start.shape[0]
+    low = jnp.bfloat16
+    return pl.pallas_call(
+        attend_back_kernel,
+        out_shape=[
+            jax.ShapeDtypeStruct((5, D, D), low),
+            jax.ShapeDtypeStruct((HEADS, TILE, TILE), jnp.float32),
+            jax.ShapeDtypeStruct((8, D), jnp.float32),
+            jax.ShapeDtypeStruct((D, tokens), low),
+        ],
+        scratch_shapes=[
+            pltpu.VMEM((tokens, D), low),
+            pltpu.VMEM((D, tokens), low),
+            pltpu.VMEM((tokens, D), low),
+            pltpu.VMEM((tokens, D), low),
+            pltpu.VMEM((tokens, D), low),
+            pltpu.VMEM((tokens, tokens), low),
+        ],
+        compiler_params=pltpu.CompilerParams(vmem_limit_bytes=VMEM_CAP),
+        name="attend_backward",
+    )(
+        grad_middle, grad_low, grad_proj, pooled, start, queries, keys_here, values_here, mixed, square, gains, bias,
+        mask, rank,
+    )
 
 
 def shards(
@@ -525,7 +1239,10 @@
     hard_negative,
 ):
     both = ("dp", "fsdp")
-    count = lax.axis_size("dp") * lax.axis_size("fsdp")
+    dp_size, fsdp_size = lax.axis_size("dp"), lax.axis_size("fsdp")
+    count = dp_size * fsdp_size
+    direct = dp_size == 8 and fsdp_size == 4
+    position = lax.axis_index(both)
     feats, vocab_size = embed_table.shape
     feats_pad = up8(feats)
     fold = fold_rows(vocab_size)
@@ -534,38 +1251,51 @@
     short_length = query_tokens.shape[1]
     long_length = answer_tokens.shape[1]
     short_tokens = jnp.concatenate([query_tokens, premise_tokens, hypothesis_tokens], axis=0)
-    short_lengths = jnp.concatenate(
-        [query_length, jnp.full((2 * nli_rows,), short_length, jnp.int32)]
+    lengths = jnp.concatenate(
+        [query_length, jnp.full((2 * nli_rows,), short_length, jnp.int32), answer_length]
     )
     all_tokens = jnp.concatenate([short_tokens.reshape(-1), answer_tokens.reshape(-1)])
     token_count = all_tokens.shape[0]
-    packed, hit = token_keys(all_tokens, fold)
-    packed_all = exchange(packed.reshape(1, -1, LANES), True, 0, "share_keys")
-    packed_all = packed_all.reshape(count, 1, token_count)
+    hypo_start = query_rows + nli_rows
+    answer_start = query_rows + 2 * nli_rows
+    seq_count = answer_start + query_rows
+    seq_pad = -(-seq_count // 16) * 16
+    split_at = short_tokens.shape[0] * short_length
+
+    packed, rank = token_keys(all_tokens, fold)
+    start_info = jnp.concatenate(
+        [
+            packed.reshape(-1, LANES).astype(jnp.float32),
+            jnp.pad(hard_negative, (0, LANES - nli_rows)).reshape(1, LANES).astype(jnp.float32),
+            jnp.pad(norm_gains, ((0, 7 - 3), (0, LANES - feats))),
+        ],
+        axis=0,
+    )
+    key_rows = token_count // LANES
+    info_all = exchange(start_info[None], True, 0, "share_start")
+    packed_all = info_all[:, :key_rows].astype(jnp.int32).reshape(count, 1, token_count)
+    negative_all = info_all[:, key_rows, :nli_rows].astype(jnp.int32).reshape(-1)
+    gains = info_all[:, key_rows + 1 : key_rows + 4, :feats].transpose(1, 0, 2).reshape(3, D)
+    gains = jnp.pad(gains.astype(jnp.bfloat16).astype(jnp.float32), ((0, 5), (0, 0)))
     row_all, group_all = packed_all >> 2, packed_all & 3
 
-    def gather_layer():
-        def whole(weight, row_axis):
-            low = weight.astype(jnp.bfloat16)
-            parts = lax.all_gather(low, both, axis=0, tiled=False)
-            dp, fsdp = lax.axis_size("dp"), lax.axis_size("fsdp")
-            parts = parts.reshape((dp, fsdp) + low.shape)
-            lead = tuple(range(2, 2 + row_axis))
-            order = lead + (0, 2 + row_axis, 1, 3 + row_axis)
-            shape = low.shape[:row_axis] + (dp * low.shape[row_axis], fsdp * low.shape[row_axis + 1])
-            return parts.transpose(order).reshape(shape)
-
-        gains = exchange(jnp.pad(norm_gains, ((0, 5), (0, LANES - feats)))[None], True, 1, "share_gains")
-        gains = gains[:, :3, :feats].transpose(1, 0, 2).reshape(3, D)
-        return (
-            whole(square_weights, 1),
-            whole(expand_weight, 0),
-            whole(reduce_weight, 0),
-            gains.astype(jnp.bfloat16).astype(jnp.float32),
-            position_bias,
-        )
-
-    layer = gather_layer()
+    square_low = square_weights.astype(jnp.bfloat16)
+    expand_low = expand_weight.astype(jnp.bfloat16)
+    reduce_low = reduce_weight.astype(jnp.bfloat16).T
+    if direct:
+        square_pieces = square_low.reshape(5, 2, 48, 192).transpose(1, 0, 2, 3)
+        square_all, expand_all, reduce_all = gather_blocks(square_pieces, expand_low, reduce_low, 1)
+    else:
+
+        def whole(piece, row_name, column_name):
+            axis = piece.ndim - 2
+            wide = lax.all_gather(piece, column_name, axis=axis + 1, tiled=True)
+            return lax.all_gather(wide, row_name, axis=axis, tiled=True)
+
+        square_all = whole(square_low, "dp", "fsdp")
+        expand_all = whole(expand_low, "dp", "fsdp")
+        reduce_all = whole(reduce_low, "fsdp", "dp")
+
     table_low = embed_table.astype(jnp.bfloat16).astype(jnp.float32)
     if feats_pad > feats:
         table_low = jnp.pad(table_low, ((0, feats_pad - feats), (0, 0)))
@@ -573,40 +1303,39 @@
     half = token_count // 2
     found = found.reshape(count, 2, feats_pad, half)[:, :, :feats]
     found = found.transpose(0, 2, 1, 3).reshape(D, token_count)
-    embedded = product_right(hit, found)
-    split_at = short_tokens.shape[0] * short_length
-    short_mask = jnp.arange(short_length)[None, :] < short_lengths[:, None]
-    long_mask = jnp.arange(long_length)[None, :] < answer_length[:, None]
-    short_out, short_stored = layer_forward(embedded[:split_at], short_mask, layer, short_length)
-    long_out, long_stored = layer_forward(embedded[split_at:], long_mask, layer, long_length)
-    pooled = jnp.concatenate(
+
+    sequence = np.concatenate(
         [
-            pool_rows(short_out, short_mask, short_lengths, short_length),
-            pool_rows(long_out, long_mask, answer_length, long_length),
-        ],
-        axis=0,
-    )
-    pooled_low = pooled.astype(jnp.bfloat16)
-    projected = product(pooled_low, layer[0][4])
-    inverse = lax.rsqrt(jnp.sum(projected * projected, axis=-1, keepdims=True) + NORM_EPS)
-    embeds = projected * inverse
-    embeds_low = embeds.astype(jnp.bfloat16)
-    hypo_start = query_rows + nli_rows
-    answer_start = query_rows + 2 * nli_rows
-    seq_count = answer_start + query_rows
-    seq_pad = -(-seq_count // 16) * 16
-    gathered = exchange(
-        jnp.pad(embeds_low, ((0, seq_pad - seq_count), (0, 0)))[None], True, 3, "share_embeds"
-    )
-    negative_all = exchange(
-        jnp.pad(hard_negative, (0, 8 * LANES - nli_rows)).reshape(1, 8, LANES), True, 4, "share_negatives"
-    ).reshape(count, -1)[:, :nli_rows].reshape(-1)
+            np.repeat(np.arange(answer_start), short_length),
+            answer_start + np.repeat(np.arange(query_rows), long_length),
+        ]
+    )
+    inside = np.concatenate(
+        [
+            np.tile(np.arange(short_length), answer_start),
+            np.tile(np.arange(long_length), query_rows),
+        ]
+    )
+    lengths_pad = jnp.pad(lengths, (0, seq_pad - seq_count), constant_values=1)
+    pool = (sequence[None, :] == np.arange(seq_pad)[:, None]) & (inside[None, :] < lengths_pad[:, None])
+    token_ok = jnp.any(pool, axis=0).reshape(-1, 1, TILE)
+    sequence_tiles = sequence.reshape(-1, TILE)
+    together = sequence_tiles[:, :, None] == sequence_tiles[:, None, :]
+    mask = jnp.where(together & token_ok, 0.0, -1e30).astype(jnp.float32)
+    pool = pool.astype(jnp.float32)
+    length_rows = jnp.broadcast_to(lengths_pad.astype(jnp.float32)[:, None], (seq_pad, LANES))
+    rank_rows = jnp.broadcast_to(rank[:, None], (token_count, LANES))
+    bias, onehot = attention_bias(position_bias, TILE)
+
+    (start, queries, keys_here, values_here, mixed, middle, ending, embeds_low, pooled, embeds, inverse) = run_forward(
+        found, rank_rows, square_all, expand_all, reduce_all, gains, bias, mask, pool, length_rows
+    )
+    gathered = exchange(embeds_low[None], True, 3, "share_embeds")
     queries_all = gathered[:, :query_rows].reshape(-1, D)
     premises_all = gathered[:, query_rows:hypo_start].reshape(-1, D)
     hypotheses_all = gathered[:, hypo_start:answer_start].reshape(-1, D)
     answers_all = gathered[:, answer_start:seq_count].reshape(-1, D)
     scale = jnp.exp(log_scale[0])
-    position = lax.axis_index(both)
 
     def contrast(left, right, extra, own):
         sims = product_right(left, right)
@@ -634,55 +1363,52 @@
         premises_all, hypotheses_all, negatives, nli_rows
     )
     grad_embeds = jnp.concatenate(
-        [grad_queries, grad_premises, grad_hypotheses, grad_answers], axis=0
-    )
-    grad_projected = (
-        inverse * (grad_embeds - embeds * jnp.sum(grad_embeds * embeds, axis=-1, keepdims=True))
-    ).astype(jnp.bfloat16)
-    grad_proj_weight = product_left(pooled_low, grad_projected)
-    grad_pooled = product_right(grad_projected, layer[0][4])
-    short_rows = short_tokens.shape[0]
-    grad_short_start, short_grads = layer_backward(
-        spread_rows(grad_pooled[:short_rows], short_mask, short_lengths),
-        short_mask,
-        layer,
-        short_stored,
-        short_length,
-    )
-    grad_long_start, long_grads = layer_backward(
-        spread_rows(grad_pooled[short_rows:], long_mask, answer_length),
-        long_mask,
-        layer,
-        long_stored,
-        long_length,
-    )
-    grad_squares = jnp.concatenate([short_grads[0] + long_grads[0], grad_proj_weight[None]], axis=0)
-    grad_expand = short_grads[1] + long_grads[1]
-    grad_reduce = short_grads[2] + long_grads[2]
-    grad_gains = short_grads[3] + long_grads[3]
-    grad_position = short_grads[4] + long_grads[4]
+        [
+            grad_queries,
+            grad_premises,
+            grad_hypotheses,
+            grad_answers,
+            jnp.zeros((seq_pad - seq_count, D), jnp.float32),
+        ],
+        axis=0,
+    )
+    (grad_expand, grad_reduce, grad_middle, grad_middle_low, grad_proj, late_gains) = run_feed_back(
+        grad_embeds, embeds, inverse, pool, length_rows, square_all, middle, ending, expand_all, reduce_all, gains
+    )
+    (grad_square, grad_scores, first_gain, merged) = run_attend_back(
+        grad_middle, grad_middle_low, grad_proj, pooled, start, queries, keys_here, values_here, mixed, square_all,
+        gains, bias, mask, rank_rows
+    )
+    grad_gains = jnp.concatenate([first_gain[:1], late_gains[1:3]], axis=0)
+    grad_position = lax.dot_general(
+        onehot, grad_scores.reshape(HEADS, TILE * TILE), (((0,), (1,)), ((), ())), precision=HIGHEST
+    )
     grad_scale = ((first_dscale + second_dscale) * scale).reshape(1)
-    grad_tokens = jnp.concatenate([grad_short_start, grad_long_start], axis=0)
-    merged = product_left(grad_tokens.astype(jnp.bfloat16), hit).astype(jnp.bfloat16)
     merged = merged.reshape(count, feats, 2, half).transpose(0, 2, 1, 3)
     if feats_pad > feats:
         merged = jnp.pad(merged, ((0, 0), (0, 0), (0, feats_pad - feats), (0, 0)))
-    returned = exchange(merged.reshape(count, 2 * feats_pad, half), False, 5, "send_gradients")
+    returned = exchange(merged.reshape(count, 2 * feats_pad, half), False, 4, "send_gradients")
     grad_table = scatter(returned, row_all, group_all, vocab_size)[:feats]
-    squares_part = lax.psum_scatter(grad_squares, "dp", scatter_dimension=1, tiled=True)
-    reduced = (
-        lax.psum_scatter(squares_part, "fsdp", scatter_dimension=2, tiled=True),
-        lax.psum_scatter(
-            lax.psum_scatter(grad_expand, "dp", scatter_dimension=0, tiled=True),
-            "fsdp", scatter_dimension=1, tiled=True),
-        lax.psum_scatter(
-            lax.psum_scatter(grad_reduce, "dp", scatter_dimension=0, tiled=True),
-            "fsdp", scatter_dimension=1, tiled=True),
-    )
+    if direct:
+        square_sum, expand_sum, reduce_sum = reduce_blocks(grad_square, grad_expand, grad_reduce, 5)
+        square_sum = square_sum.transpose(1, 0, 2, 3).reshape(5, 96, 192)
+    else:
+
+        def shard(gradient, row_name, column_name):
+            axis = gradient.ndim - 2
+            part = lax.psum_scatter(
+                gradient.astype(jnp.float32), row_name, scatter_dimension=axis, tiled=True
+            )
+            return lax.psum_scatter(part, column_name, scatter_dimension=axis + 1, tiled=True)
+
+        square_sum = shard(grad_square, "dp", "fsdp")
+        expand_sum = shard(grad_expand, "dp", "fsdp")
+        reduce_sum = shard(grad_reduce, "fsdp", "dp")
+    reduced = (square_sum, expand_sum, reduce_sum.T)
     local_square = (
         jnp.sum(reduced[0] * reduced[0])
         + jnp.sum(reduced[1] * reduced[1])
-        + jnp.sum(reduced[2] * reduced[2])
+        + jnp.sum(reduce_sum * reduce_sum)
         + jnp.sum(grad_table * grad_table)
     )
     small = jnp.concatenate([grad_gains.reshape(-1), grad_position.reshape(-1), local_square.reshape(1)])

time: 1160 us -> 658 us (0.57)
  waiting for transfers between devices: 442 us -> 0 us
  Pallas kernels: 272 us -> 549 us
  local copies, waits for them, and re-layouts: 185 us -> 26.4 us
  matrix products: 154 us -> 6.72 us
  other arithmetic: 71.6 us -> 49.4 us
  between operations: 29.3 us -> 13.9 us
    reduce_scatter x4 -> x0, waiting for transfers between devices: 390 us -> none  [the longest x1 189 us: shards(): lax.psum_scatter(grad_squares, 'dp', scatter_dimension=1, tiled=True)]
    pallas_call x0 -> x5, Pallas kernels: none -> 295 us  [the longest x1 77.4 us: gather_blocks(): pl.pallas_call(functools.partial(gather_kernel, depth), out_shape=[jax.Sh...]
    reshape x24 -> x2, local copies, waits for them, and re-layouts: 70.5 us -> 0.72 us  [the longest x1 0.71 us: shards(): square_pieces = square_low.reshape(5, 2, 48, 192).transpose(1, 0, 2, 3)]
    all_gather x3 -> x0, waiting for transfers between devices: 52 us -> none  [whole(): parts = lax.all_gather(low, both, axis=0, tiled=False)]
    dot_general x16 -> x2, matrix products: 53 us -> 1.53 us  [product_right(): lax.dot_general(left, right, (((1,), (1,)), ((), ())), preferred_element_...]
    dot_general x15 -> x2, matrix products: 40.4 us -> 1.27 us  [product(): return jnp.dot(left, right, preferred_element_type=jnp.float32)]
    unnamed x375 -> x54, local copies, waits for them, and re-layouts: 42.9 us -> 3.75 us
    dot_general x16 -> x2, matrix products: 32.7 us -> 0.96 us  [product_left(): lax.dot_general(left, right, (((0,), (0,)), ((), ())), preferred_element_...]
  transfers between devices with their start and end apart: 9 -> 0, of which waited for: 4 -> 0; matrix products, arithmetic and copies ran while one was open for 19% -> 0% of each run, Pallas kernels for 20% -> 0%
where the time goes in v2:
time: 658 us; the launch traced here: 646 us
  Pallas kernels  549 us (83%)
  other arithmetic  49.4 us (8%)
  local copies, waits for them, and re-layouts  26.4 us (4%)
  between operations  13.9 us (2%)
  matrix products  6.72 us (1%)
    pallas_call x5, Pallas kernels, exchange(): pl.pallas_call(functools.partial(exchange_kernel, same), out_shape=jax.Sh...  137 us
    pallas_call x1, Pallas kernels, gather_blocks(): pl.pallas_call(functools.partial(gather_kernel, depth), out_shape=[jax.Sh...  77.4 us
    pallas_call x1, Pallas kernels, reduce_blocks(): pl.pallas_call(functools.partial(reduce_kernel, depth), out_shape=[jax.Sh...  71.8 us
    pallas_call x1, Pallas kernels, scatter(): pl.pallas_call(functools.partial(scatter_kernel, fold), grid=(n,), out_sh...  68.4 us
    pallas_call x1, Pallas kernels, run_feed_back(): pl.pallas_call(feed_back_kernel, grid=(1,), out_shape=[jax.ShapeDtypeStru...  52.7 us
    pallas_call x1, Pallas kernels, run_attend_back(): pl.pallas_call(attend_back_kernel, out_shape=[jax.ShapeDtypeStruct((5, D,...  49 us
    pallas_call x1, Pallas kernels, lookup(): pl.pallas_call(functools.partial(lookup_kernel, fold), grid=(n,), out_sha...  48 us
    pallas_call x1, Pallas kernels, run_forward(): pl.pallas_call(forward_kernel, out_shape=[flat, flat, flat, flat, flat, f...  44.5 us

profile of v2, /device:TPU:15, one launch (start us, length us, event | category | flops | bytes accessed | tf_op | source)
XLA Modules:
  0.0 645.7 jit_solution(16550847648215193604)
XLA Ops:
  6.4 13.1 %share_start.1 = f32[32,16,128]{2,1,0:T(8,128)} custom-call(f32[1,16,128]{2,1,0:T(8,128)} %fusion.20.src), custom_call_target="tpu_custom_call" | custom-call | tf_op jit(solution)/shard_map/share_start/pallas_call | solution.py:275
  19.5 1.6 convert_and_fusion
  21.1 3.7 convert_convert_fusion.table_ref
  24.9 48.0 %lookup.1.src = bf16[32,48,512]{2,1,0:T(8,128)(2,1)} custom-call(s32[32,1,1024]{2,1,0:T(1,128)} %bitcast.85, s32[32,1,1024]{2,1,0:T(1,128)} %bitcast.83, f32[24,32128]{1,0:T(8,128)} %convert_convert_fusion.table_ref), custom_call_target="tpu_custom_call" | custom-call | tf_op jit(solution)/shard_map/lookup/pallas_call | solution.py:139
  72.9 42.5 %send_features.1 = bf16[32,48,512]{2,1,0:T(8,128)(2,1)} custom-call(bf16[32,48,512]{2,1,0:T(8,128)(2,1)} %lookup.1.src), custom_call_target="tpu_custom_call" | custom-call | tf_op jit(solution)/shard_map/send_features/pallas_call | solution.py:275
  115.4 3.0 copy.84
  118.6 1.6 copy.94
  124.9 77.4 %gather_layer.1 = (bf16[5,768,768]{2,1,0:T(8,128)(2,1)}, bf16[768,3072]{1,0:T(8,128)(2,1)}, bf16[768,3072]{1,0:T(8,128)(2,1)}) custom-call(bf16[2,5,48,192]{3,2,1,0:T(8,128)(2,1)} %bitcast.87, bf16[96,768]{1,0:T(8,128)(2,1)} %convert_element_type.89.refs_1_, bf16[192,384]{1,0:T(8,128)(2,1)} %convert_bitcast_fusion.refs_2_), custom_call_target="tpu_custom_call" | custom-call | tf_op jit(solution)/shard_map/gather_layer/pallas_call | solution.py:541
  207.0 44.5 %layer_forward.1 = (bf16[1024,768]{1,0:T(8,128)(2,1)}, bf16[1024,768]{1,0:T(8,128)(2,1)}, bf16[1024,768]{1,0:T(8,128)(2,1)}, bf16[1024,768]{1,0:T(8,128)(2,1)}, ...) custom-call(bf16[768,1024]{1,0:T(8,128)(2,1)} %bitcast.75, ...), custom_call_target="tpu_custom_call" | custom-call | tf_op jit(solution)/shard_map/layer_forward/pallas_call | solution.py:971
  251.5 24.7 %share_embeds.1 = bf16[32,16,768]{2,1,0:T(8,128)(2,1)} custom-call(bf16[1,16,768]{2,1,0:T(8,128)(2,1)} %bitcast.90), custom_call_target="tpu_custom_call" | custom-call | tf_op jit(solution)/shard_map/share_embeds/pallas_call | solution.py:275
  279.1 2.0 fusion.38
  282.1 1.3 multiply_reduce_fusion.7
  287.1 1.9 pad_maximum_fusion.1
  288.9 1.4 multiply_reduce_fusion.6
  290.3 1.9 multiply_reduce_fusion.4
  297.1 52.7 %feed_backward.1 = (bf16[768,3072]{1,0:T(8,128)(2,1)}, bf16[768,3072]{1,0:T(8,128)(2,1)}, f32[1024,768]{1,0:T(8,128)}, bf16[1024,768]{1,0:T(8,128)(2,1)}, bf16[16,768]{1,0:T(8,128)(2,1)}, /*index=5*/f32[8,768]{1,0:T(8,128)}) custom-call(f32[16,768]{1,0:T(8,128)} %concatenate.58.grad_embed_ref, f32[16,768]{1,0:T(8,128)} %get-tuple-element.54.embed_ref, ...), custom_call_target="tpu_custom_call" | custom-call | tf_op jit(solution)/shard_map/feed_backward/pallas_call | solution.py:1061
  349.8 49.0 %attend_backward.1 = (bf16[5,768,768]{2,1,0:T(8,128)(2,1)}, f32[12,128,128]{2,1,0:T(8,128)}, f32[8,768]{1,0:T(8,128)}, bf16[768,1024]{1,0:T(8,128)(2,1)}) custom-call(f32[1024,768]{1,0:T(8,128)} %get-tuple-element.58.grad_middle_ref, bf16[1024,768]{1,0:T(8,128)(2,1)} %get-tuple-element.59.grad_low_ref, bf16[16,768]{1,0:T(8,128)(2,1)} %get-tuple-element.60.grad_proj_ref, ...), custom_call_target="tpu_custom_call" | custom-call | tf_op jit(solution)/shard_map/attend_backward/pallas_call | solution.py:1187
  400.3 71.8 %reduce_layer.1 = (f32[2,5,48,192]{3,2,1,0:T(8,128)}, f32[96,768]{1,0:T(8,128)}, f32[192,384]{1,0:T(8,128)}) custom-call(bf16[5,768,768]{2,1,0:T(8,128)(2,1)} %get-tuple-element.71.refs_0_, bf16[768,3072]{1,0:T(8,128)(2,1)} %get-tuple-element.72.refs_1_, bf16[768,3072]{1,0:T(8,128)(2,1)} %get-tuple-element.73.refs_2_), custom_call_target="tpu_custom_call" | custom-call | tf_op jit(solution)/shard_map/reduce_layer/pallas_call | solution.py:784
  472.1 1.8 multiply_reduce_fusion.1
  473.8 1.6 multiply_reduce_fusion.3
  476.8 1.6 multiply_reduce_fusion.2
  479.1 3.8 reshape.322
  482.9 2.9 copy.87
  485.8 42.8 %send_gradients.1.grad_ref = bf16[32,48,512]{2,1,0:T(8,128)(2,1)} custom-call(bf16[32,48,512]{2,1,0:T(8,128)(2,1)} %bitcast.78), custom_call_target="tpu_custom_call" | custom-call | tf_op jit(solution)/shard_map/send_gradients/pallas_call | solution.py:275
  528.6 68.4 %scatter.1 = f32[24,32128]{1,0:T(8,128)} custom-call(s32[32,1,1024]{2,1,0:T(1,128)} %bitcast.86, s32[32,1,1024]{2,1,0:T(1,128)} %bitcast.84, bf16[32,48,512]{2,1,0:T(8,128)(2,1)} %send_gradients.1.grad_ref), custom_call_target="tpu_custom_call" | custom-call | tf_op jit(solution)/shard_map/scatter/pallas_call | solution.py:201
  597.0 3.3 multiply_reduce_fusion
  602.8 1.8 fusion.42
  605.4 14.3 %share_small.1 = f32[32,24,128]{2,1,0:T(8,128)} custom-call(f32[1,24,128]{2,1,0:T(8,128)} %fusion.18.src), custom_call_target="tpu_custom_call" | custom-call | tf_op jit(solution)/shard_map/share_small/pallas_call | solution.py:275
  627.5 2.3 multiply_subtract_fusion.2
  629.8 2.3 multiply_subtract_fusion.3
  632.2 2.5 multiply_subtract_fusion.1
  634.7 6.3 multiply_subtract_fusion
  (116 shorter events, 34.0 us)
Async XLA Ops:
  115.4 7.4 %copy-start.5 = (f32[5,96,192]{2,1,0:T(8,128)S(1)}, f32[5,96,192]{2,1,0:T(8,128)}, u32[]{:S(2)}) copy-start(f32[5,96,192]{2,1,0:T(8,128)} %param.33) | copy-start | bytes 1105924
  118.4 5.1 copy-start.6
  118.5 5.7 copy-start.7
  118.5 83.8 %copy-start.23 = (s32[4]{0:T(128)S(1)}, s32[4]{0:T(128)}, u32[]{:S(2)}) copy-start(s32[4]{0:T(128)} %param.56) | copy-start | bytes 52
  118.5 83.8 %copy-start.24 = (s32[4]{0:T(128)S(1)}, s32[4]{0:T(128)}, u32[]{:S(2)}) copy-start(s32[4]{0:T(128)} %param.55) | copy-start | bytes 52
  118.5 83.9 %copy-start.14 = (pred[16,1024]{1,0:T(8,128)(4,1)S(1)}, pred[16,1024]{1,0:T(8,128)(4,1)}, u32[]{:S(2)}) copy-start(pred[16,1024]{1,0:T(8,128)(4,1)} %constant.89.clone) | copy-start | bytes 49156
  118.5 83.9 %copy-start.20 = (s32[1024]{0:T(1024)S(1)}, s32[1024]{0:T(1024)}, u32[]{:S(2)}) copy-start(s32[1024]{0:T(1024)} %constant.203) | copy-start | bytes 12292
  118.5 84.6 %copy-start.11 = (pred[8,128,128]{2,1,0:T(32,128)(4,1)S(1)}, pred[8,128,128]{2,1,0:T(32,128)(4,1)}, u32[]{:S(2)}) copy-start(pred[8,128,128]{2,1,0:T(32,128)(4,1)} %constant.90.clone) | copy-start | bytes 393220
  118.5 86.1 %copy-start.2 = (f32[16384,32]{0,1:T(8,128)S(1)}, f32[16384,32]{0,1:T(8,128)}, u32[]{:S(2)}) copy-start(f32[16384,32]{0,1:T(8,128)} %constant.91.clone) | copy-start | bytes 6291460
  118.5 86.1 %copy-start.12 = (f32[32,12]{0,1:T(8,128)S(1)}, f32[32,12]{0,1:T(8,128)}, u32[]{:S(2)}) copy-start(f32[32,12]{0,1:T(8,128)} %param.37) | copy-start | bytes 4612
  278.5 2.7 copy-start.15
  278.5 2.6 copy-start.19
  602.1 24.0 %copy-start.13 = (f32[32,12]{0,1:T(8,128)S(1)}, f32[32,12]{0,1:T(8,128)}, u32[]{:S(2)}) copy-start(f32[32,12]{0,1:T(8,128)} %param.37) | copy-start | bytes 4612
  602.1 24.0 %copy-start.16 = (f32[32,12]{0,1:T(8,128)S(1)}, f32[32,12]{0,1:T(8,128)}, u32[]{:S(2)}) copy-start(f32[32,12]{0,1:T(8,128)} %param.50) | copy-start | bytes 4612
  602.2 24.0 %copy-start.17 = (f32[32,12]{0,1:T(8,128)S(1)}, f32[32,12]{0,1:T(8,128)}, u32[]{:S(2)}) copy-start(f32[32,12]{0,1:T(8,128)} %param.49) | copy-start | bytes 4612
  602.2 24.6 %copy-start.18 = (f32[3,24]{1,0:T(4,128)S(1)}, f32[3,24]{1,0:T(4,128)}, u32[]{:S(2)}) copy-start(f32[3,24]{1,0:T(4,128)} %param.36) | copy-start | bytes 868
  602.2 24.6 %copy-start.21 = (f32[3,24]{1,0:T(4,128)S(1)}, f32[3,24]{1,0:T(4,128)}, u32[]{:S(2)}) copy-start(f32[3,24]{1,0:T(4,128)} %param.48) | copy-start | bytes 868
  602.2 24.6 %copy-start.22 = (f32[3,24]{1,0:T(4,128)S(1)}, f32[3,24]{1,0:T(4,128)}, u32[]{:S(2)}) copy-start(f32[3,24]{1,0:T(4,128)} %param.47) | copy-start | bytes 868
  602.8 27.0 %copy-start.8 = (f32[96,768]{1,0:T(8,128)S(1)}, f32[96,768]{1,0:T(8,128)}, u32[]{:S(2)}) copy-start(f32[96,768]{1,0:T(8,128)} %param.34) | copy-start | bytes 884740
  604.6 25.2 %copy-start.9 = (f32[96,768]{1,0:T(8,128)S(1)}, f32[96,768]{1,0:T(8,128)}, u32[]{:S(2)}) copy-start(f32[96,768]{1,0:T(8,128)} %get-tuple-element.75) | copy-start | bytes 884740
  604.6 27.5 %copy-start.4 = (f32[2,5,48,192]{3,2,1,0:T(8,128)S(1)}, f32[2,5,48,192]{3,2,1,0:T(8,128)}, u32[]{:S(2)}) copy-start(f32[2,5,48,192]{3,2,1,0:T(8,128)} %get-tuple-element.74) | copy-start | bytes 1105924
  625.1 7.0 %copy-start.10 = (f32[5,96,192]{2,1,0:T(8,128)S(1)}, f32[5,96,192]{2,1,0:T(8,128)}, u32[]{:S(2)}) copy-start(f32[5,96,192]{2,1,0:T(8,128)} %param.42) | copy-start | bytes 1105924
  627.5 7.2 %copy-start.3 = (f32[24,32128]{1,0:T(8,128)S(1)}, f32[24,32128]{1,0:T(8,128)}, u32[]{:S(2)}) copy-start(f32[24,32128]{1,0:T(8,128)} %param.40) | copy-start | bytes 9252868
  629.8 4.9 copy-start.1
  632.1 2.6 copy-start

commit v3 on v2

--- a/solution.py
+++ b/solution.py
@@ -100,37 +100,51 @@
     c = lax.broadcasted_iota(jnp.int32, (LANES, LANES), 1)
     return (r == c).astype(jnp.float32).astype(jnp.bfloat16)
 
+def turn_table(fold, table_ref, turned):
+    feats, vocab = table_ref.shape
+    pad = jnp.zeros((SLOT - feats, LANES), jnp.float32)
+
+    def build(b, carry):
+        parts = []
+        for j in range(GROUPS):
+            start = jnp.minimum(j * fold + b * LANES, vocab - LANES)
+            start = pl.multiple_of(start, LANES)
+            parts += [table_ref[:, pl.ds(start, LANES)], pad]
+        tile = jnp.concatenate(parts, axis=0)
+        turned[pl.ds(pl.multiple_of(b * LANES, LANES), LANES), :] = tile.T
+        return carry
+
+    lax.fori_loop(0, fold // LANES, build, 0)
+    turned[pl.ds(fold, 8), :] = jnp.zeros((8, LANES), jnp.float32)
+
+
+def look_up(row_ref, group_ref, source, turned, rows, feats):
+    tokens = rows.shape[0]
+    batch = 32
+
+    def fetch(b, carry):
+        for k in range(batch):
+            t = b * batch + k
+            rows[pl.ds(t, 1), :] = turned[pl.ds(row_ref[source, t], 1), :]
+        return carry
+
+    lax.fori_loop(0, tokens // batch, fetch, 0)
+    wide = dot_nt(eye(), rows[...].astype(jnp.bfloat16))
+    group = group_ref[source]
+    total = jnp.where(group == 0, wide[:SLOT], 0.0)
+    for j in range(1, GROUPS):
+        total = total + jnp.where(group == j, wide[j * SLOT : (j + 1) * SLOT], 0.0)
+    half = tokens // 2
+    return jnp.concatenate([total[:feats, :half], total[:feats, half:]], axis=0).astype(jnp.bfloat16)
+
+
 def lookup_kernel(fold, row_ref, group_ref, table_ref, out_ref, turned, rows):
-    feats, vocab = table_ref.shape
-    tokens = rows.shape[0]
     @pl.when(pl.program_id(0) == 0)
     def _():
-        pad = jnp.zeros((SLOT - feats, LANES), jnp.float32)
-        def build(b, _):
-            parts = []
-            for j in range(GROUPS):
-                start = jnp.minimum(j * fold + b * LANES, vocab - LANES)
-                start = pl.multiple_of(start, LANES)
-                parts += [table_ref[:, pl.ds(start, LANES)], pad]
-            tile = jnp.concatenate(parts, axis=0)
-            turned[pl.ds(pl.multiple_of(b * LANES, LANES), LANES), :] = tile.T
-            return 0
-        lax.fori_loop(0, fold // LANES, build, 0)
-        turned[pl.ds(fold, 8), :] = jnp.zeros((8, LANES), jnp.float32)
-    UN = 32
-    def fetch(b, _):
-        for k in range(UN):
-            t = b * UN + k
-            rows[pl.ds(t, 1), :] = turned[pl.ds(row_ref[0, 0, t], 1), :]
-        return 0
-    lax.fori_loop(0, tokens // UN, fetch, 0)
-    wide = lax.dot_general(eye(), rows[...].astype(jnp.bfloat16), (((1,), (1,)), ((), ())), preferred_element_type=jnp.float32)
-    group = group_ref[0]
-    total = jnp.where(group == 0, wide[:SLOT], 0.0)
-    for j in range(1, GROUPS):
-        total = total + jnp.where(group == j, wide[j * SLOT:(j + 1) * SLOT], 0.0)
-    half = tokens // 2
-    out_ref[0] = jnp.concatenate([total[:feats, :half], total[:feats, half:]], axis=0).astype(jnp.bfloat16)
+        turn_table(fold, table_ref, turned)
+
+    out_ref[0] = look_up(row_ref, group_ref, 0, turned, rows, table_ref.shape[0])
+
 
 def lookup(table, rows_idx, groups_idx):
     feats, vocab = table.shape
@@ -141,7 +155,7 @@
         grid=(n,),
         out_shape=jax.ShapeDtypeStruct((n, 2 * feats, tokens // 2), jnp.bfloat16),
         in_specs=[
-            pl.BlockSpec((1, 1, tokens), lambda s: (s, 0, 0), memory_space=pltpu.SMEM),
+            pl.BlockSpec((None, 1, tokens), lambda s: (s, 0, 0), memory_space=pltpu.SMEM),
             pl.BlockSpec((1, 1, tokens), lambda s: (s, 0, 0)),
             pl.BlockSpec((feats, vocab), lambda s: (0, 0)),
         ],
@@ -228,6 +242,18 @@
 MESH = pl.DeviceIdType.MESH
 
 
+def greet_all(count, cols, me):
+    barrier = pltpu.get_barrier_semaphore()
+
+    def greet(k, carry):
+        to = lax.rem(me + k, count)
+        pl.semaphore_signal(barrier, inc=1, device_id=(to // cols, lax.rem(to, cols)), device_id_type=MESH)
+        return carry
+
+    lax.fori_loop(1, count, greet, 0)
+    pl.semaphore_wait(barrier, count - 1)
+
+
 def exchange_kernel(same, src, dst, send_sem, recv_sem, own_sem):
     rows, cols = lax.axis_size("dp"), lax.axis_size("fsdp")
     count = rows * cols
@@ -387,14 +413,20 @@
         device_id=target, device_id_type=MESH)
 
 
-def gather_kernel(depth, *refs):
-    mine, outs = refs[:KINDS], refs[KINDS : 2 * KINDS]
-    theirs, own = refs[2 * KINDS : 2 * KINDS + 2]
-    pair_send, pair_recv, own_sem, send, got, sib_send, sib_got, diag_got = refs[2 * KINDS + 2 :]
+def front_kernel(fold, depth, row_ref, group_ref, table_ref, square_in, expand_in, reduce_in, *refs):
+    mine = (square_in, expand_in, reduce_in)
+    found, outs = refs[0], refs[1 : 1 + KINDS]
+    theirs, own, turned, rows, blocks = refs[1 + KINDS : 6 + KINDS]
+    (
+        pair_send, pair_recv, own_sem, send, got, sib_send, sib_got, diag_got, part_send, part_got, part_own
+    ) = refs[6 + KINDS :]
+    dp_size, fsdp_size = lax.axis_size("dp"), lax.axis_size("fsdp")
+    count = dp_size * fsdp_size
+    me = lax.axis_index("dp") * fsdp_size + lax.axis_index("fsdp")
     z, x, y, core = place()
     sibling = device_at(z, x, y, 1 - core)
     x_next, y_next = device_at(z, 1 - x, y, core), device_at(z, x, 1 - y, core)
-    greet_neighbours(depth)
+    greet_all(count, fsdp_size, me)
     pair = remote(mine[SQUARE].at[1 - core], theirs, pair_send, pair_recv, sibling)
     pair.start()
 
@@ -499,13 +531,42 @@
 
         sides(step, act)
 
+    turn_table(fold, table_ref, turned)
+
+    def part_copy(k):
+        target = lax.rem(me + k, count)
+        return pltpu.make_async_remote_copy(
+            src_ref=blocks.at[target],
+            dst_ref=found.at[me],
+            send_sem=part_send.at[k],
+            recv_sem=part_got.at[k],
+            device_id=(target // fsdp_size, lax.rem(target, fsdp_size)),
+            device_id_type=MESH,
+        )
+
+    def serve(k, carry):
+        target = lax.rem(me + k, count)
+        blocks[target] = look_up(row_ref, group_ref, target, turned, rows, table_ref.shape[0])
+        part_copy(k).start()
+        return carry
+
+    relays = []
     for step in range(1, depth + 2):
         if step < depth:
-            first(step)
+            relays.append((first, step))
         if 0 <= step - 1 < depth:
-            second(step - 1)
+            relays.append((second, step - 1))
         if 0 <= step - 2 < depth:
-            third(step - 2)
+            relays.append((third, step - 2))
+    done = 1
+    for n, (relay, step) in enumerate(relays):
+        until = min(count, 1 + ((n + 1) * count) // len(relays)) if n < len(relays) - 1 else count
+        lax.fori_loop(done, until, serve, 0)
+        done = until
+        relay(step)
+    blocks[me] = look_up(row_ref, group_ref, me, turned, rows, table_ref.shape[0])
+    own_part = pltpu.make_async_copy(blocks.at[me], found.at[me], part_own)
+    own_part.start()
 
     pair.wait_send()
     for a in range(KINDS):
@@ -533,37 +594,57 @@
         return carry
 
     lax.fori_loop(0, depth, finish, 0)
-
-
-def gather_blocks(square, expand, reduce_turned, call_id):
+    own_part.wait()
+
+    def end_part(k, carry):
+        part_copy(k).wait()
+        return carry
+
+    lax.fori_loop(1, count, end_part, 0)
+
+
+def run_front(row_all, group_all, table, square, expand, reduce_turned, call_id):
     depth = lax.axis_size("dp") // 2
-    count = 4 * depth
+    spots = 4 * depth
+    count, tokens = row_all.shape
+    feats, vocab = table.shape
+    fold = fold_rows(vocab)
+    blocks = (count, 2 * feats, tokens // 2)
+    whole = pl.BlockSpec(memory_space=pltpu.VMEM)
+    anywhere = pl.BlockSpec(memory_space=pl.ANY)
     return pl.pallas_call(
-        functools.partial(gather_kernel, depth),
+        functools.partial(front_kernel, fold, depth),
         out_shape=[
+            jax.ShapeDtypeStruct(blocks, jnp.bfloat16),
             jax.ShapeDtypeStruct((5, 768, 768), jnp.bfloat16),
             jax.ShapeDtypeStruct((768, 3072), jnp.bfloat16),
             jax.ShapeDtypeStruct((768, 3072), jnp.bfloat16),
         ],
-        in_specs=[pl.BlockSpec(memory_space=pltpu.VMEM)] * KINDS,
-        out_specs=[pl.BlockSpec(memory_space=pltpu.VMEM)] * KINDS,
+        in_specs=[pl.BlockSpec(memory_space=pltpu.SMEM)] + [whole] * 5,
+        out_specs=[anywhere] * 4,
         scratch_shapes=[
             pltpu.VMEM((5, 48, 192), jnp.bfloat16),
             pltpu.VMEM((5, 48, 384), jnp.bfloat16),
+            pltpu.VMEM((fold + 8, LANES), jnp.float32),
+            pltpu.VMEM((tokens, LANES), jnp.float32),
+            pltpu.VMEM(blocks, jnp.bfloat16),
             pltpu.SemaphoreType.DMA,
             pltpu.SemaphoreType.DMA,
             pltpu.SemaphoreType.DMA((KINDS,)),
-            pltpu.SemaphoreType.DMA((4, KINDS, count)),
-            pltpu.SemaphoreType.DMA((KINDS, count)),
-            pltpu.SemaphoreType.DMA((KINDS, count)),
-            pltpu.SemaphoreType.DMA((KINDS, count)),
+            pltpu.SemaphoreType.DMA((4, KINDS, spots)),
+            pltpu.SemaphoreType.DMA((KINDS, spots)),
+            pltpu.SemaphoreType.DMA((KINDS, spots)),
+            pltpu.SemaphoreType.DMA((KINDS, spots)),
             pltpu.SemaphoreType.DMA((KINDS, depth, 2)),
+            pltpu.SemaphoreType.DMA((count,)),
+            pltpu.SemaphoreType.DMA((count,)),
+            pltpu.SemaphoreType.DMA,
         ],
         compiler_params=pltpu.CompilerParams(
             collective_id=call_id, has_side_effects=True, vmem_limit_bytes=VMEM_CAP
         ),
-        name="gather_layer",
-    )(square, expand, reduce_turned)
+        name="front",
+    )(row_all, group_all.reshape(count, 1, tokens), table, square, expand, reduce_turned)
 
 
 def reduce_kernel(depth, *refs):
@@ -1282,9 +1363,12 @@
     square_low = square_weights.astype(jnp.bfloat16)
     expand_low = expand_weight.astype(jnp.bfloat16)
     reduce_low = reduce_weight.astype(jnp.bfloat16).T
+    table_low = embed_table.astype(jnp.bfloat16).astype(jnp.float32)
     if direct:
         square_pieces = square_low.reshape(5, 2, 48, 192).transpose(1, 0, 2, 3)
-        square_all, expand_all, reduce_all = gather_blocks(square_pieces, expand_low, reduce_low, 1)
+        found, square_all, expand_all, reduce_all = run_front(
+            row_all[:, 0], group_all[:, 0], table_low, square_pieces, expand_low, reduce_low, 1
+        )
     else:
 
         def whole(piece, row_name, column_name):
@@ -1295,11 +1379,9 @@
         square_all = whole(square_low, "dp", "fsdp")
         expand_all = whole(expand_low, "dp", "fsdp")
         reduce_all = whole(reduce_low, "fsdp", "dp")
-
-    table_low = embed_table.astype(jnp.bfloat16).astype(jnp.float32)
-    if feats_pad > feats:
-        table_low = jnp.pad(table_low, ((0, feats_pad - feats), (0, 0)))
-    found = exchange(lookup(table_low, row_all, group_all), False, 2, "send_features")
+        if feats_pad > feats:
+            table_low = jnp.pad(table_low, ((0, feats_pad - feats), (0, 0)))
+        found = exchange(lookup(table_low, row_all, group_all), False, 2, "send_features")
     half = token_count // 2
     found = found.reshape(count, 2, feats_pad, half)[:, :, :feats]
     found = found.transpose(0, 2, 1, 3).reshape(D, token_count)

time: 658 us -> 598 us (0.909)
  Pallas kernels: 549 us -> 494 us
    pallas_call x5 -> x4, Pallas kernels: 137 us -> 95 us  [exchange(): pl.pallas_call(functools.partial(exchange_kernel, same), out_shape=jax.Sh...]
    pallas_call x2 -> x1, Pallas kernels: 125 us -> 113 us  [run_front(): pl.pallas_call(functools.partial(front_kernel, fold, depth), out_shape=[j...]
where the time goes in v3:
time: 598 us; the launch traced here: 591 us
  Pallas kernels  494 us (83%)
  other arithmetic  49.5 us (8%)
  local copies, waits for them, and re-layouts  27.2 us (5%)
  between operations  13.9 us (2%)
  matrix products  6.72 us (1%)
    pallas_call x1, Pallas kernels, run_front(): pl.pallas_call(functools.partial(front_kernel, fold, depth), out_shape=[j...  113 us
    pallas_call x4, Pallas kernels, exchange(): pl.pallas_call(functools.partial(exchange_kernel, same), out_shape=jax.Sh...  95 us
    pallas_call x1, Pallas kernels, reduce_blocks(): pl.pallas_call(functools.partial(reduce_kernel, depth), out_shape=[jax.Sh...  71.8 us
    pallas_call x1, Pallas kernels, scatter(): pl.pallas_call(functools.partial(scatter_kernel, fold), grid=(n,), out_sh...  68.4 us
    pallas_call x1, Pallas kernels, run_feed_back(): pl.pallas_call(feed_back_kernel, grid=(1,), out_shape=[jax.ShapeDtypeStru...  52.2 us
    pallas_call x1, Pallas kernels, run_attend_back(): pl.pallas_call(attend_back_kernel, out_shape=[jax.ShapeDtypeStruct((5, D,...  49.5 us
    pallas_call x1, Pallas kernels, run_forward(): pl.pallas_call(forward_kernel, out_shape=[flat, flat, flat, flat, flat, f...  44.5 us
    sub x6, other arithmetic, adam_update(): weight - rate * (moment_hat / (jnp.sqrt(second_hat) + ADAM_EPS) + WEIGHT_...  14.7 us

profile of v3, /device:TPU:15, one launch (start us, length us, event | category | flops | bytes accessed | tf_op | source)
XLA Modules:
  0.0 591.2 jit_solution(16306049540161835986)
XLA Ops:
  5.1 1.3 fusion.20.src
  6.4 13.1 %share_start.1 = f32[32,16,128]{2,1,0:T(8,128)} custom-call(f32[1,16,128]{2,1,0:T(8,128)} %fusion.20.src), custom_call_target="tpu_custom_call" | custom-call | tf_op jit(solution)/shard_map/share_start/pallas_call | solution.py:301
  19.5 1.6 convert_and_fusion
  21.8 3.8 convert_convert_fusion.table_ref
  27.7 112.6 %front.1 = (bf16[32,48,512]{2,1,0:T(8,128)(2,1)}, bf16[5,768,768]{2,1,0:T(8,128)(2,1)}, bf16[768,3072]{1,0:T(8,128)(2,1)}, bf16[768,3072]{1,0:T(8,128)(2,1)}) custom-call(s32[32,1024]{1,0:T(8,128)} %bitcast.93, s32[32,1,1024]{2,1,0:T(1,128)} %bitcast.87, f32[24,32128]{1,0:T(8,128)} %convert_convert_fusion.table_ref, bf16[2,5,48,192]{3,2,1,0:T(8,128)(2,1)} %bitcast.91, ...), custom_call_target="tpu_custom_call" | custom-call | tf_op jit(solution)/shard_map/front/pallas_call | solution.py:615
  140.4 3.0 copy.85
  143.4 1.6 copy.95
  152.3 44.5 %layer_forward.1 = (bf16[1024,768]{1,0:T(8,128)(2,1)}, bf16[1024,768]{1,0:T(8,128)(2,1)}, bf16[1024,768]{1,0:T(8,128)(2,1)}, bf16[1024,768]{1,0:T(8,128)(2,1)}, ...) custom-call(bf16[768,1024]{1,0:T(8,128)(2,1)} %bitcast.79, ...), custom_call_target="tpu_custom_call" | custom-call | tf_op jit(solution)/shard_map/layer_forward/pallas_call | solution.py:1052
  196.8 24.8 %share_embeds.1 = bf16[32,16,768]{2,1,0:T(8,128)(2,1)} custom-call(bf16[1,16,768]{2,1,0:T(8,128)(2,1)} %bitcast.95), custom_call_target="tpu_custom_call" | custom-call | tf_op jit(solution)/shard_map/share_embeds/pallas_call | solution.py:301
  224.6 2.1 fusion.38
  227.6 1.3 multiply_reduce_fusion.7
  232.6 1.9 pad_maximum_fusion.1
  234.4 1.4 multiply_reduce_fusion.6
  235.8 1.9 multiply_reduce_fusion.4
  241.3 1.3 concatenate.58.grad_embed_ref
  242.6 52.2 %feed_backward.1 = (bf16[768,3072]{1,0:T(8,128)(2,1)}, bf16[768,3072]{1,0:T(8,128)(2,1)}, f32[1024,768]{1,0:T(8,128)}, bf16[1024,768]{1,0:T(8,128)(2,1)}, bf16[16,768]{1,0:T(8,128)(2,1)}, /*index=5*/f32[8,768]{1,0:T(8,128)}) custom-call(f32[16,768]{1,0:T(8,128)} %concatenate.58.grad_embed_ref, f32[16,768]{1,0:T(8,128)} %get-tuple-element.56.embed_ref, ...), custom_call_target="tpu_custom_call" | custom-call | tf_op jit(solution)/shard_map/feed_backward/pallas_call | solution.py:1142
  294.8 49.5 %attend_backward.1 = (bf16[5,768,768]{2,1,0:T(8,128)(2,1)}, f32[12,128,128]{2,1,0:T(8,128)}, f32[8,768]{1,0:T(8,128)}, bf16[768,1024]{1,0:T(8,128)(2,1)}) custom-call(f32[1024,768]{1,0:T(8,128)} %get-tuple-element.60.grad_middle_ref, bf16[1024,768]{1,0:T(8,128)(2,1)} %get-tuple-element.61.grad_low_ref, bf16[16,768]{1,0:T(8,128)(2,1)} %get-tuple-element.62.grad_proj_ref, ...), custom_call_target="tpu_custom_call" | custom-call | tf_op jit(solution)/shard_map/attend_backward/pallas_call | solution.py:1268
  345.8 71.8 %reduce_layer.1 = (f32[2,5,48,192]{3,2,1,0:T(8,128)}, f32[96,768]{1,0:T(8,128)}, f32[192,384]{1,0:T(8,128)}) custom-call(bf16[5,768,768]{2,1,0:T(8,128)(2,1)} %get-tuple-element.73.refs_0_, bf16[768,3072]{1,0:T(8,128)(2,1)} %get-tuple-element.74.refs_1_, bf16[768,3072]{1,0:T(8,128)(2,1)} %get-tuple-element.75.refs_2_), custom_call_target="tpu_custom_call" | custom-call | tf_op jit(solution)/shard_map/reduce_layer/pallas_call | solution.py:865
  417.6 1.8 multiply_reduce_fusion.1
  419.4 1.6 multiply_reduce_fusion.3
  422.3 1.6 multiply_reduce_fusion.2
  424.6 3.8 reshape.325
  428.5 2.9 copy.87
  431.4 42.8 %send_gradients.1.grad_ref = bf16[32,48,512]{2,1,0:T(8,128)(2,1)} custom-call(bf16[32,48,512]{2,1,0:T(8,128)(2,1)} %bitcast.81), custom_call_target="tpu_custom_call" | custom-call | tf_op jit(solution)/shard_map/send_gradients/pallas_call | solution.py:301
  474.2 68.4 %scatter.1 = f32[24,32128]{1,0:T(8,128)} custom-call(s32[32,1,1024]{2,1,0:T(1,128)} %bitcast.90, s32[32,1,1024]{2,1,0:T(1,128)} %bitcast.88, bf16[32,48,512]{2,1,0:T(8,128)(2,1)} %send_gradients.1.grad_ref), custom_call_target="tpu_custom_call" | custom-call | tf_op jit(solution)/shard_map/scatter/pallas_call | solution.py:215
  542.6 3.3 multiply_reduce_fusion
  548.4 1.8 fusion.42
  550.9 14.3 %share_small.1 = f32[32,24,128]{2,1,0:T(8,128)} custom-call(f32[1,24,128]{2,1,0:T(8,128)} %fusion.18.src), custom_call_target="tpu_custom_call" | custom-call | tf_op jit(solution)/shard_map/share_small/pallas_call | solution.py:301
  573.0 2.3 multiply_subtract_fusion.2
  575.4 2.3 multiply_subtract_fusion.3
  577.7 2.5 multiply_subtract_fusion.1
  580.3 6.3 %multiply_subtract_fusion = (f32[24,32128]{1,0:T(8,128)}, f32[24,32128]{1,0:T(8,128)}, f32[24,32128]{1,0:T(8,128)}) fusion(f32[24,32128]{1,0:T(8,128)S(1)} %copy-done.1, f32[24,32128]{1,0:T(8,128)S(1)} %copy-done, f32[]{:T(128)S(6)} %min.3, f32[24,32128]{1,0:T(8,128)S(1)} %copy-done.3, f32[24,32128]{1,0:T(8,128)} %param.39), kind=kLoop, calls=%fused_computation.9 | loop fusion | flops 12337152 | bytes 21590020 | tf_op jit(solution)/shard_map/sub | solution.py:80
  (117 shorter events, 32.2 us)
Async XLA Ops:
  21.1 4.5 copy-start.10
  21.8 3.8 copy-start.5
  21.8 4.6 copy-start.6
  21.8 5.2 copy-start.7
  140.3 7.3 %copy-start.24 = (s32[4]{0:T(128)S(1)}, s32[4]{0:T(128)}, u32[]{:S(2)}) copy-start(s32[4]{0:T(128)} %param.56) | copy-start | bytes 52
  140.3 7.3 %copy-start.25 = (s32[4]{0:T(128)S(1)}, s32[4]{0:T(128)}, u32[]{:S(2)}) copy-start(s32[4]{0:T(128)} %param.55) | copy-start | bytes 52
  140.3 7.4 %copy-start.15 = (pred[16,1024]{1,0:T(8,128)(4,1)S(1)}, pred[16,1024]{1,0:T(8,128)(4,1)}, u32[]{:S(2)}) copy-start(pred[16,1024]{1,0:T(8,128)(4,1)} %constant.89.clone) | copy-start | bytes 49156
  140.3 7.4 %copy-start.21 = (s32[1024]{0:T(1024)S(1)}, s32[1024]{0:T(1024)}, u32[]{:S(2)}) copy-start(s32[1024]{0:T(1024)} %constant.203) | copy-start | bytes 12292
  140.3 8.1 %copy-start.12 = (pred[8,128,128]{2,1,0:T(32,128)(4,1)S(1)}, pred[8,128,128]{2,1,0:T(32,128)(4,1)}, u32[]{:S(2)}) copy-start(pred[8,128,128]{2,1,0:T(32,128)(4,1)} %constant.90.clone) | copy-start | bytes 393220
  143.4 6.6 %copy-start.2 = (f32[16384,32]{0,1:T(8,128)S(1)}, f32[16384,32]{0,1:T(8,128)}, u32[]{:S(2)}) copy-start(f32[16384,32]{0,1:T(8,128)} %constant.91.clone) | copy-start | bytes 6291460
  143.4 6.6 %copy-start.13 = (f32[32,12]{0,1:T(8,128)S(1)}, f32[32,12]{0,1:T(8,128)}, u32[]{:S(2)}) copy-start(f32[32,12]{0,1:T(8,128)} %param.37) | copy-start | bytes 4612
  223.9 2.7 copy-start.16
  223.9 2.7 copy-start.20
  547.7 24.0 %copy-start.14 = (f32[32,12]{0,1:T(8,128)S(1)}, f32[32,12]{0,1:T(8,128)}, u32[]{:S(2)}) copy-start(f32[32,12]{0,1:T(8,128)} %param.37) | copy-start | bytes 4612
  547.7 24.0 %copy-start.17 = (f32[32,12]{0,1:T(8,128)S(1)}, f32[32,12]{0,1:T(8,128)}, u32[]{:S(2)}) copy-start(f32[32,12]{0,1:T(8,128)} %param.50) | copy-start | bytes 4612
  547.7 24.0 %copy-start.18 = (f32[32,12]{0,1:T(8,128)S(1)}, f32[32,12]{0,1:T(8,128)}, u32[]{:S(2)}) copy-start(f32[32,12]{0,1:T(8,128)} %param.49) | copy-start | bytes 4612
  547.7 24.6 %copy-start.19 = (f32[3,24]{1,0:T(4,128)S(1)}, f32[3,24]{1,0:T(4,128)}, u32[]{:S(2)}) copy-start(f32[3,24]{1,0:T(4,128)} %param.36) | copy-start | bytes 868
  547.8 24.6 %copy-start.22 = (f32[3,24]{1,0:T(4,128)S(1)}, f32[3,24]{1,0:T(4,128)}, u32[]{:S(2)}) copy-start(f32[3,24]{1,0:T(4,128)} %param.48) | copy-start | bytes 868
  547.8 24.6 %copy-start.23 = (f32[3,24]{1,0:T(4,128)S(1)}, f32[3,24]{1,0:T(4,128)}, u32[]{:S(2)}) copy-start(f32[3,24]{1,0:T(4,128)} %param.47) | copy-start | bytes 868
  548.4 27.0 %copy-start.8 = (f32[96,768]{1,0:T(8,128)S(1)}, f32[96,768]{1,0:T(8,128)}, u32[]{:S(2)}) copy-start(f32[96,768]{1,0:T(8,128)} %param.34) | copy-start | bytes 884740
  550.2 25.2 %copy-start.9 = (f32[96,768]{1,0:T(8,128)S(1)}, f32[96,768]{1,0:T(8,128)}, u32[]{:S(2)}) copy-start(f32[96,768]{1,0:T(8,128)} %get-tuple-element.77) | copy-start | bytes 884740
  550.2 27.5 %copy-start.4 = (f32[2,5,48,192]{3,2,1,0:T(8,128)S(1)}, f32[2,5,48,192]{3,2,1,0:T(8,128)}, u32[]{:S(2)}) copy-start(f32[2,5,48,192]{3,2,1,0:T(8,128)} %get-tuple-element.76) | copy-start | bytes 1105924
  570.7 7.0 %copy-start.11 = (f32[5,96,192]{2,1,0:T(8,128)S(1)}, f32[5,96,192]{2,1,0:T(8,128)}, u32[]{:S(2)}) copy-start(f32[5,96,192]{2,1,0:T(8,128)} %param.42) | copy-start | bytes 1105924
  573.0 7.2 %copy-start.3 = (f32[24,32128]{1,0:T(8,128)S(1)}, f32[24,32128]{1,0:T(8,128)}, u32[]{:S(2)}) copy-start(f32[24,32128]{1,0:T(8,128)} %param.40) | copy-start | bytes 9252868
  575.4 4.9 copy-start.1
  577.6 2.6 copy-start

commit v4 on v3

--- a/solution.py
+++ b/solution.py
@@ -647,126 +647,164 @@
     )(row_all, group_all.reshape(count, 1, tokens), table, square, expand, reduce_turned)
 
 
-def reduce_kernel(depth, *refs):
-    count = KINDS
-    grads, outs = refs[:count], refs[count : 2 * count]
-    work, paired, step_one, from_x, from_y, from_z = [
-        refs[(2 + k) * count : (3 + k) * count] for k in range(6)
-    ]
-    spare = refs[8 * count]
-    load_sem, pair_send, pair_got, send, one_got, x_got, y_got, z_got, end_send, end_got = refs[8 * count + 1 :]
-    z, x, y, core = place()
-    sibling = device_at(z, x, y, 1 - core)
-    x_next, y_next = device_at(z, 1 - x, y, core), device_at(z, x, 1 - y, core)
-    greet_neighbours(depth)
-
-    def index(z_at, x_at):
-        return z_at * 2 + x_at
-
-    def load(a, z_at, x_at, y_at):
-        i = index(z_at, x_at)
+class Reduction:
+    def __init__(self, kinds, depth, grads, outs, work, buffers, sems):
+        self.kinds, self.depth, self.grads, self.outs, self.own_work = kinds, depth, grads, outs, work
+        count = len(kinds)
+        self.paired, self.step_one, self.from_x, self.from_y, self.from_z = [
+            dict(zip(kinds, buffers[k * count : (k + 1) * count])) for k in range(5)
+        ]
+        self.load_sem, self.pair_send, self.pair_got, self.send, self.one_got = sems[:5]
+        self.x_got, self.y_got, self.z_got = sems[5:8]
+        self.number = {a: n for n, a in enumerate(kinds)}
+        z, x, y, core = place()
+        self.z, self.x, self.y, self.core = z, x, y, core
+        self.sibling = device_at(z, x, y, 1 - core)
+        self.x_next, self.y_next = device_at(z, 1 - x, y, core), device_at(z, x, 1 - y, core)
+
+    def work(self, a, z_at, x_at, y_at):
+        if self.own_work is None:
+            return spot(self.grads, a, z_at, x_at, y_at, self.core)
+        return self.own_work[a].at[z_at * 2 + x_at, y_at]
+
+    def load(self, a, z_at, x_at, y_at):
         return pltpu.make_async_copy(
-            spot(grads, a, z_at, x_at, y_at, core), work[a].at[i, y_at], load_sem.at[a, i, y_at]
+            spot(self.grads, a, z_at, x_at, y_at, self.core),
+            self.work(a, z_at, x_at, y_at),
+            self.load_sem.at[self.number[a], z_at * 2 + x_at, y_at],
         )
 
-    def pair(a, z_at, x_at, y_at):
-        i = index(z_at, x_at)
+    def pair(self, a, z_at, x_at, y_at):
+        n, i = self.number[a], z_at * 2 + x_at
         return remote(
-            spot(grads, a, z_at, x_at, y_at, 1 - core),
-            paired[a].at[i, y_at],
-            pair_send.at[a, i, y_at],
-            pair_got.at[a, i, y_at],
-            sibling,
+            spot(self.grads, a, z_at, x_at, y_at, 1 - self.core),
+            self.paired[a].at[i, y_at],
+            self.pair_send.at[n, i, y_at],
+            self.pair_got.at[n, i, y_at],
+            self.sibling,
         )
 
-    rounds = list(range(depth - 1, -1, -1))
-
-    def sides(step, act):
+    def sides(self, step, act):
         if step == 0:
-            act(z)
+            act(self.z)
             return
         for sign in (1, -1):
-            z_at = z + sign * step
-
-            @pl.when((z_at >= 0) & (z_at < depth))
+            z_at = self.z + sign * step
+
+            @pl.when((z_at >= 0) & (z_at < self.depth))
             def _():
                 act(z_at)
 
-    for x_at, y_at in ((1 - x, 1 - y), (1 - x, y), (x, 1 - y), (x, y)):
-        for step in rounds:
-
-            def begin(z_at):
-                for a in range(count):
-                    load(a, z_at, x_at, y_at).start()
-                    pair(a, z_at, x_at, y_at).start()
-
-            sides(step, begin)
-
-    def ready(a, z_at, x_at, y_at):
-        load(a, z_at, x_at, y_at).wait()
-        pair(a, z_at, x_at, y_at).wait_recv()
-
-    def total(a, z_at, x_at, y_at, first, last, extra=()):
-        i = index(z_at, x_at)
+    def begin(self):
+        x, y = self.x, self.y
+        for x_at, y_at in ((1 - x, 1 - y), (1 - x, y), (x, 1 - y), (x, y)):
+            for step in range(self.depth - 1, -1, -1):
+
+                def start(z_at):
+                    for a in self.kinds:
+                        if self.own_work is not None:
+                            self.load(a, z_at, x_at, y_at).start()
+                        self.pair(a, z_at, x_at, y_at).start()
+
+                self.sides(step, start)
+
+    def ready(self, a, z_at, x_at, y_at):
+        if self.own_work is not None:
+            self.load(a, z_at, x_at, y_at).wait()
+        self.pair(a, z_at, x_at, y_at).wait_recv()
+
+    def total(self, a, z_at, x_at, y_at, first, last, extra=()):
+        here = self.work(a, z_at, x_at, y_at)
+        paired = self.paired[a].at[z_at * 2 + x_at, y_at]
 
         def add(k, carry):
-            here = block_step(work[a].at[i, y_at], a, k)
-            value = here[...].astype(jnp.float32)
-            value = value + block_step(paired[a].at[i, y_at], a, k)[...].astype(jnp.float32)
+            step = block_step(here, a, k)
+            value = step[...].astype(jnp.float32) + block_step(paired, a, k)[...].astype(jnp.float32)
             for buffer in extra:
                 value = value + block_step(buffer, a, k)[...].astype(jnp.float32)
-            here[...] = value.astype(jnp.bfloat16)
+            step[...] = value.astype(jnp.bfloat16)
             return carry
 
         lax.fori_loop(first, last, add, 0)
 
-    def diag_copy(a, z_at, part):
+    def diag_copy(self, a, z_at, part):
+        n = self.number[a]
         return remote(
-            block_part(work[a].at[index(z_at, 1 - x), 1 - y], a, part),
-            block_part(step_one[a].at[z_at], a, part),
-            send.at[part, a, z_at],
-            one_got.at[a, part, z_at],
-            y_next if part == 0 else x_next,
+            block_part(self.work(a, z_at, 1 - self.x, 1 - self.y), a, part),
+            block_part(self.step_one[a].at[z_at], a, part),
+            self.send.at[part, n, z_at],
+            self.one_got.at[n, part, z_at],
+            self.y_next if part == 0 else self.x_next,
         )
 
-    def diag(z_at):
-        for a in range(count):
-            ready(a, z_at, 1 - x, 1 - y)
-            total(a, z_at, 1 - x, 1 - y, 0, STEPS[a])
-            for part in range(2):
-                diag_copy(a, z_at, part).start()
-
-    def x_copy(a, z_at):
-        return remote(work[a].at[index(z_at, 1 - x), y], from_x[a].at[z_at], send.at[2, a, z_at], x_got.at[a, z_at], x_next)
-
-    def y_copy(a, z_at):
-        return remote(work[a].at[index(z_at, x), 1 - y], from_y[a].at[z_at], send.at[3, a, z_at], y_got.at[a, z_at], y_next)
-
-    def columns(z_at):
-        for a in range(count):
-            middle, last = FIRST[a], STEPS[a]
-            ready(a, z_at, 1 - x, y)
-            diag_copy(a, z_at, 0).wait_recv()
-            total(a, z_at, 1 - x, y, 0, middle, [step_one[a].at[z_at]])
-            total(a, z_at, 1 - x, y, middle, last)
-            x_copy(a, z_at).start()
-            ready(a, z_at, x, 1 - y)
-            diag_copy(a, z_at, 1).wait_recv()
-            total(a, z_at, x, 1 - y, 0, middle)
-            total(a, z_at, x, 1 - y, middle, last, [step_one[a].at[z_at]])
-            y_copy(a, z_at).start()
-
-    def z_copy(a, z_at, side):
-        target = device_at(z + 1, x, y, core) if side == 0 else device_at(z - 1, x, y, core)
-        return remote(work[a].at[index(z_at, x), y], from_z[a].at[side, z_at], send.at[4, a, z_at], z_got.at[a, side, z_at], target)
-
-    def line(step):
+    def diag(self, step):
         def act(z_at):
-            for a in range(count):
-                ready(a, z_at, x, y)
-                x_copy(a, z_at).wait_recv()
-                y_copy(a, z_at).wait_recv()
-                across = [from_x[a].at[z_at], from_y[a].at[z_at]]
+            for a in self.kinds:
+                self.ready(a, z_at, 1 - self.x, 1 - self.y)
+                self.total(a, z_at, 1 - self.x, 1 - self.y, 0, STEPS[a])
+                for part in range(2):
+                    self.diag_copy(a, z_at, part).start()
+
+        self.sides(step, act)
+
+    def x_copy(self, a, z_at):
+        n = self.number[a]
+        return remote(
+            self.work(a, z_at, 1 - self.x, self.y),
+            self.from_x[a].at[z_at],
+            self.send.at[2, n, z_at],
+            self.x_got.at[n, z_at],
+            self.x_next,
+        )
+
+    def y_copy(self, a, z_at):
+        n = self.number[a]
+        return remote(
+            self.work(a, z_at, self.x, 1 - self.y),
+            self.from_y[a].at[z_at],
+            self.send.at[3, n, z_at],
+            self.y_got.at[n, z_at],
+            self.y_next,
+        )
+
+    def columns(self, step):
+        x, y = self.x, self.y
+
+        def act(z_at):
+            for a in self.kinds:
+                middle, last = FIRST[a], STEPS[a]
+                self.ready(a, z_at, 1 - x, y)
+                self.diag_copy(a, z_at, 0).wait_recv()
+                self.total(a, z_at, 1 - x, y, 0, middle, [self.step_one[a].at[z_at]])
+                self.total(a, z_at, 1 - x, y, middle, last)
+                self.x_copy(a, z_at).start()
+                self.ready(a, z_at, x, 1 - y)
+                self.diag_copy(a, z_at, 1).wait_recv()
+                self.total(a, z_at, x, 1 - y, 0, middle)
+                self.total(a, z_at, x, 1 - y, middle, last, [self.step_one[a].at[z_at]])
+                self.y_copy(a, z_at).start()
+
+        self.sides(step, act)
+
+    def z_copy(self, a, z_at, side, target):
+        n = self.number[a]
+        return remote(
+            self.work(a, z_at, self.x, self.y),
+            self.from_z[a].at[side, z_at],
+            self.send.at[4, n, z_at],
+            self.z_got.at[n, side, z_at],
+            target,
+        )
+
+    def line(self, step, keep=None):
+        z, x, y, core, depth = self.z, self.x, self.y, self.core, self.depth
+
+        def act(z_at):
+            for a in self.kinds:
+                self.ready(a, z_at, x, y)
+                self.x_copy(a, z_at).wait_recv()
+                self.y_copy(a, z_at).wait_recv()
+                across = [self.from_x[a].at[z_at], self.from_y[a].at[z_at]]
                 if step > 0:
                     upward = z_at > z
                     before = (upward & (z > 0)) | (jnp.logical_not(upward) & (z < depth - 1))
@@ -774,127 +812,101 @@
 
                     @pl.when(before)
                     def _():
-                        remote(
-                            work[a].at[index(z_at, x), y],
-                            from_z[a].at[side, z_at],
-                            send.at[4, a, z_at],
-                            z_got.at[a, side, z_at],
-                            sibling,
-                        ).wait_recv()
-                        total(a, z_at, x, y, 0, STEPS[a], across + [from_z[a].at[side, z_at]])
+                        self.z_copy(a, z_at, side, self.sibling).wait_recv()
+                        self.total(a, z_at, x, y, 0, STEPS[a], across + [self.from_z[a].at[side, z_at]])
 
                     @pl.when(jnp.logical_not(before))
                     def _():
-                        total(a, z_at, x, y, 0, STEPS[a], across)
+                        self.total(a, z_at, x, y, 0, STEPS[a], across)
 
                     @pl.when(upward)
                     def _():
-                        z_copy(a, z_at, 0).start()
+                        self.z_copy(a, z_at, 0, device_at(z + 1, x, y, core)).start()
 
                     @pl.when(jnp.logical_not(upward))
                     def _():
-                        z_copy(a, z_at, 1).start()
+                        self.z_copy(a, z_at, 1, device_at(z - 1, x, y, core)).start()
                 else:
                     for side in range(2):
                         present = (z > 0) if side == 0 else (z < depth - 1)
 
                         @pl.when(present)
                         def _():
-                            z_copy(a, z, side).wait_recv()
+                            self.z_copy(a, z, side, self.sibling).wait_recv()
 
                         @pl.when(jnp.logical_not(present))
                         def _():
-                            from_z[a][side, z] = jnp.zeros(BLOCKS[a], jnp.bfloat16)
+                            self.from_z[a][side, z] = jnp.zeros(BLOCKS[a], jnp.bfloat16)
+
+                    here, paired = self.work(a, z, x, y), self.paired[a].at[z * 2 + x, y]
 
                     def finish(k, carry):
-                        i = index(z, x)
-                        value = block_step(work[a].at[i, y], a, k)[...].astype(jnp.float32)
-                        for buffer in [paired[a].at[i, y]] + across + [from_z[a].at[0, z], from_z[a].at[1, z]]:
+                        value = block_step(here, a, k)[...].astype(jnp.float32)
+                        for buffer in [paired] + across + [self.from_z[a].at[0, z], self.from_z[a].at[1, z]]:
                             value = value + block_step(buffer, a, k)[...].astype(jnp.float32)
                         if a == SQUARE:
+                            spare = self.outs[3]
                             low, high = value[:, :192], pltpu.roll(value, 192, 1)[:, :192]
-                            outs[a][core, k] = jnp.where(core == 0, low, high)
+                            self.outs[SQUARE][core, k] = jnp.where(core == 0, low, high)
                             spare[k] = jnp.where(core == 0, high, low)
                         else:
-                            block_step(outs[a], a, k)[...] = value
+                            block_step(self.outs[a], a, k)[...] = value
                         return carry
 
                     lax.fori_loop(0, STEPS[a], finish, 0)
-                    if a == SQUARE:
-                        end_copy().start()
-
-        sides(step, act)
-
-    def end_copy():
-        return remote(spare, outs[SQUARE].at[core], end_send, end_got, sibling)
-
-    for k in range(depth + 2):
-        if k < depth:
-            sides(rounds[k], diag)
-        if 0 <= k - 1 < depth:
-            sides(rounds[k - 1], columns)
-        if 0 <= k - 2 < depth:
-            line(rounds[k - 2])
-
-    def finish_all(z_at, carry):
-        for a in range(count):
-            for x_at in range(2):
-                for y_at in range(2):
-                    pair(a, z_at, x_at, y_at).wait_send()
-            for part in range(2):
-                diag_copy(a, z_at, part).wait_send()
-            x_copy(a, z_at).wait_send()
-            y_copy(a, z_at).wait_send()
-
-            @pl.when(z_at != z)
-            def _():
-                z_copy(a, z_at, 0).wait_send()
-        return carry
-
-    lax.fori_loop(0, depth, finish_all, 0)
-    end_copy().wait_send()
-    remote(spare, outs[SQUARE].at[1 - core], end_send, end_got, sibling).wait_recv()
-
-
-def reduce_blocks(square, expand, reduce_turned, call_id):
-    depth = lax.axis_size("dp") // 2
-
+
+        self.sides(step, act)
+
+    def groups(self):
+        rounds = list(range(self.depth - 1, -1, -1))
+        for k in range(self.depth + 2):
+            group = []
+            if k < self.depth:
+                group.append((self.diag, rounds[k]))
+            if 0 <= k - 1 < self.depth:
+                group.append((self.columns, rounds[k - 1]))
+            if 0 <= k - 2 < self.depth:
+                group.append((self.line, rounds[k - 2]))
+            yield group
+
+    def finish(self):
+        def wait(z_at, carry):
+            for a in self.kinds:
+                for x_at in range(2):
+                    for y_at in range(2):
+                        self.pair(a, z_at, x_at, y_at).wait_send()
+                for part in range(2):
+                    self.diag_copy(a, z_at, part).wait_send()
+                self.x_copy(a, z_at).wait_send()
+                self.y_copy(a, z_at).wait_send()
+
+                @pl.when(z_at != self.z)
+                def _():
+                    self.z_copy(a, z_at, 0, self.sibling).wait_send()
+            return carry
+
+        lax.fori_loop(0, self.depth, wait, 0)
+
+
+def reduction_scratch(kinds, depth):
     def buffers(*lead):
-        return [pltpu.VMEM(lead + block, jnp.bfloat16) for block in BLOCKS]
-
-    return pl.pallas_call(
-        functools.partial(reduce_kernel, depth),
-        out_shape=[
-            jax.ShapeDtypeStruct((2, 5, 48, 192), jnp.float32),
-            jax.ShapeDtypeStruct((96, 768), jnp.float32),
-            jax.ShapeDtypeStruct((192, 384), jnp.float32),
+        return [pltpu.VMEM(lead + BLOCKS[a], jnp.bfloat16) for a in kinds]
+
+    count = len(kinds)
+    spots = pltpu.SemaphoreType.DMA((count, 2 * depth, 2))
+    return (
+        buffers(2 * depth, 2) + buffers(depth) + buffers(depth) + buffers(depth) + buffers(2, depth),
+        [
+            spots,
+            spots,
+            spots,
+            pltpu.SemaphoreType.DMA((5, count, depth)),
+            pltpu.SemaphoreType.DMA((count, 2, depth)),
+            pltpu.SemaphoreType.DMA((count, depth)),
+            pltpu.SemaphoreType.DMA((count, depth)),
+            pltpu.SemaphoreType.DMA((count, 2, depth)),
         ],
-        in_specs=[pl.BlockSpec(memory_space=pl.ANY)] * KINDS,
-        out_specs=[pl.BlockSpec(memory_space=pltpu.VMEM)] * KINDS,
-        scratch_shapes=buffers(2 * depth, 2)
-        + buffers(2 * depth, 2)
-        + buffers(depth)
-        + buffers(depth)
-        + buffers(depth)
-        + buffers(2, depth)
-        + [
-            pltpu.VMEM((5, 48, 192), jnp.float32),
-            pltpu.SemaphoreType.DMA((KINDS, 2 * depth, 2)),
-            pltpu.SemaphoreType.DMA((KINDS, 2 * depth, 2)),
-            pltpu.SemaphoreType.DMA((KINDS, 2 * depth, 2)),
-            pltpu.SemaphoreType.DMA((5, KINDS, depth)),
-            pltpu.SemaphoreType.DMA((KINDS, 2, depth)),
-            pltpu.SemaphoreType.DMA((KINDS, depth)),
-            pltpu.SemaphoreType.DMA((KINDS, depth)),
-            pltpu.SemaphoreType.DMA((KINDS, 2, depth)),
-            pltpu.SemaphoreType.DMA,
-            pltpu.SemaphoreType.DMA,
-        ],
-        compiler_params=pltpu.CompilerParams(
-            collective_id=call_id, has_side_effects=True, vmem_limit_bytes=VMEM_CAP
-        ),
-        name="reduce_layer",
-    )(square, expand, reduce_turned)
+    )
 
 
 TILE = 128
@@ -1166,11 +1178,11 @@
     )(grad_embed, embeds, inverse, pool, lengths, square, middle, ending, expand, reduce_turned, gains)
 
 
-def attend_back_kernel(
+def attend_back_steps(
     grad_middle_ref, grad_low_ref, grad_proj_ref, pooled_ref, start_ref, query_ref, key_ref, value_ref, mixed_ref,
     square_ref, gains_ref, bias_ref, mask_ref, rank_ref,
-    grad_square_ref, grad_score_ref, grad_gain_ref, send_ref,
-    grad_mixed, turned, grad_query, grad_key, grad_value, start_low,
+    grad_square_ref, grad_score_ref, grad_gain_ref, grad_mixed, turned, grad_query, grad_key, grad_value,
+    between, squares_done, put,
 ):
     tokens = start_ref.shape[0]
     big = 512
@@ -1216,7 +1228,15 @@
             grad_key[rows, lanes] = (dot_tn(grad_scores, split_heads(query)) * HEAD ** (-0.5)).astype(jnp.bfloat16)
         return carry
 
-    lax.fori_loop(0, tokens // TILE, attend, 0)
+    tiles = tokens // TILE
+    done = 0
+    for n, act in enumerate(between):
+        until = ((n + 1) * tiles) // (len(between) + 1)
+        if until > done:
+            lax.fori_loop(done, until, attend, 0)
+        done = until
+        act()
+    lax.fori_loop(done, tiles, attend, 0)
 
     def renorm(r, carry):
         rows = rows_at(r, 256)
@@ -1228,6 +1248,7 @@
     outer(0, grad_query)
     outer(1, grad_key)
     outer(2, grad_value)
+    squares_done()
     grad_gain_ref[...] = jnp.zeros_like(grad_gain_ref)
 
     def end(r, carry):
@@ -1244,26 +1265,41 @@
 
     lax.fori_loop(0, tokens // 256, end, 0)
 
-    def hot(r, carry):
-        rows = rows_at(r, 256)
-        start_low[rows, :] = hot_rows(rank_ref, rows, tokens)
-        return carry
-
-    lax.fori_loop(0, tokens // 256, hot, 0)
-
-    def gather_rows(r, carry):
+    def merge(r, carry):
         rows = rows_at(r, 384)
-        send_ref[rows, :] = dot_nn(turned[rows, :], start_low[...]).astype(jnp.bfloat16)
-        return carry
-
-    lax.fori_loop(0, D // 384, gather_rows, 0)
-
-
-def run_attend_back(
-    grad_middle, grad_low, grad_proj, pooled, start, queries, keys_here, values_here, mixed, square, gains, bias,
-    mask, rank,
-):
-    tokens = start.shape[0]
+        total = jnp.zeros((384, tokens), jnp.float32)
+        for c in range(tokens // 256):
+            at = pl.ds(c * 256, 256)
+            total = total + dot_nn(turned[rows, at], hot_rows(rank_ref, at, tokens))
+        put(r, total)
+        return carry
+
+    lax.fori_loop(0, D // 384, merge, 0)
+
+
+def attend_back_kernel(*refs):
+    ins, rest = refs[:14], refs[14:]
+    grad_square_ref, grad_score_ref, grad_gain_ref, send_ref = rest[:4]
+
+    def put(r, total):
+        send_ref[rows_at(r, 384), :] = total.astype(jnp.bfloat16)
+
+    attend_back_steps(*ins, grad_square_ref, grad_score_ref, grad_gain_ref, *rest[4:], [], lambda: None, put)
+
+
+def attend_scratch(tokens):
+    low = jnp.bfloat16
+    return [
+        pltpu.VMEM((tokens, D), low),
+        pltpu.VMEM((D, tokens), low),
+        pltpu.VMEM((tokens, D), low),
+        pltpu.VMEM((tokens, D), low),
+        pltpu.VMEM((tokens, D), low),
+    ]
+
+
+def run_attend_back(*ins):
+    tokens = ins[0].shape[0]
     low = jnp.bfloat16
     return pl.pallas_call(
         attend_back_kernel,
@@ -1273,20 +1309,141 @@
             jax.ShapeDtypeStruct((8, D), jnp.float32),
             jax.ShapeDtypeStruct((D, tokens), low),
         ],
-        scratch_shapes=[
-            pltpu.VMEM((tokens, D), low),
-            pltpu.VMEM((D, tokens), low),
-            pltpu.VMEM((tokens, D), low),
-            pltpu.VMEM((tokens, D), low),
-            pltpu.VMEM((tokens, D), low),
-            pltpu.VMEM((tokens, tokens), low),
-        ],
+        scratch_shapes=attend_scratch(tokens),
         compiler_params=pltpu.CompilerParams(vmem_limit_bytes=VMEM_CAP),
         name="attend_backward",
-    )(
-        grad_middle, grad_low, grad_proj, pooled, start, queries, keys_here, values_here, mixed, square, gains, bias,
-        mask, rank,
-    )
+    )(*ins)
+
+
+FEED_KINDS = (EXPAND, REDUCE)
+SQUARE_KINDS = (SQUARE,)
+BACK_CAP = 62 * 1024 * 1024
+
+
+def back_kernel(depth, *refs):
+    ins, refs = refs[:14], refs[14:]
+    grad_expand, grad_reduce = refs[:2]
+    square_sum, expand_sum, reduce_sum, grad_score_ref, grad_gain_ref, returned = refs[2:8]
+    grad_square, *steps = refs[8:14]
+    blocks, spare, work_expand, work_reduce = refs[14:18]
+    refs = refs[18:]
+    feed_buffers, refs = refs[:10], refs[10:]
+    feed_sems, refs = refs[:8], refs[8:]
+    square_buffers, refs = refs[:5], refs[5:]
+    square_sems, refs = refs[:8], refs[8:]
+    part_send, part_got, part_own, end_send, end_got = refs
+    dp_size, fsdp_size = lax.axis_size("dp"), lax.axis_size("fsdp")
+    count = dp_size * fsdp_size
+    me = lax.axis_index("dp") * fsdp_size + lax.axis_index("fsdp")
+    greet_all(count, fsdp_size, me)
+    grads = (grad_square, grad_expand, grad_reduce)
+    outs = (square_sum, expand_sum, reduce_sum, spare)
+    feed = Reduction(
+        FEED_KINDS, depth, grads, outs, {EXPAND: work_expand, REDUCE: work_reduce}, feed_buffers, feed_sems
+    )
+    square = Reduction(SQUARE_KINDS, depth, grads, outs, None, square_buffers, square_sems)
+    feed.begin()
+
+    def relay(group):
+        def act():
+            for move, step in group:
+                move(step)
+
+        return act
+
+    feats, half = blocks.shape[1] // 2, blocks.shape[2]
+
+    def put(r, total):
+        each = 384 // feats
+        for p in range(each):
+            part = total[p * feats : (p + 1) * feats]
+            blocks[r * each + p] = jnp.concatenate([part[:, :half], part[:, half:]], axis=0).astype(jnp.bfloat16)
+
+    attend_back_steps(
+        *ins, grad_square, grad_score_ref, grad_gain_ref, *steps,
+        [relay(group) for group in feed.groups()], square.begin, put,
+    )
+
+    def part_copy(k):
+        target = lax.rem(me + k, count)
+        return pltpu.make_async_remote_copy(
+            src_ref=blocks.at[target],
+            dst_ref=returned.at[me],
+            send_sem=part_send.at[k],
+            recv_sem=part_got.at[k],
+            device_id=(target // fsdp_size, lax.rem(target, fsdp_size)),
+            device_id_type=MESH,
+        )
+
+    def start_part(k, carry):
+        part_copy(k).start()
+        return carry
+
+    lax.fori_loop(1, count, start_part, 0)
+    own_part = pltpu.make_async_copy(blocks.at[me], returned.at[me], part_own)
+    own_part.start()
+    for group in square.groups():
+        relay(group)()
+    end_copy = remote(spare, square_sum.at[square.core], end_send, end_got, square.sibling)
+    end_copy.start()
+    feed.finish()
+    square.finish()
+    end_copy.wait_send()
+    remote(spare, square_sum.at[1 - square.core], end_send, end_got, square.sibling).wait_recv()
+    own_part.wait()
+
+    def end_part(k, carry):
+        part_copy(k).wait()
+        return carry
+
+    lax.fori_loop(1, count, end_part, 0)
+
+
+def run_back(ins, grad_expand, grad_reduce, count, feats, call_id):
+    depth = lax.axis_size("dp") // 2
+    tokens = ins[0].shape[0]
+    low = jnp.bfloat16
+    blocks = (count, 2 * feats, tokens // 2)
+    whole = pl.BlockSpec(memory_space=pltpu.VMEM)
+    anywhere = pl.BlockSpec(memory_space=pl.ANY)
+    feed_buffers, feed_sems = reduction_scratch(FEED_KINDS, depth)
+    square_buffers, square_sems = reduction_scratch(SQUARE_KINDS, depth)
+    return pl.pallas_call(
+        functools.partial(back_kernel, depth),
+        out_shape=[
+            jax.ShapeDtypeStruct((2, 5, 48, 192), jnp.float32),
+            jax.ShapeDtypeStruct((96, 768), jnp.float32),
+            jax.ShapeDtypeStruct((192, 384), jnp.float32),
+            jax.ShapeDtypeStruct((HEADS, TILE, TILE), jnp.float32),
+            jax.ShapeDtypeStruct((8, D), jnp.float32),
+            jax.ShapeDtypeStruct(blocks, low),
+        ],
+        in_specs=[whole] * 14 + [anywhere] * 2,
+        out_specs=[whole] * 5 + [anywhere],
+        scratch_shapes=[pltpu.VMEM((5, D, D), low)]
+        + attend_scratch(tokens)
+        + [
+            pltpu.VMEM(blocks, low),
+            pltpu.VMEM((5, 48, 192), jnp.float32),
+            pltpu.VMEM((2 * depth, 2) + BLOCKS[EXPAND], low),
+            pltpu.VMEM((2 * depth, 2) + BLOCKS[REDUCE], low),
+        ]
+        + feed_buffers
+        + feed_sems
+        + square_buffers
+        + square_sems
+        + [
+            pltpu.SemaphoreType.DMA((count,)),
+            pltpu.SemaphoreType.DMA((count,)),
+            pltpu.SemaphoreType.DMA,
+            pltpu.SemaphoreType.DMA,
+            pltpu.SemaphoreType.DMA,
+        ],
+        compiler_params=pltpu.CompilerParams(
+            collective_id=call_id, has_side_effects=True, vmem_limit_bytes=BACK_CAP
+        ),
+        name="back",
+    )(*ins, grad_expand, grad_reduce)
 
 
 def shards(
@@ -1457,22 +1614,14 @@
     (grad_expand, grad_reduce, grad_middle, grad_middle_low, grad_proj, late_gains) = run_feed_back(
         grad_embeds, embeds, inverse, pool, length_rows, square_all, middle, ending, expand_all, reduce_all, gains
     )
-    (grad_square, grad_scores, first_gain, merged) = run_attend_back(
+    back_ins = (
         grad_middle, grad_middle_low, grad_proj, pooled, start, queries, keys_here, values_here, mixed, square_all,
-        gains, bias, mask, rank_rows
-    )
-    grad_gains = jnp.concatenate([first_gain[:1], late_gains[1:3]], axis=0)
-    grad_position = lax.dot_general(
-        onehot, grad_scores.reshape(HEADS, TILE * TILE), (((0,), (1,)), ((), ())), precision=HIGHEST
-    )
-    grad_scale = ((first_dscale + second_dscale) * scale).reshape(1)
-    merged = merged.reshape(count, feats, 2, half).transpose(0, 2, 1, 3)
-    if feats_pad > feats:
-        merged = jnp.pad(merged, ((0, 0), (0, 0), (0, feats_pad - feats), (0, 0)))
-    returned = exchange(merged.reshape(count, 2 * feats_pad, half), False, 4, "send_gradients")
-    grad_table = scatter(returned, row_all, group_all, vocab_size)[:feats]
+        gains, bias, mask, rank_rows,
+    )
     if direct:
-        square_sum, expand_sum, reduce_sum = reduce_blocks(grad_square, grad_expand, grad_reduce, 5)
+        (square_sum, expand_sum, reduce_sum, grad_scores, first_gain, returned) = run_back(
+            back_ins, grad_expand, grad_reduce, count, feats, 5
+        )
         square_sum = square_sum.transpose(1, 0, 2, 3).reshape(5, 96, 192)
     else:
 
@@ -1483,9 +1632,20 @@
             )
             return lax.psum_scatter(part, column_name, scatter_dimension=axis + 1, tiled=True)
 
+        (grad_square, grad_scores, first_gain, merged) = run_attend_back(*back_ins)
         square_sum = shard(grad_square, "dp", "fsdp")
         expand_sum = shard(grad_expand, "dp", "fsdp")
         reduce_sum = shard(grad_reduce, "fsdp", "dp")
+        merged = merged.reshape(count, feats, 2, half).transpose(0, 2, 1, 3)
+        if feats_pad > feats:
+            merged = jnp.pad(merged, ((0, 0), (0, 0), (0, feats_pad - feats), (0, 0)))
+        returned = exchange(merged.reshape(count, 2 * feats_pad, half), False, 4, "send_gradients")
+    grad_table = scatter(returned, row_all, group_all, vocab_size)[:feats]
+    grad_gains = jnp.concatenate([first_gain[:1], late_gains[1:3]], axis=0)
+    grad_position = lax.dot_general(
+        onehot, grad_scores.reshape(HEADS, TILE * TILE), (((0,), (1,)), ((), ())), precision=HIGHEST
+    )
+    grad_scale = ((first_dscale + second_dscale) * scale).reshape(1)
     reduced = (square_sum, expand_sum, reduce_sum.T)
     local_square = (
         jnp.sum(reduced[0] * reduced[0])

time: 598 us -> 551 us (0.921)
  Pallas kernels: 494 us -> 462 us
  local copies, waits for them, and re-layouts: 27.2 us -> 18.4 us
    pallas_call x4 -> x3, Pallas kernels: 95 us -> 53.2 us  [exchange(): pl.pallas_call(functools.partial(exchange_kernel, same), out_shape=jax.Sh...]
    pallas_call x2 -> x1, Pallas kernels: 121 us -> 131 us  [run_back(): pl.pallas_call(functools.partial(back_kernel, depth), out_shape=[jax.Shap...]
    reshape x2 -> x0, local copies, waits for them, and re-layouts: 6.73 us -> none  [shards(): merged = merged.reshape(count, feats, 2, half).transpose(0, 2, 1, 3)]
where the time goes in v4:
time: 551 us; the launch traced here: 545 us
  Pallas kernels  462 us (84%)
  other arithmetic  46.1 us (8%)
  local copies, waits for them, and re-layouts  18.4 us (3%)
  between operations  13.8 us (3%)
    pallas_call x1, Pallas kernels, run_back(): pl.pallas_call(functools.partial(back_kernel, depth), out_shape=[jax.Shap...  131 us
    pallas_call x1, Pallas kernels, run_front(): pl.pallas_call(functools.partial(front_kernel, fold, depth), out_shape=[j...  113 us
    pallas_call x1, Pallas kernels, scatter(): pl.pallas_call(functools.partial(scatter_kernel, fold), grid=(n,), out_sh...  68.4 us
    pallas_call x3, Pallas kernels, exchange(): pl.pallas_call(functools.partial(exchange_kernel, same), out_shape=jax.Sh...  53.2 us
    pallas_call x1, Pallas kernels, run_feed_back(): pl.pallas_call(feed_back_kernel, grid=(1,), out_shape=[jax.ShapeDtypeStru...  52.3 us
    pallas_call x1, Pallas kernels, run_forward(): pl.pallas_call(forward_kernel, out_shape=[flat, flat, flat, flat, flat, f...  44.5 us
    sub x6, other arithmetic, adam_update(): weight - rate * (moment_hat / (jnp.sqrt(second_hat) + ADAM_EPS) + WEIGHT_...  14.6 us

profile of v4, /device:TPU:15, one launch (start us, length us, event | category | flops | bytes accessed | tf_op | source)
XLA Modules:
  0.0 544.6 jit_solution(6508169777240782513)
XLA Ops:
  3.3 1.1 select_reduce_fusion
  5.1 1.3 fusion.20.src
  6.4 13.1 %share_start.1 = f32[32,16,128]{2,1,0:T(8,128)} custom-call(f32[1,16,128]{2,1,0:T(8,128)} %fusion.20.src), custom_call_target="tpu_custom_call" | custom-call | tf_op jit(solution)/shard_map/share_start/pallas_call | solution.py:301
  19.5 1.6 convert_and_fusion
  21.8 3.8 convert_convert_fusion.table_ref
  27.7 112.9 %front.1 = (bf16[32,48,512]{2,1,0:T(8,128)(2,1)}, bf16[5,768,768]{2,1,0:T(8,128)(2,1)}, bf16[768,3072]{1,0:T(8,128)(2,1)}, bf16[768,3072]{1,0:T(8,128)(2,1)}) custom-call(s32[32,1024]{1,0:T(8,128)} %bitcast.89, s32[32,1,1024]{2,1,0:T(1,128)} %bitcast.83, f32[24,32128]{1,0:T(8,128)} %convert_convert_fusion.table_ref, bf16[2,5,48,192]{3,2,1,0:T(8,128)(2,1)} %bitcast.87, ...), custom_call_target="tpu_custom_call" | custom-call | tf_op jit(solution)/shard_map/front/pallas_call | solution.py:615
  140.7 3.0 copy.82
  143.7 1.6 copy.91
  147.0 1.0 broadcast_in_dim.33.rank_ref.refs_13_
  150.3 1.2 fusion.41
  152.7 44.5 %layer_forward.1 = (bf16[1024,768]{1,0:T(8,128)(2,1)}, bf16[1024,768]{1,0:T(8,128)(2,1)}, bf16[1024,768]{1,0:T(8,128)(2,1)}, bf16[1024,768]{1,0:T(8,128)(2,1)}, ...) custom-call(bf16[768,1024]{1,0:T(8,128)(2,1)} %bitcast.76, ...), custom_call_target="tpu_custom_call" | custom-call | tf_op jit(solution)/shard_map/layer_forward/pallas_call | solution.py:1064
  197.2 24.8 %share_embeds.1 = bf16[32,16,768]{2,1,0:T(8,128)(2,1)} custom-call(bf16[1,16,768]{2,1,0:T(8,128)(2,1)} %bitcast.91), custom_call_target="tpu_custom_call" | custom-call | tf_op jit(solution)/shard_map/share_embeds/pallas_call | solution.py:301
  222.0 1.2 fusion.39
  224.9 1.4 fusion.38
  226.6 1.0 convert_reduce_fusion.1
  228.3 1.9 pad_maximum_fusion.1
  233.6 1.3 concatenate.58.grad_embed_ref
  234.9 52.3 %feed_backward.1 = (bf16[768,3072]{1,0:T(8,128)(2,1)}, bf16[768,3072]{1,0:T(8,128)(2,1)}, f32[1024,768]{1,0:T(8,128)}, bf16[1024,768]{1,0:T(8,128)(2,1)}, bf16[16,768]{1,0:T(8,128)(2,1)}, /*index=5*/f32[8,768]{1,0:T(8,128)}) custom-call(f32[16,768]{1,0:T(8,128)} %concatenate.58.grad_embed_ref, f32[16,768]{1,0:T(8,128)} %get-tuple-element.55.embed_ref, ...), custom_call_target="tpu_custom_call" | custom-call | tf_op jit(solution)/shard_map/feed_backward/pallas_call | solution.py:1154
  287.2 130.8 %back.1 = (f32[2,5,48,192]{3,2,1,0:T(8,128)}, f32[96,768]{1,0:T(8,128)}, f32[192,384]{1,0:T(8,128)}, f32[12,128,128]{2,1,0:T(8,128)}, f32[8,768]{1,0:T(8,128)}, /*index=5*/bf16[32,48,512]{2,1,0:T(8,128)(2,1)}) custom-call(f32[1024,768]{1,0:T(8,128)} %get-tuple-element.59.refs_0_, bf16[1024,768]{1,0:T(8,128)(2,1)} %get-tuple-element.60.refs_1_, ...), custom_call_target="tpu_custom_call" | custom-call | tf_op jit(solution)/shard_map/back/pallas_call | solution.py:1411
  419.5 1.8 multiply_reduce_fusion.1
  421.3 1.6 multiply_reduce_fusion.3
  424.2 1.6 multiply_reduce_fusion.2
  426.5 68.4 %scatter.1 = f32[24,32128]{1,0:T(8,128)} custom-call(s32[32,1,1024]{2,1,0:T(1,128)} %bitcast.86, s32[32,1,1024]{2,1,0:T(1,128)} %bitcast.84, bf16[32,48,512]{2,1,0:T(8,128)(2,1)} %get-tuple-element.70.grad_ref), custom_call_target="tpu_custom_call" | custom-call | tf_op jit(solution)/shard_map/scatter/pallas_call | solution.py:215
  494.9 3.4 multiply_reduce_fusion
  498.9 1.2 pad.50
  500.9 1.8 fusion.42
  503.4 15.3 %share_small.1 = f32[32,24,128]{2,1,0:T(8,128)} custom-call(f32[1,24,128]{2,1,0:T(8,128)} %fusion.18.src), custom_call_target="tpu_custom_call" | custom-call | tf_op jit(solution)/shard_map/share_small/pallas_call | solution.py:301
  518.7 1.0 reduce_sum.165
  526.5 2.3 multiply_subtract_fusion.2
  528.8 2.2 multiply_subtract_fusion.3
  531.1 2.5 multiply_subtract_fusion.1
  533.6 6.3 %multiply_subtract_fusion = (f32[24,32128]{1,0:T(8,128)}, f32[24,32128]{1,0:T(8,128)}, f32[24,32128]{1,0:T(8,128)}) fusion(f32[24,32128]{1,0:T(8,128)S(1)} %copy-done.1, f32[24,32128]{1,0:T(8,128)S(1)} %copy-done, f32[]{:T(128)S(6)} %min.3, f32[24,32128]{1,0:T(8,128)S(1)} %copy-done.4, f32[24,32128]{1,0:T(8,128)} %param.39), kind=kLoop, calls=%fused_computation.9 | loop fusion | flops 12337152 | bytes 21590020 | tf_op jit(solution)/shard_map/sub | solution.py:80
  (109 shorter events, 21.6 us)
Async XLA Ops:
  21.1 4.5 copy-start.10
  21.8 3.8 copy-start.6
  21.8 4.6 copy-start.7
  21.8 5.2 copy-start.8
  140.6 7.3 %copy-start.22 = (s32[4]{0:T(128)S(1)}, s32[4]{0:T(128)}, u32[]{:S(2)}) copy-start(s32[4]{0:T(128)} %param.56) | copy-start | bytes 52
  140.7 7.3 %copy-start.23 = (s32[4]{0:T(128)S(1)}, s32[4]{0:T(128)}, u32[]{:S(2)}) copy-start(s32[4]{0:T(128)} %param.55) | copy-start | bytes 52
  140.7 7.4 %copy-start.15 = (pred[16,1024]{1,0:T(8,128)(4,1)S(1)}, pred[16,1024]{1,0:T(8,128)(4,1)}, u32[]{:S(2)}) copy-start(pred[16,1024]{1,0:T(8,128)(4,1)} %constant.89.clone) | copy-start | bytes 49156
  140.7 7.4 %copy-start.19 = (s32[1024]{0:T(1024)S(1)}, s32[1024]{0:T(1024)}, u32[]{:S(2)}) copy-start(s32[1024]{0:T(1024)} %constant.203) | copy-start | bytes 12292
  140.7 8.1 %copy-start.13 = (pred[8,128,128]{2,1,0:T(32,128)(4,1)S(1)}, pred[8,128,128]{2,1,0:T(32,128)(4,1)}, u32[]{:S(2)}) copy-start(pred[8,128,128]{2,1,0:T(32,128)(4,1)} %constant.90.clone) | copy-start | bytes 393220
  143.7 6.6 %copy-start.2 = (f32[16384,32]{0,1:T(8,128)S(1)}, f32[16384,32]{0,1:T(8,128)}, u32[]{:S(2)}) copy-start(f32[16384,32]{0,1:T(8,128)} %constant.91.clone) | copy-start | bytes 6291460
  143.7 6.6 %copy-start.14 = (f32[32,12]{0,1:T(8,128)S(1)}, f32[32,12]{0,1:T(8,128)}, u32[]{:S(2)}) copy-start(f32[32,12]{0,1:T(8,128)} %param.37) | copy-start | bytes 4612
  494.9 6.0 %copy-start.3 = (f32[16384,32]{0,1:T(8,128)S(1)}, f32[16384,32]{0,1:T(8,128)}, u32[]{:S(2)}) copy-start(f32[16384,32]{0,1:T(8,128)} %constant.91.clone) | copy-start | bytes 6291460
  500.2 24.9 %copy-start.16 = (f32[32,12]{0,1:T(8,128)S(1)}, f32[32,12]{0,1:T(8,128)}, u32[]{:S(2)}) copy-start(f32[32,12]{0,1:T(8,128)} %param.50) | copy-start | bytes 4612
  500.2 24.9 %copy-start.17 = (f32[32,12]{0,1:T(8,128)S(1)}, f32[32,12]{0,1:T(8,128)}, u32[]{:S(2)}) copy-start(f32[32,12]{0,1:T(8,128)} %param.49) | copy-start | bytes 4612
  500.2 25.6 %copy-start.18 = (f32[3,24]{1,0:T(4,128)S(1)}, f32[3,24]{1,0:T(4,128)}, u32[]{:S(2)}) copy-start(f32[3,24]{1,0:T(4,128)} %param.36) | copy-start | bytes 868
  500.2 25.6 %copy-start.20 = (f32[3,24]{1,0:T(4,128)S(1)}, f32[3,24]{1,0:T(4,128)}, u32[]{:S(2)}) copy-start(f32[3,24]{1,0:T(4,128)} %param.48) | copy-start | bytes 868
  500.2 25.6 %copy-start.21 = (f32[3,24]{1,0:T(4,128)S(1)}, f32[3,24]{1,0:T(4,128)}, u32[]{:S(2)}) copy-start(f32[3,24]{1,0:T(4,128)} %param.47) | copy-start | bytes 868
  500.9 28.0 %copy-start.9 = (f32[96,768]{1,0:T(8,128)S(1)}, f32[96,768]{1,0:T(8,128)}, u32[]{:S(2)}) copy-start(f32[96,768]{1,0:T(8,128)} %get-tuple-element.75) | copy-start | bytes 884740
  502.6 26.2 %copy-start.12 = (f32[96,768]{1,0:T(8,128)S(1)}, f32[96,768]{1,0:T(8,128)}, u32[]{:S(2)}) copy-start(f32[96,768]{1,0:T(8,128)} %param.44) | copy-start | bytes 884740
  502.7 28.3 %copy-start.5 = (f32[2,5,48,192]{3,2,1,0:T(8,128)S(1)}, f32[2,5,48,192]{3,2,1,0:T(8,128)}, u32[]{:S(2)}) copy-start(f32[2,5,48,192]{3,2,1,0:T(8,128)} %get-tuple-element.74) | copy-start | bytes 1105924
  524.1 7.0 %copy-start.11 = (f32[5,96,192]{2,1,0:T(8,128)S(1)}, f32[5,96,192]{2,1,0:T(8,128)}, u32[]{:S(2)}) copy-start(f32[5,96,192]{2,1,0:T(8,128)} %param.42) | copy-start | bytes 1105924
  526.5 7.2 %copy-start.4 = (f32[24,32128]{1,0:T(8,128)S(1)}, f32[24,32128]{1,0:T(8,128)}, u32[]{:S(2)}) copy-start(f32[24,32128]{1,0:T(8,128)} %param.40) | copy-start | bytes 9252868
  528.8 4.8 copy-start.1
  531.0 2.6 copy-start

commit v5 on v4

--- a/solution.py
+++ b/solution.py
@@ -110,7 +110,7 @@
             start = jnp.minimum(j * fold + b * LANES, vocab - LANES)
             start = pl.multiple_of(start, LANES)
             parts += [table_ref[:, pl.ds(start, LANES)], pad]
-        tile = jnp.concatenate(parts, axis=0)
+        tile = jnp.concatenate(parts, axis=0).astype(jnp.bfloat16).astype(jnp.float32)
         turned[pl.ds(pl.multiple_of(b * LANES, LANES), LANES), :] = tile.T
         return carry
 
@@ -118,24 +118,28 @@
     turned[pl.ds(fold, 8), :] = jnp.zeros((8, LANES), jnp.float32)
 
 
-def look_up(row_ref, group_ref, source, turned, rows, feats):
+def pick_group(rows, group, feats):
     tokens = rows.shape[0]
-    batch = 32
-
-    def fetch(b, carry):
-        for k in range(batch):
-            t = b * batch + k
-            rows[pl.ds(t, 1), :] = turned[pl.ds(row_ref[source, t], 1), :]
-        return carry
-
-    lax.fori_loop(0, tokens // batch, fetch, 0)
     wide = dot_nt(eye(), rows[...].astype(jnp.bfloat16))
-    group = group_ref[source]
     total = jnp.where(group == 0, wide[:SLOT], 0.0)
     for j in range(1, GROUPS):
         total = total + jnp.where(group == j, wide[j * SLOT : (j + 1) * SLOT], 0.0)
     half = tokens // 2
     return jnp.concatenate([total[:feats, :half], total[:feats, half:]], axis=0).astype(jnp.bfloat16)
+
+
+def look_up(row_ref, group_ref, source, turned, rows, feats):
+    tokens = rows.shape[0]
+    batch = 32
+
+    def fetch(b, carry):
+        for k in range(batch):
+            t = b * batch + k
+            rows[pl.ds(t, 1), :] = turned[pl.ds(row_ref[source, t], 1), :]
+        return carry
+
+    lax.fori_loop(0, tokens // batch, fetch, 0)
+    return pick_group(rows, group_ref[source], feats)
 
 
 def lookup_kernel(fold, row_ref, group_ref, table_ref, out_ref, turned, rows):
@@ -413,187 +417,275 @@
         device_id=target, device_id_type=MESH)
 
 
-def front_kernel(fold, depth, row_ref, group_ref, table_ref, square_in, expand_in, reduce_in, *refs):
-    mine = (square_in, expand_in, reduce_in)
-    found, outs = refs[0], refs[1 : 1 + KINDS]
-    theirs, own, turned, rows, blocks = refs[1 + KINDS : 6 + KINDS]
-    (
-        pair_send, pair_recv, own_sem, send, got, sib_send, sib_got, diag_got, part_send, part_got, part_own
-    ) = refs[6 + KINDS :]
+class Gather:
+    def __init__(self, kinds, depth, sources, outs, sems):
+        self.kinds, self.depth, self.sources, self.outs = kinds, depth, sources, outs
+        self.own_sem, self.send, self.got, self.sib_send, self.sib_got, self.diag_got = sems
+        self.number = {a: n for n, a in enumerate(kinds)}
+        z, x, y, core = place()
+        self.z, self.x, self.y, self.core = z, x, y, core
+        self.sibling = device_at(z, x, y, 1 - core)
+        self.x_next, self.y_next = device_at(z, 1 - x, y, core), device_at(z, x, 1 - y, core)
+
+    def to(self, way, a, z_at, x_at, y_at, target, part=None, src=None):
+        n, k = self.number[a], (z_at * 2 + x_at) * 2 + y_at
+        if part is None:
+            spot_at, recv = spot(self.outs, a, z_at, x_at, y_at, self.core), self.got.at[n, k]
+        else:
+            spot_at = spot_part(self.outs, a, z_at, x_at, y_at, self.core, part)
+            recv = self.diag_got.at[n, z_at, part]
+        return remote(spot_at if src is None else src, spot_at, self.send.at[way, n, k], recv, target)
+
+    def to_sibling(self, a, z_at, x_at, y_at, src=None, core=None):
+        spot_at = spot(self.outs, a, z_at, x_at, y_at, self.core if core is None else core)
+        n, k = self.number[a], (z_at * 2 + x_at) * 2 + y_at
+        return remote(
+            spot_at if src is None else src, spot_at, self.sib_send.at[n, k], self.sib_got.at[n, k], self.sibling
+        )
+
+    def own_copy(self, a):
+        return pltpu.make_async_copy(
+            self.sources[a], spot(self.outs, a, self.z, self.x, self.y, self.core), self.own_sem.at[self.number[a]]
+        )
+
+    def begin(self):
+        z, x, y, core = self.z, self.x, self.y, self.core
+        for a in self.kinds:
+            source = self.sources[a]
+            self.own_copy(a).start()
+
+            @pl.when(z < self.depth - 1)
+            def _():
+                self.to(0, a, z, x, y, device_at(z + 1, x, y, core), src=source).start()
+
+            @pl.when(z > 0)
+            def _():
+                self.to(1, a, z, x, y, device_at(z - 1, x, y, core), src=source).start()
+
+            self.to(2, a, z, x, y, self.x_next, src=source).start()
+            self.to(3, a, z, x, y, self.y_next, src=source).start()
+            self.to_sibling(a, z, x, y, src=source).start()
+
+    def sides(self, step, act):
+        if step == 0:
+            act(self.z)
+            return
+        for sign in (1, -1):
+            z_at = self.z + sign * step
+
+            @pl.when((z_at >= 0) & (z_at < self.depth))
+            def _():
+                act(z_at)
+
+    def first(self, step):
+        z, x, y, core = self.z, self.x, self.y, self.core
+
+        def act(z_at):
+            for a in self.kinds:
+                self.to(0, a, z_at, x, y, self.sibling).wait_recv()
+
+                @pl.when((z_at < z) & (z < self.depth - 1))
+                def _():
+                    self.to(0, a, z_at, x, y, device_at(z + 1, x, y, core)).start()
+
+                @pl.when((z_at > z) & (z > 0))
+                def _():
+                    self.to(1, a, z_at, x, y, device_at(z - 1, x, y, core)).start()
+
+                self.to(2, a, z_at, x, y, self.x_next).start()
+                self.to(3, a, z_at, x, y, self.y_next).start()
+                self.to_sibling(a, z_at, x, y).start()
+
+        self.sides(step, act)
+
+    def second(self, step):
+        x, y = self.x, self.y
+
+        def act(z_at):
+            for a in self.kinds:
+                self.to(0, a, z_at, 1 - x, y, self.sibling).wait_recv()
+                self.to(3, a, z_at, 1 - x, y, self.y_next, 0).start()
+                self.to_sibling(a, z_at, 1 - x, y).start()
+                self.to(0, a, z_at, x, 1 - y, self.sibling).wait_recv()
+                self.to(2, a, z_at, x, 1 - y, self.x_next, 1).start()
+                self.to_sibling(a, z_at, x, 1 - y).start()
+
+        self.sides(step, act)
+
+    def third(self, step):
+        x, y = self.x, self.y
+
+        def act(z_at):
+            for a in self.kinds:
+                for part in range(2):
+                    self.to(0, a, z_at, 1 - x, 1 - y, self.sibling, part).wait_recv()
+                self.to_sibling(a, z_at, 1 - x, 1 - y).start()
+
+        self.sides(step, act)
+
+    def relays(self):
+        for step in range(1, self.depth + 2):
+            if step < self.depth:
+                yield functools.partial(self.first, step)
+            if 0 <= step - 1 < self.depth:
+                yield functools.partial(self.second, step - 1)
+            if 0 <= step - 2 < self.depth:
+                yield functools.partial(self.third, step - 2)
+
+    def arrive(self):
+        for a in self.kinds:
+            self.own_copy(a).wait()
+
+        def wait(z_at, carry):
+            for a in self.kinds:
+                for x_at in range(2):
+                    for y_at in range(2):
+                        self.to_sibling(a, z_at, x_at, y_at, core=1 - self.core).wait_recv()
+            return carry
+
+        lax.fori_loop(0, self.depth, wait, 0)
+
+    def finish(self):
+        z, x, y = self.z, self.x, self.y
+
+        def wait(z_at, carry):
+            for a in self.kinds:
+
+                @pl.when((z_at <= z) & (z < self.depth - 1))
+                def _():
+                    self.to(0, a, z_at, x, y, self.x_next).wait_send()
+
+                @pl.when((z_at >= z) & (z > 0))
+                def _():
+                    self.to(1, a, z_at, x, y, self.x_next).wait_send()
+
+                self.to(2, a, z_at, x, y, self.x_next).wait_send()
+                self.to(3, a, z_at, x, y, self.y_next).wait_send()
+                self.to(3, a, z_at, 1 - x, y, self.y_next, 0).wait_send()
+                self.to(2, a, z_at, x, 1 - y, self.x_next, 1).wait_send()
+                for x_at in range(2):
+                    for y_at in range(2):
+                        self.to_sibling(a, z_at, x_at, y_at).wait_send()
+            return carry
+
+        lax.fori_loop(0, self.depth, wait, 0)
+
+
+def gather_sems(kinds, depth):
+    count, spots = len(kinds), 4 * depth
+    return [
+        pltpu.SemaphoreType.DMA((count,)),
+        pltpu.SemaphoreType.DMA((4, count, spots)),
+        pltpu.SemaphoreType.DMA((count, spots)),
+        pltpu.SemaphoreType.DMA((count, spots)),
+        pltpu.SemaphoreType.DMA((count, spots)),
+        pltpu.SemaphoreType.DMA((count, depth, 2)),
+    ]
+
+
+FEED_KINDS = (EXPAND, REDUCE)
+SQUARE_KINDS = (SQUARE,)
+
+
+def front_kernel(fold, depth, keys_ref, gains_ref, table_ref, square_in, *refs):
+    found, square_out, keys_all, gains_all = refs[:4]
+    theirs, own, turned, rows, blocks, row_low, row_all = refs[4:11]
+    gather_sem, refs = refs[11:17], refs[17:]
+    pair_send, pair_recv, part_send, part_got, part_own, keys_send, keys_got, gains_send, gains_got, near_sem = refs
     dp_size, fsdp_size = lax.axis_size("dp"), lax.axis_size("fsdp")
     count = dp_size * fsdp_size
     me = lax.axis_index("dp") * fsdp_size + lax.axis_index("fsdp")
     z, x, y, core = place()
     sibling = device_at(z, x, y, 1 - core)
-    x_next, y_next = device_at(z, 1 - x, y, core), device_at(z, x, 1 - y, core)
     greet_all(count, fsdp_size, me)
-    pair = remote(mine[SQUARE].at[1 - core], theirs, pair_send, pair_recv, sibling)
+
+    def info_copies(k):
+        target = lax.rem(me + k, count)
+        device = (target // fsdp_size, lax.rem(target, fsdp_size))
+        return (
+            remote(keys_ref, keys_all.at[me], keys_send.at[k], keys_got.at[k], device),
+            remote(gains_ref, gains_all.at[me], gains_send.at[k], gains_got.at[k], device),
+        )
+
+    def start_info(k, carry):
+        for copy in info_copies(k):
+            copy.start()
+        return carry
+
+    lax.fori_loop(1, count, start_info, 0)
+    keys_all[me] = keys_ref[...]
+    gains_all[me] = gains_ref[...]
+    pair = remote(square_in.at[1 - core], theirs, pair_send, pair_recv, sibling)
     pair.start()
-
-    def number(z_at, x_at, y_at):
-        return (z_at * 2 + x_at) * 2 + y_at
-
-    def to(way, a, z_at, x_at, y_at, target, part=None, src=None):
-        k = number(z_at, x_at, y_at)
-        if part is None:
-            spot_at, recv = spot(outs, a, z_at, x_at, y_at, core), got.at[a, k]
-        else:
-            spot_at = spot_part(outs, a, z_at, x_at, y_at, core, part)
-            recv = diag_got.at[a, z_at, part]
-        return remote(spot_at if src is None else src, spot_at, send.at[way, a, k], recv, target)
-
-    def to_sibling(a, z_at, x_at, y_at, src=None):
-        spot_at = spot(outs, a, z_at, x_at, y_at, core)
-        k = number(z_at, x_at, y_at)
-        return remote(spot_at if src is None else src, spot_at, sib_send.at[a, k], sib_got.at[a, k], sibling)
-
-    def from_sibling(a, z_at, x_at, y_at):
-        spot_at = spot(outs, a, z_at, x_at, y_at, 1 - core)
-        k = number(z_at, x_at, y_at)
-        return remote(spot_at, spot_at, sib_send.at[a, k], sib_got.at[a, k], sibling)
-
-    UP, DOWN, ACROSS_X, ACROSS_Y = range(4)
-    sources = [own, mine[EXPAND], mine[REDUCE]]
-    for a in (EXPAND, REDUCE, SQUARE):
-        if a == SQUARE:
-            row = lax.broadcasted_iota(jnp.int32, (192, 384), 0)
-            col = lax.broadcasted_iota(jnp.int32, (192, 384), 1)
-            here = (row + core * 192 == col).astype(jnp.float32).astype(jnp.bfloat16)
-            there = (row + (1 - core) * 192 == col).astype(jnp.float32).astype(jnp.bfloat16)
-            pair.wait_recv()
-            for k in range(5):
-                block = jnp.dot(mine[a][core, k], here, preferred_element_type=jnp.float32) + jnp.dot(
-                    theirs[k], there, preferred_element_type=jnp.float32
-                )
-                own[k] = block.astype(jnp.bfloat16)
-        pltpu.make_async_copy(sources[a], spot(outs, a, z, x, y, core), own_sem.at[a]).start()
-
-        @pl.when(z < depth - 1)
-        def _():
-            to(UP, a, z, x, y, device_at(z + 1, x, y, core), src=sources[a]).start()
-
-        @pl.when(z > 0)
-        def _():
-            to(DOWN, a, z, x, y, device_at(z - 1, x, y, core), src=sources[a]).start()
-
-        to(ACROSS_X, a, z, x, y, x_next, src=sources[a]).start()
-        to(ACROSS_Y, a, z, x, y, y_next, src=sources[a]).start()
-        to_sibling(a, z, x, y, src=sources[a]).start()
-
-    def sides(step, act):
-        if step == 0:
-            act(z)
-            return
-        for sign in (1, -1):
-            z_at = z + sign * step
-
-            @pl.when((z_at >= 0) & (z_at < depth))
-            def _():
-                act(z_at)
-
-    def first(step):
-        def act(z_at):
-            for a in range(KINDS):
-                to(UP, a, z_at, x, y, sibling).wait_recv()
-
-                @pl.when((z_at < z) & (z < depth - 1))
-                def _():
-                    to(UP, a, z_at, x, y, device_at(z + 1, x, y, core)).start()
-
-                @pl.when((z_at > z) & (z > 0))
-                def _():
-                    to(DOWN, a, z_at, x, y, device_at(z - 1, x, y, core)).start()
-
-                to(ACROSS_X, a, z_at, x, y, x_next).start()
-                to(ACROSS_Y, a, z_at, x, y, y_next).start()
-                to_sibling(a, z_at, x, y).start()
-
-        sides(step, act)
-
-    def second(step):
-        def act(z_at):
-            for a in range(KINDS):
-                to(UP, a, z_at, 1 - x, y, sibling).wait_recv()
-                to(ACROSS_Y, a, z_at, 1 - x, y, y_next, 0).start()
-                to_sibling(a, z_at, 1 - x, y).start()
-                to(UP, a, z_at, x, 1 - y, sibling).wait_recv()
-                to(ACROSS_X, a, z_at, x, 1 - y, x_next, 1).start()
-                to_sibling(a, z_at, x, 1 - y).start()
-
-        sides(step, act)
-
-    def third(step):
-        def act(z_at):
-            for a in range(KINDS):
-                for part in range(2):
-                    to(UP, a, z_at, 1 - x, 1 - y, sibling, part).wait_recv()
-                to_sibling(a, z_at, 1 - x, 1 - y).start()
-
-        sides(step, act)
-
+    gather = Gather(SQUARE_KINDS, depth, {SQUARE: own}, {SQUARE: square_out}, gather_sem)
+    row = lax.broadcasted_iota(jnp.int32, (192, 384), 0)
+    col = lax.broadcasted_iota(jnp.int32, (192, 384), 1)
+    here = (row + core * 192 == col).astype(jnp.float32).astype(jnp.bfloat16)
+    there = (row + (1 - core) * 192 == col).astype(jnp.float32).astype(jnp.bfloat16)
+    pair.wait_recv()
+    for k in range(5):
+        block = jnp.dot(square_in[core, k], here, preferred_element_type=jnp.float32) + jnp.dot(
+            theirs[k], there, preferred_element_type=jnp.float32
+        )
+        own[k] = block.astype(jnp.bfloat16)
+    gather.begin()
     turn_table(fold, table_ref, turned)
+
+    def end_info(k, carry):
+        for copy in info_copies(k):
+            copy.wait()
+        return carry
+
+    lax.fori_loop(1, count, end_info, 0)
+    key_rows = row_low.shape[0] // count
+
+    def split_row(k, carry):
+        row_low[pl.ds(pl.multiple_of(k * key_rows, 8), key_rows)] = keys_all[k, :key_rows] >> 2
+        return carry
+
+    lax.fori_loop(0, count, split_row, 0)
+    near = pltpu.make_async_copy(row_low, row_all, near_sem)
+    near.start()
+    near.wait()
+
+    def find(target):
+        keys = keys_all[target]
+        group = jnp.concatenate([keys[r : r + 1] for r in range(key_rows)], axis=1) & 3
+
+        def fetch(r, carry):
+            line = target * key_rows + r
+            start = pl.multiple_of(r * LANES, LANES)
+            for k in range(LANES):
+                rows[pl.ds(start + k, 1), :] = turned[pl.ds(row_all[line, k], 1), :]
+            return carry
+
+        lax.fori_loop(0, key_rows, fetch, 0)
+        return pick_group(rows, group, table_ref.shape[0])
 
     def part_copy(k):
         target = lax.rem(me + k, count)
-        return pltpu.make_async_remote_copy(
-            src_ref=blocks.at[target],
-            dst_ref=found.at[me],
-            send_sem=part_send.at[k],
-            recv_sem=part_got.at[k],
-            device_id=(target // fsdp_size, lax.rem(target, fsdp_size)),
-            device_id_type=MESH,
-        )
+        device = (target // fsdp_size, lax.rem(target, fsdp_size))
+        return remote(blocks.at[target], found.at[me], part_send.at[k], part_got.at[k], device)
 
     def serve(k, carry):
         target = lax.rem(me + k, count)
-        blocks[target] = look_up(row_ref, group_ref, target, turned, rows, table_ref.shape[0])
+        blocks[target] = find(target)
         part_copy(k).start()
         return carry
 
-    relays = []
-    for step in range(1, depth + 2):
-        if step < depth:
-            relays.append((first, step))
-        if 0 <= step - 1 < depth:
-            relays.append((second, step - 1))
-        if 0 <= step - 2 < depth:
-            relays.append((third, step - 2))
+    relays = list(gather.relays())
     done = 1
-    for n, (relay, step) in enumerate(relays):
-        until = min(count, 1 + ((n + 1) * count) // len(relays)) if n < len(relays) - 1 else count
+    for n, relay in enumerate(relays):
+        until = 1 + ((n + 1) * (count - 1)) // len(relays)
         lax.fori_loop(done, until, serve, 0)
         done = until
-        relay(step)
-    blocks[me] = look_up(row_ref, group_ref, me, turned, rows, table_ref.shape[0])
+        relay()
+    blocks[me] = find(me)
     own_part = pltpu.make_async_copy(blocks.at[me], found.at[me], part_own)
     own_part.start()
-
     pair.wait_send()
-    for a in range(KINDS):
-        pltpu.make_async_copy(sources[a], spot(outs, a, z, x, y, core), own_sem.at[a]).wait()
-
-    def finish(z_at, carry):
-        for a in range(KINDS):
-
-            @pl.when((z_at <= z) & (z < depth - 1))
-            def _():
-                to(UP, a, z_at, x, y, x_next).wait_send()
-
-            @pl.when((z_at >= z) & (z > 0))
-            def _():
-                to(DOWN, a, z_at, x, y, x_next).wait_send()
-
-            to(ACROSS_X, a, z_at, x, y, x_next).wait_send()
-            to(ACROSS_Y, a, z_at, x, y, y_next).wait_send()
-            to(ACROSS_Y, a, z_at, 1 - x, y, y_next, 0).wait_send()
-            to(ACROSS_X, a, z_at, x, 1 - y, x_next, 1).wait_send()
-            for x_at in range(2):
-                for y_at in range(2):
-                    to_sibling(a, z_at, x_at, y_at).wait_send()
-                    from_sibling(a, z_at, x_at, y_at).wait_recv()
-        return carry
-
-    lax.fori_loop(0, depth, finish, 0)
+    gather.arrive()
+    gather.finish()
     own_part.wait()
 
     def end_part(k, carry):
@@ -603,48 +695,44 @@
     lax.fori_loop(1, count, end_part, 0)
 
 
-def run_front(row_all, group_all, table, square, expand, reduce_turned, call_id):
+def run_front(keys, gains, tokens, table, square, call_id):
     depth = lax.axis_size("dp") // 2
-    spots = 4 * depth
-    count, tokens = row_all.shape
+    count = lax.axis_size("dp") * lax.axis_size("fsdp")
     feats, vocab = table.shape
     fold = fold_rows(vocab)
     blocks = (count, 2 * feats, tokens // 2)
     whole = pl.BlockSpec(memory_space=pltpu.VMEM)
     anywhere = pl.BlockSpec(memory_space=pl.ANY)
+    many = pltpu.SemaphoreType.DMA((count,))
     return pl.pallas_call(
         functools.partial(front_kernel, fold, depth),
         out_shape=[
             jax.ShapeDtypeStruct(blocks, jnp.bfloat16),
             jax.ShapeDtypeStruct((5, 768, 768), jnp.bfloat16),
-            jax.ShapeDtypeStruct((768, 3072), jnp.bfloat16),
-            jax.ShapeDtypeStruct((768, 3072), jnp.bfloat16),
+            jax.ShapeDtypeStruct((count,) + keys.shape, keys.dtype),
+            jax.ShapeDtypeStruct((count,) + gains.shape, gains.dtype),
         ],
-        in_specs=[pl.BlockSpec(memory_space=pltpu.SMEM)] + [whole] * 5,
-        out_specs=[anywhere] * 4,
+        in_specs=[whole] * 4,
+        out_specs=[anywhere] * 2 + [whole] * 2,
         scratch_shapes=[
             pltpu.VMEM((5, 48, 192), jnp.bfloat16),
             pltpu.VMEM((5, 48, 384), jnp.bfloat16),
             pltpu.VMEM((fold + 8, LANES), jnp.float32),
             pltpu.VMEM((tokens, LANES), jnp.float32),
             pltpu.VMEM(blocks, jnp.bfloat16),
-            pltpu.SemaphoreType.DMA,
-            pltpu.SemaphoreType.DMA,
-            pltpu.SemaphoreType.DMA((KINDS,)),
-            pltpu.SemaphoreType.DMA((4, KINDS, spots)),
-            pltpu.SemaphoreType.DMA((KINDS, spots)),
-            pltpu.SemaphoreType.DMA((KINDS, spots)),
-            pltpu.SemaphoreType.DMA((KINDS, spots)),
-            pltpu.SemaphoreType.DMA((KINDS, depth, 2)),
-            pltpu.SemaphoreType.DMA((count,)),
-            pltpu.SemaphoreType.DMA((count,)),
-            pltpu.SemaphoreType.DMA,
-        ],
+            pltpu.VMEM((count * tokens // LANES, LANES), jnp.int32),
+            pltpu.SMEM((count * tokens // LANES, LANES), jnp.int32),
+        ]
+        + gather_sems(SQUARE_KINDS, depth)
+        + [pltpu.SemaphoreType.DMA, pltpu.SemaphoreType.DMA]
+        + [many, many, pltpu.SemaphoreType.DMA]
+        + [many] * 4
+        + [pltpu.SemaphoreType.DMA],
         compiler_params=pltpu.CompilerParams(
             collective_id=call_id, has_side_effects=True, vmem_limit_bytes=VMEM_CAP
         ),
         name="front",
-    )(row_all, group_all.reshape(count, 1, tokens), table, square, expand, reduce_turned)
+    )(keys, gains, table, square)
 
 
 class Reduction:
@@ -973,22 +1061,40 @@
     return jnp.tanh(inner)
 
 
-def forward_kernel(
-    found_ref, rank_ref, square_ref, expand_ref, reduce_ref, gains_ref, bias_ref, mask_ref, pool_ref, length_ref,
+def forward_steps(
+    found_ref, rank_ref, square_ref, gains_ref, bias_ref, mask_ref, pool_ref, length_ref,
     start_ref, query_ref, key_ref, value_ref, mixed_ref, middle_ref, ending_ref, low_ref, pooled_ref, embed_ref,
-    inverse_ref, normed, pooled_sum,
+    inverse_ref, normed, pooled_sum, wide_found, low_found, expand_ref, reduce_ref, between, before_feed,
 ):
+    between = list(between)
+
+    def relay(count):
+        for _ in range(min(count, len(between))):
+            between.pop(0)()
+
     tokens = start_ref.shape[0]
     big = 512
+    feats, half = found_ref.shape[1] // 2, found_ref.shape[2]
+
+    def assemble(p, carry):
+        block = found_ref[p].astype(jnp.float32)
+        at = pl.ds(pl.multiple_of(p * feats, 8), feats)
+        wide_found[at, :half] = block[:feats]
+        wide_found[at, half:] = block[feats:]
+        return carry
+
+    lax.fori_loop(0, found_ref.shape[0], assemble, 0)
+    low_found[...] = wide_found[...].astype(jnp.bfloat16)
 
     def begin(r, carry):
         rows = rows_at(r, 256)
-        start = dot_nt(hot_rows(rank_ref, rows, tokens), found_ref[...])
+        start = dot_nt(hot_rows(rank_ref, rows, tokens), low_found[...])
         start_ref[rows, :] = start.astype(jnp.bfloat16)
         normed[rows, :] = norm_rows(start, gains_ref[0:1]).astype(jnp.bfloat16)
         return carry
 
     lax.fori_loop(0, tokens // 256, begin, 0)
+    relay(1)
     for k, target in enumerate((query_ref, key_ref, value_ref)):
 
         def project(r, carry):
@@ -997,6 +1103,7 @@
             return carry
 
         lax.fori_loop(0, tokens // big, project, 0)
+        relay(1)
 
     def attend(t, carry):
         rows = rows_at(t, TILE)
@@ -1008,7 +1115,13 @@
             mixed_ref[rows, lanes] = mixed.astype(jnp.bfloat16)
         return carry
 
-    lax.fori_loop(0, tokens // TILE, attend, 0)
+    tiles = tokens // TILE
+    if between:
+        for t in range(tiles):
+            lax.fori_loop(t, t + 1, attend, 0)
+            relay(1)
+    else:
+        lax.fori_loop(0, tiles, attend, 0)
 
     def merge(r, carry):
         rows = rows_at(r, big)
@@ -1019,6 +1132,8 @@
         return carry
 
     lax.fori_loop(0, tokens // big, merge, 0)
+    relay(len(between))
+    before_feed()
     wide = expand_ref.shape[1]
 
     def feed(c, carry):
@@ -1055,25 +1170,91 @@
     inverse_ref[...] = jnp.broadcast_to(inverse, inverse_ref.shape)
 
 
-def run_forward(found, rank, square, expand, reduce_turned, gains, bias, mask, pool, lengths):
-    tokens = found.shape[1]
-    seqs = pool.shape[0]
-    low = jnp.bfloat16
-    flat = jax.ShapeDtypeStruct((tokens, D), low)
+def forward_kernel(*refs):
+    ins, expand_ref, reduce_ref, rest = refs[:8], refs[8], refs[9], refs[10:]
+    forward_steps(*ins, *rest, expand_ref, reduce_ref, [], lambda: None)
+
+
+def relayed_forward_kernel(depth, *refs):
+    ins, expand_in, reduce_in = refs[:8], refs[8], refs[9]
+    outs, expand_out, reduce_out = refs[10:21], refs[21], refs[22]
+    steps, expand_all, reduce_all = refs[23:27], refs[27], refs[28]
+    sems, save = refs[29:35], refs[35]
+    greet_neighbours(depth)
+    gather = Gather(
+        FEED_KINDS, depth, {EXPAND: expand_in, REDUCE: reduce_in}, {EXPAND: expand_all, REDUCE: reduce_all}, sems
+    )
+    gather.begin()
+
+    def saves():
+        return (
+            pltpu.make_async_copy(expand_all, expand_out, save.at[0]),
+            pltpu.make_async_copy(reduce_all, reduce_out, save.at[1]),
+        )
+
+    def before_feed():
+        gather.arrive()
+        for copy in saves():
+            copy.start()
+
+    forward_steps(*ins, *outs, *steps, expand_all, reduce_all, gather.relays(), before_feed)
+    gather.finish()
+    for copy in saves():
+        copy.wait()
+
+
+def forward_outs(tokens, seqs):
+    flat = jax.ShapeDtypeStruct((tokens, D), jnp.bfloat16)
     full = jax.ShapeDtypeStruct((tokens, D), jnp.float32)
+    few = jax.ShapeDtypeStruct((seqs, D), jnp.bfloat16)
+    return [
+        flat, flat, flat, flat, flat, full, full, few, few,
+        jax.ShapeDtypeStruct((seqs, D), jnp.float32),
+        jax.ShapeDtypeStruct((seqs, LANES), jnp.float32),
+    ]
+
+
+def forward_scratch(tokens, seqs):
+    return [
+        pltpu.VMEM((tokens, D), jnp.bfloat16),
+        pltpu.VMEM((seqs, D), jnp.float32),
+        pltpu.VMEM((D, tokens), jnp.float32),
+        pltpu.VMEM((D, tokens), jnp.bfloat16),
+    ]
+
+
+def run_forward(ins, expand, reduce_turned):
+    tokens, seqs = ins[1].shape[0], ins[6].shape[0]
     return pl.pallas_call(
         forward_kernel,
-        out_shape=[
-            flat, flat, flat, flat, flat, full, full,
-            jax.ShapeDtypeStruct((seqs, D), low),
-            jax.ShapeDtypeStruct((seqs, D), low),
-            jax.ShapeDtypeStruct((seqs, D), jnp.float32),
-            jax.ShapeDtypeStruct((seqs, LANES), jnp.float32),
-        ],
-        scratch_shapes=[pltpu.VMEM((tokens, D), low), pltpu.VMEM((seqs, D), jnp.float32)],
+        out_shape=forward_outs(tokens, seqs),
+        scratch_shapes=forward_scratch(tokens, seqs),
         compiler_params=pltpu.CompilerParams(vmem_limit_bytes=VMEM_CAP),
         name="layer_forward",
-    )(found, rank, square, expand, reduce_turned, gains, bias, mask, pool, lengths)
+    )(*ins, expand, reduce_turned)
+
+
+def run_relayed_forward(ins, expand_piece, reduce_piece, call_id):
+    depth = lax.axis_size("dp") // 2
+    tokens, seqs = ins[1].shape[0], ins[6].shape[0]
+    weight = (768, 3072)
+    outs = forward_outs(tokens, seqs)
+    whole = pl.BlockSpec(memory_space=pltpu.VMEM)
+    anywhere = pl.BlockSpec(memory_space=pl.ANY)
+    return pl.pallas_call(
+        functools.partial(relayed_forward_kernel, depth),
+        out_shape=outs + [jax.ShapeDtypeStruct(weight, jnp.bfloat16)] * 2,
+        in_specs=[whole] * (len(ins) + 2),
+        out_specs=[whole] * len(outs) + [anywhere] * 2,
+        scratch_shapes=forward_scratch(tokens, seqs)
+        + [pltpu.VMEM(weight, jnp.bfloat16)] * 2
+        + gather_sems(FEED_KINDS, depth)
+        + [pltpu.SemaphoreType.DMA((2,))],
+        compiler_params=pltpu.CompilerParams(
+            collective_id=call_id, has_side_effects=True, vmem_limit_bytes=VMEM_CAP
+        ),
+        name="layer_forward",
+    )(*ins, expand_piece, reduce_piece)
 
 
 def norm_back_rows(values, gain, grad):
@@ -1315,8 +1496,6 @@
     )(*ins)
 
 
-FEED_KINDS = (EXPAND, REDUCE)
-SQUARE_KINDS = (SQUARE,)
 BACK_CAP = 62 * 1024 * 1024
 
 
@@ -1446,6 +1625,119 @@
     )(*ins, grad_expand, grad_reduce)
 
 
+def loss_kernel(
+    query_rows, nli_rows, embeds_ref, negative_ref, scale_ref, grad_ref, stats_ref, everyone, grad_sims, turned_sims,
+    send, got, hand_send, hand_got,
+):
+    dp_size, fsdp_size = lax.axis_size("dp"), lax.axis_size("fsdp")
+    count = dp_size * fsdp_size
+    chips = count // 2
+    slots = embeds_ref.shape[0]
+    dp, fsdp = lax.axis_index("dp"), lax.axis_index("fsdp")
+    me = dp * fsdp_size + fsdp
+    core = lax.rem(fsdp, 2)
+    chip = me // 2
+    sibling = (dp, fsdp + 1 - 2 * core)
+    greet_all(count, fsdp_size, me)
+
+    def device(number):
+        return (number // fsdp_size, lax.rem(number, fsdp_size))
+
+    def across(k):
+        target = lax.rem(chip + k, chips) * 2 + core
+        return remote(embeds_ref, everyone.at[me], send.at[k], got.at[k], device(target))
+
+    def hand(k, of):
+        source = lax.rem(chip + chips - k, chips) * 2 + of
+        return remote(everyone.at[source], everyone.at[source], hand_send.at[k], hand_got.at[k], sibling)
+
+    def start(k, carry):
+        across(k).start()
+        return carry
+
+    def relay(k, carry):
+        across(k).wait_recv()
+        hand(k, core).start()
+        return carry
+
+    def end(k, carry):
+        across(k).wait_send()
+        hand(k, core).wait_send()
+        hand(k, 1 - core).wait_recv()
+        return carry
+
+    first = remote(embeds_ref, everyone.at[me], hand_send.at[0], hand_got.at[0], sibling)
+    first.start()
+    everyone[me] = embeds_ref[...]
+    lax.fori_loop(1, chips, start, 0)
+    lax.fori_loop(1, chips, relay, 0)
+    lax.fori_loop(1, chips, end, 0)
+    first.wait_send()
+    hand(0, 1 - core).wait_recv()
+
+    total_rows = count * slots
+    embeds = everyone[...].reshape(total_rows, D)
+    scale = jnp.exp(scale_ref[...])
+    sims = dot_nt(embeds, embeds)
+    row = lax.broadcasted_iota(jnp.int32, sims.shape, 0)
+    col = lax.broadcasted_iota(jnp.int32, sims.shape, 1)
+    row_slot, col_slot = row & (slots - 1), col & (slots - 1)
+    hypo, answer = query_rows + nli_rows, query_rows + 2 * nli_rows
+    is_query = row_slot < query_rows
+    is_premise = (row_slot >= query_rows) & (row_slot < hypo)
+    is_hypo = (col_slot >= hypo) & (col_slot < answer)
+    is_answer = (col_slot >= answer) & (col_slot < answer + query_rows)
+    allowed = (is_query & is_answer) | (is_premise & is_hypo)
+    target = (is_query & (col == row + answer)) | (is_premise & (col == row + nli_rows))
+    target = jnp.where(target, 1.0, 0.0)
+    logits = scale * sims
+    shown = jnp.where(allowed, logits, -1e30)
+    row_top = jnp.max(shown, axis=1, keepdims=True)
+    weight = jnp.where(negative_ref[:, :1] == col, 2.0, 1.0)
+    raised = jnp.where(allowed, weight * jnp.exp(shown - row_top), 0.0)
+    left = is_query | is_premise
+    row_total = jnp.where(left[:, :1], jnp.sum(raised, axis=1, keepdims=True), 1.0)
+    hits = jnp.sum(jnp.where(target > 0.0, logits, 0.0), axis=1, keepdims=True)
+    losses = jnp.where(left[:, :1], row_top + jnp.log(row_total), 0.0) - hits
+    first_loss = jnp.sum(jnp.where(is_query[:, :1], losses, 0.0), keepdims=True)
+    second_loss = jnp.sum(jnp.where(is_premise[:, :1], losses, 0.0), keepdims=True)
+    grad_logits = raised / row_total - target
+    grad_scale = scale * jnp.sum(grad_logits * sims, keepdims=True)
+    lane = lax.broadcasted_iota(jnp.int32, stats_ref.shape, 1)
+    stats_ref[...] = jnp.where(lane == 0, first_loss, jnp.where(lane == 1, second_loss, grad_scale))
+    grads = scale * grad_logits
+    grad_sims[...] = grads
+    turned_sims[...] = grads.T
+    own = pl.ds(pl.multiple_of(me * slots, 8), slots)
+    grad_ref[...] = dot_nn(grad_sims[own, :].astype(jnp.bfloat16), embeds) + dot_nn(
+        turned_sims[own, :].astype(jnp.bfloat16), embeds
+    )
+
+
+def run_loss(embeds, negative, log_scale, query_rows, nli_rows, call_id):
+    count = lax.axis_size("dp") * lax.axis_size("fsdp")
+    slots = embeds.shape[0]
+    square = (count * slots, count * slots)
+    chips = count // 2
+    return pl.pallas_call(
+        functools.partial(loss_kernel, query_rows, nli_rows),
+        out_shape=[jax.ShapeDtypeStruct((slots, D), jnp.float32), jax.ShapeDtypeStruct((8, LANES), jnp.float32)],
+        scratch_shapes=[
+            pltpu.VMEM((count, slots, D), jnp.bfloat16),
+            pltpu.VMEM(square, jnp.float32),
+            pltpu.VMEM(square, jnp.float32),
+            pltpu.SemaphoreType.DMA((chips,)),
+            pltpu.SemaphoreType.DMA((chips,)),
+            pltpu.SemaphoreType.DMA((chips,)),
+            pltpu.SemaphoreType.DMA((chips,)),
+        ],
+        compiler_params=pltpu.CompilerParams(
+            collective_id=call_id, has_side_effects=True, vmem_limit_bytes=VMEM_CAP
+        ),
+        name="loss",
+    )(embeds, negative, log_scale)
+
+
 def shards(
     embed_table,
     square_weights,
@@ -1501,32 +1793,28 @@
     split_at = short_tokens.shape[0] * short_length
 
     packed, rank = token_keys(all_tokens, fold)
-    start_info = jnp.concatenate(
+    key_rows = token_count // LANES
+    info = jnp.concatenate(
         [
-            packed.reshape(-1, LANES).astype(jnp.float32),
-            jnp.pad(hard_negative, (0, LANES - nli_rows)).reshape(1, LANES).astype(jnp.float32),
-            jnp.pad(norm_gains, ((0, 7 - 3), (0, LANES - feats))),
+            packed.reshape(key_rows, LANES),
+            jnp.pad(hard_negative, (0, LANES - nli_rows)).reshape(1, LANES),
+            jnp.zeros((7, LANES), jnp.int32),
         ],
         axis=0,
     )
-    key_rows = token_count // LANES
-    info_all = exchange(start_info[None], True, 0, "share_start")
-    packed_all = info_all[:, :key_rows].astype(jnp.int32).reshape(count, 1, token_count)
-    negative_all = info_all[:, key_rows, :nli_rows].astype(jnp.int32).reshape(-1)
-    gains = info_all[:, key_rows + 1 : key_rows + 4, :feats].transpose(1, 0, 2).reshape(3, D)
-    gains = jnp.pad(gains.astype(jnp.bfloat16).astype(jnp.float32), ((0, 5), (0, 0)))
-    row_all, group_all = packed_all >> 2, packed_all & 3
-
+    own_gains = jnp.pad(norm_gains, ((0, 5), (0, LANES - feats)))
     square_low = square_weights.astype(jnp.bfloat16)
     expand_low = expand_weight.astype(jnp.bfloat16)
     reduce_low = reduce_weight.astype(jnp.bfloat16).T
-    table_low = embed_table.astype(jnp.bfloat16).astype(jnp.float32)
+    half = token_count // 2
     if direct:
         square_pieces = square_low.reshape(5, 2, 48, 192).transpose(1, 0, 2, 3)
-        found, square_all, expand_all, reduce_all = run_front(
-            row_all[:, 0], group_all[:, 0], table_low, square_pieces, expand_low, reduce_low, 1
+        found, square_all, info_all, gains_all = run_front(
+            info, own_gains, token_count, embed_table, square_pieces, 1
         )
     else:
+        info_all = exchange(info[None], True, 0, "share_keys")
+        gains_all = exchange(own_gains[None], True, 6, "share_gains")
 
         def whole(piece, row_name, column_name):
             axis = piece.ndim - 2
@@ -1536,12 +1824,16 @@
         square_all = whole(square_low, "dp", "fsdp")
         expand_all = whole(expand_low, "dp", "fsdp")
         reduce_all = whole(reduce_low, "fsdp", "dp")
-        if feats_pad > feats:
-            table_low = jnp.pad(table_low, ((0, feats_pad - feats), (0, 0)))
-        found = exchange(lookup(table_low, row_all, group_all), False, 2, "send_features")
-    half = token_count // 2
-    found = found.reshape(count, 2, feats_pad, half)[:, :, :feats]
-    found = found.transpose(0, 2, 1, 3).reshape(D, token_count)
+        padded = jnp.pad(embed_table, ((0, feats_pad - feats), (0, 0)))
+        key_all = info_all[:, :key_rows].reshape(count, 1, token_count)
+        found = exchange(lookup(padded, key_all >> 2, key_all & 3), False, 8, "send_features")
+        found = found.reshape(count, 2, feats_pad, half)[:, :, :feats]
+        found = found.transpose(1, 0, 2, 3).reshape(1, 2 * D, half)
+    packed_all = info_all[:, :key_rows].reshape(count, 1, token_count)
+    row_all, group_all = packed_all >> 2, packed_all & 3
+    negative_all = info_all[:, key_rows, :nli_rows]
+    gains = gains_all[:, :3, :feats].transpose(1, 0, 2).reshape(3, D)
+    gains = jnp.pad(gains.astype(jnp.bfloat16).astype(jnp.float32), ((0, 5), (0, 0)))
 
     sequence = np.concatenate(
         [
@@ -1566,51 +1858,67 @@
     rank_rows = jnp.broadcast_to(rank[:, None], (token_count, LANES))
     bias, onehot = attention_bias(position_bias, TILE)
 
-    (start, queries, keys_here, values_here, mixed, middle, ending, embeds_low, pooled, embeds, inverse) = run_forward(
-        found, rank_rows, square_all, expand_all, reduce_all, gains, bias, mask, pool, length_rows
-    )
-    gathered = exchange(embeds_low[None], True, 3, "share_embeds")
-    queries_all = gathered[:, :query_rows].reshape(-1, D)
-    premises_all = gathered[:, query_rows:hypo_start].reshape(-1, D)
-    hypotheses_all = gathered[:, hypo_start:answer_start].reshape(-1, D)
-    answers_all = gathered[:, answer_start:seq_count].reshape(-1, D)
-    scale = jnp.exp(log_scale[0])
-
-    def contrast(left, right, extra, own):
-        sims = product_right(left, right)
-        logits = scale * sims
-        row_top = jnp.max(logits, axis=1, keepdims=True)
-        raised = (1.0 + extra) * jnp.exp(logits - row_top)
-        row_total = jnp.sum(raised, axis=1, keepdims=True)
-        spread = row_top[:, 0] + jnp.log(row_total[:, 0])
-        target_hit = jnp.eye(left.shape[0], dtype=jnp.float32)
-        loss_sum = jnp.sum(spread - jnp.sum(target_hit * logits, axis=1))
-        grad_logits = raised / row_total - target_hit
-        grad_scale = jnp.sum(grad_logits * sims)
-        grad_sims = (scale * grad_logits).astype(jnp.bfloat16)
-        mine_left = lax.dynamic_slice_in_dim(grad_sims, position * own, own, 0)
-        mine_right = lax.dynamic_slice_in_dim(grad_sims, position * own, own, 1)
-        return (loss_sum, grad_scale, product(mine_left, right), product_left(mine_right, left))
-
-    first_loss, first_dscale, grad_queries, grad_answers = contrast(
-        queries_all, answers_all, 0.0, query_rows
-    )
-    negatives = (jnp.arange(hypotheses_all.shape[0])[None, :] == negative_all[:, None]).astype(
-        jnp.float32
-    )
-    second_loss, second_dscale, grad_premises, grad_hypotheses = contrast(
-        premises_all, hypotheses_all, negatives, nli_rows
-    )
-    grad_embeds = jnp.concatenate(
-        [
-            grad_queries,
-            grad_premises,
-            grad_hypotheses,
-            grad_answers,
-            jnp.zeros((seq_pad - seq_count, D), jnp.float32),
-        ],
-        axis=0,
-    )
+    forward_ins = (found, rank_rows, square_all, gains, bias, mask, pool, length_rows)
+    if direct:
+        *forward_all, expand_all, reduce_all = run_relayed_forward(forward_ins, expand_low, reduce_low, 2)
+    else:
+        forward_all = run_forward(forward_ins, expand_all, reduce_all)
+    (start, queries, keys_here, values_here, mixed, middle, ending, embeds_low, pooled, embeds, inverse) = forward_all
+    if direct:
+        negative_place = (negative_all // nli_rows) * seq_pad + hypo_start + negative_all % nli_rows
+        negative_place = jnp.pad(
+            negative_place, ((0, 0), (query_rows, seq_pad - hypo_start)), constant_values=-1
+        )
+        negative_place = jnp.broadcast_to(negative_place.reshape(-1, 1), (count * seq_pad, LANES))
+        grad_embeds, stats = run_loss(
+            embeds_low, negative_place, log_scale.reshape(1, 1), query_rows, nli_rows, 3
+        )
+        losses, grad_scale = stats[0, :2], stats[0, 2:3]
+    else:
+        gathered = exchange(embeds_low[None], True, 3, "share_embeds")
+        queries_all = gathered[:, :query_rows].reshape(-1, D)
+        premises_all = gathered[:, query_rows:hypo_start].reshape(-1, D)
+        hypotheses_all = gathered[:, hypo_start:answer_start].reshape(-1, D)
+        answers_all = gathered[:, answer_start:seq_count].reshape(-1, D)
+        scale = jnp.exp(log_scale[0])
+
+        def contrast(left, right, extra, own):
+            sims = product_right(left, right)
+            logits = scale * sims
+            row_top = jnp.max(logits, axis=1, keepdims=True)
+            raised = (1.0 + extra) * jnp.exp(logits - row_top)
+            row_total = jnp.sum(raised, axis=1, keepdims=True)
+            spread = row_top[:, 0] + jnp.log(row_total[:, 0])
+            target_hit = jnp.eye(left.shape[0], dtype=jnp.float32)
+            loss_sum = jnp.sum(spread - jnp.sum(target_hit * logits, axis=1))
+            grad_logits = raised / row_total - target_hit
+            grad_scale = jnp.sum(grad_logits * sims)
+            grad_sims = (scale * grad_logits).astype(jnp.bfloat16)
+            mine_left = lax.dynamic_slice_in_dim(grad_sims, position * own, own, 0)
+            mine_right = lax.dynamic_slice_in_dim(grad_sims, position * own, own, 1)
+            return (loss_sum, grad_scale, product(mine_left, right), product_left(mine_right, left))
+
+        first_loss, first_dscale, grad_queries, grad_answers = contrast(
+            queries_all, answers_all, 0.0, query_rows
+        )
+        negatives = (jnp.arange(hypotheses_all.shape[0])[None, :] == negative_all.reshape(-1)[:, None]).astype(
+            jnp.float32
+        )
+        second_loss, second_dscale, grad_premises, grad_hypotheses = contrast(
+            premises_all, hypotheses_all, negatives, nli_rows
+        )
+        grad_embeds = jnp.concatenate(
+            [
+                grad_queries,
+                grad_premises,
+                grad_hypotheses,
+                grad_answers,
+                jnp.zeros((seq_pad - seq_count, D), jnp.float32),
+            ],
+            axis=0,
+        )
+        losses = jnp.stack([first_loss, second_loss])
+        grad_scale = ((first_dscale + second_dscale) * scale).reshape(1)
     (grad_expand, grad_reduce, grad_middle, grad_middle_low, grad_proj, late_gains) = run_feed_back(
         grad_embeds, embeds, inverse, pool, length_rows, square_all, middle, ending, expand_all, reduce_all, gains
     )
@@ -1645,7 +1953,6 @@
     grad_position = lax.dot_general(
         onehot, grad_scores.reshape(HEADS, TILE * TILE), (((0,), (1,)), ((), ())), precision=HIGHEST
     )
-    grad_scale = ((first_dscale + second_dscale) * scale).reshape(1)
     reduced = (square_sum, expand_sum, reduce_sum.T)
     local_square = (
         jnp.sum(reduced[0] * reduced[0])
@@ -1656,12 +1963,11 @@
     small = jnp.concatenate([grad_gains.reshape(-1), grad_position.reshape(-1), local_square.reshape(1)])
     small_rows = -(-small.shape[0] // (8 * LANES)) * 8
     small = jnp.pad(small, (0, small_rows * LANES - small.shape[0])).reshape(1, small_rows, LANES)
-    summed = jnp.sum(exchange(small, True, 6, "share_small"), axis=0).reshape(-1)
+    summed = jnp.sum(exchange(small, True, 7, "share_small"), axis=0).reshape(-1)
     gains_total = summed[: 3 * D].reshape(3, D)
     position_total = summed[3 * D : 3 * D + BUCKETS * HEADS].reshape(BUCKETS, HEADS)
     square_total = summed[3 * D + BUCKETS * HEADS]
     scale_total = grad_scale
-    losses = jnp.stack([first_loss, second_loss])
     grad_gain_shard = lax.dynamic_slice_in_dim(gains_total, position * feats, feats, 1)
     gradient_norm = jnp.sqrt(
         square_total

time: 551 us -> 511 us (0.927)
  Pallas kernels: 462 us -> 435 us
  other arithmetic: 46.1 us -> 36 us
    pallas_call x1 -> x2, Pallas kernels: 44.5 us -> 96.7 us  [the longest x1 78.3 us: run_relayed_forward(): pl.pallas_call(functools.partial(relayed_forward_kernel, depth), out_shap...]
    pallas_call x1, Pallas kernels: 113 us -> 71.6 us  [run_front(): pl.pallas_call(functools.partial(front_kernel, fold, depth), out_shape=[j...]
    pallas_call x3 -> x1, Pallas kernels: 53.2 us -> 15.3 us  [exchange(): pl.pallas_call(functools.partial(exchange_kernel, same), out_shape=jax.Sh...]
where the time goes in v5:
time: 511 us; the launch traced here: 502 us
  Pallas kernels  435 us (85%)
  other arithmetic  36 us (7%)
  between operations  14.6 us (3%)
  local copies, waits for them, and re-layouts  13.4 us (3%)
    pallas_call x1, Pallas kernels, run_back(): pl.pallas_call(functools.partial(back_kernel, depth), out_shape=[jax.Shap...  130 us
    pallas_call x1, Pallas kernels, run_relayed_forward(): pl.pallas_call(functools.partial(relayed_forward_kernel, depth), out_shap...  78.3 us
    pallas_call x1, Pallas kernels, run_front(): pl.pallas_call(functools.partial(front_kernel, fold, depth), out_shape=[j...  71.6 us
    pallas_call x1, Pallas kernels, scatter(): pl.pallas_call(functools.partial(scatter_kernel, fold), grid=(n,), out_sh...  68.4 us
    pallas_call x1, Pallas kernels, run_feed_back(): pl.pallas_call(feed_back_kernel, grid=(1,), out_shape=[jax.ShapeDtypeStru...  52.3 us
    pallas_call x1, Pallas kernels, run_loss(): pl.pallas_call(functools.partial(loss_kernel, query_rows, nli_rows), out_...  18.4 us
    pallas_call x1, Pallas kernels, exchange(): pl.pallas_call(functools.partial(exchange_kernel, same), out_shape=jax.Sh...  15.3 us
    sub x6, other arithmetic, adam_update(): weight - rate * (moment_hat / (jnp.sqrt(second_hat) + ADAM_EPS) + WEIGHT_...  14.7 us

profile of v5, /device:TPU:15, one launch (start us, length us, event | category | flops | bytes accessed | tf_op | source)
XLA Modules:
  0.0 501.6 jit_solution(11760829057242828496)
XLA Ops:
  0.7 0.8 pad_add_fusion
  1.6 0.8 broadcast_add_fusion
  2.8 0.7 convert_reduce_fusion
  3.6 1.1 select_reduce_fusion
  6.1 1.1 convert_element_type.35
  7.9 1.3 pad.27.gains_ref
  9.2 71.6 %front.1 = (bf16[32,48,512]{2,1,0:T(8,128)(2,1)}, bf16[5,768,768]{2,1,0:T(8,128)(2,1)}, s32[32,16,128]{2,1,0:T(8,128)}, f32[32,8,128]{2,1,0:T(8,128)}) custom-call(s32[16,128]{1,0:T(8,128)} %add_add_fusion.keys_ref, f32[8,128]{1,0:T(8,128)} %pad.27.gains_ref, f32[24,32128]{1,0:T(8,128)} %table_ref.1, bf16[2,5,48,192]{3,2,1,0:T(8,128)(2,1)} %bitcast.77), custom_call_target="tpu_custom_call" | custom-call | tf_op jit(solution)/shard_map/front/pallas_call | solution.py:707
  80.8 0.9 fusion.11
  82.4 1.0 broadcast_in_dim.33.refs_1_.refs_13_
  84.3 0.9 and_select_fusion.refs_5_.refs_12_
  85.8 1.2 fusion.29
  87.2 0.9 bitcast_bitcast_fusion.refs_4_.refs_11_
  89.5 78.3 %layer_forward.1 = (bf16[1024,768]{1,0:T(8,128)(2,1)}, bf16[1024,768]{1,0:T(8,128)(2,1)}, bf16[1024,768]{1,0:T(8,128)(2,1)}, bf16[1024,768]{1,0:T(8,128)(2,1)}, ...) custom-call(bf16[32,48,512]{2,1,0:T(8,128)(2,1)} %get-tuple-element., ...), custom_call_target="tpu_custom_call" | custom-call | tf_op jit(solution)/shard_map/layer_forward/pallas_call | solution.py:1244
  168.2 0.8 broadcast_in_dim.62.negative_ref
  169.7 18.4 %loss.1 = (f32[16,768]{1,0:T(8,128)}, f32[8,128]{1,0:T(8,128)}) custom-call(bf16[16,768]{1,0:T(8,128)(2,1)} %get-tuple-element.58.embeds_ref, s32[512,128]{1,0:T(8,128)} %broadcast_in_dim.62.negative_ref, f32[1,1]{1,0:T(1,128)} %bitcast.72.scale_ref), custom_call_target="tpu_custom_call" | custom-call | tf_op jit(solution)/shard_map/loss/pallas_call | solution.py:1722
  188.1 52.3 %feed_backward.1 = (bf16[768,3072]{1,0:T(8,128)(2,1)}, bf16[768,3072]{1,0:T(8,128)(2,1)}, f32[1024,768]{1,0:T(8,128)}, bf16[1024,768]{1,0:T(8,128)(2,1)}, bf16[16,768]{1,0:T(8,128)(2,1)}, /*index=5*/f32[8,768]{1,0:T(8,128)}) custom-call(f32[16,768]{1,0:T(8,128)} %get-tuple-element.59.grad_embed_ref, f32[16,768]{1,0:T(8,128)} %get-tuple-element.60.embed_ref, ...), custom_call_target="tpu_custom_call" | custom-call | tf_op jit(solution)/shard_map/feed_backward/pallas_call | solution.py:1335
  240.4 130.3 %back.1 = (f32[2,5,48,192]{3,2,1,0:T(8,128)}, f32[96,768]{1,0:T(8,128)}, f32[192,384]{1,0:T(8,128)}, f32[12,128,128]{2,1,0:T(8,128)}, f32[8,768]{1,0:T(8,128)}, /*index=5*/bf16[32,48,512]{2,1,0:T(8,128)(2,1)}) custom-call(f32[1024,768]{1,0:T(8,128)} %get-tuple-element.66.refs_0_, bf16[1024,768]{1,0:T(8,128)(2,1)} %get-tuple-element.67.refs_1_, ...), custom_call_target="tpu_custom_call" | custom-call | tf_op jit(solution)/shard_map/back/pallas_call | solution.py:1590
  370.7 0.7 slice.36
  372.2 1.8 multiply_reduce_fusion.1
  374.0 1.6 multiply_reduce_fusion.3
  376.9 1.6 multiply_reduce_fusion.2
  379.9 68.4 %scatter.1 = f32[24,32128]{1,0:T(8,128)} custom-call(s32[32,1,1024]{2,1,0:T(1,128)} %bitcast.80, s32[32,1,1024]{2,1,0:T(1,128)} %bitcast.79, bf16[32,48,512]{2,1,0:T(8,128)(2,1)} %get-tuple-element.77.grad_ref), custom_call_target="tpu_custom_call" | custom-call | tf_op jit(solution)/shard_map/scatter/pallas_call | solution.py:219
  448.4 3.4 multiply_reduce_fusion
  453.2 1.8 fusion.30
  455.7 15.3 %share_small.1 = f32[32,24,128]{2,1,0:T(8,128)} custom-call(f32[1,24,128]{2,1,0:T(8,128)} %fusion.12.src), custom_call_target="tpu_custom_call" | custom-call | tf_op jit(solution)/shard_map/share_small/pallas_call | solution.py:305
  471.1 1.0 reduce_sum.93
  475.8 1.3 slice.41
  482.0 2.2 multiply_subtract_fusion.2
  484.3 2.2 multiply_subtract_fusion.3
  486.5 2.7 multiply_subtract_fusion.1
  489.2 6.3 %multiply_subtract_fusion = (f32[24,32128]{1,0:T(8,128)}, f32[24,32128]{1,0:T(8,128)}, f32[24,32128]{1,0:T(8,128)}) fusion(f32[24,32128]{1,0:T(8,128)S(1)} %copy-done.1, f32[24,32128]{1,0:T(8,128)S(1)} %copy-done, f32[]{:T(128)} %min_shard_map.3, f32[24,32128]{1,0:T(8,128)S(1)} %copy-done.4, f32[24,32128]{1,0:T(8,128)} %param.39), kind=kLoop, calls=%fused_computation.9 | loop fusion | flops 12337152 | bytes 21590020 | tf_op jit(solution)/shard_map/sub | solution.py:80
  495.5 1.2 slice_bitcast_fusion
  (95 shorter events, 13.0 us)
Async XLA Ops:
  0.7 82.9 %copy-start.20 = (s32[1024]{0:T(1024)S(1)}, s32[1024]{0:T(1024)}, u32[]{:S(2)}) copy-start(s32[1024]{0:T(1024)} %constant.223) | copy-start | bytes 12292
  0.7 82.9 %copy-start.16 = (pred[16,1024]{1,0:T(8,128)(4,1)S(1)}, pred[16,1024]{1,0:T(8,128)(4,1)}, u32[]{:S(2)}) copy-start(pred[16,1024]{1,0:T(8,128)(4,1)} %constant.93.clone) | copy-start | bytes 49156
  0.7 83.6 %copy-start.13 = (pred[8,128,128]{2,1,0:T(32,128)(4,1)S(1)}, pred[8,128,128]{2,1,0:T(32,128)(4,1)}, u32[]{:S(2)}) copy-start(pred[8,128,128]{2,1,0:T(32,128)(4,1)} %constant.94.clone) | copy-start | bytes 393220
  0.7 82.7 %copy-start.24 = (s32[4]{0:T(128)S(1)}, s32[4]{0:T(128)}, u32[]{:S(2)}) copy-start(s32[4]{0:T(128)} %param.55) | copy-start | bytes 52
  0.7 82.7 %copy-start.23 = (s32[4]{0:T(128)S(1)}, s32[4]{0:T(128)}, u32[]{:S(2)}) copy-start(s32[4]{0:T(128)} %param.56) | copy-start | bytes 52
  1.5 84.3 %copy-start.2 = (f32[16384,32]{0,1:T(8,128)S(1)}, f32[16384,32]{0,1:T(8,128)}, u32[]{:S(2)}) copy-start(f32[16384,32]{0,1:T(8,128)} %constant.98.clone) | copy-start | bytes 6291460
  1.5 84.3 %copy-start.15 = (f32[32,12]{0,1:T(8,128)S(1)}, f32[32,12]{0,1:T(8,128)}, u32[]{:S(2)}) copy-start(f32[32,12]{0,1:T(8,128)} %param.37) | copy-start | bytes 4612
  85.8 2.4 copy-start.7
  85.8 3.1 copy-start.8
  89.5 78.3 %copy-start.14 = (s32[32,16,128]{2,1,0:T(8,128)S(1)}, s32[32,16,128]{2,1,0:T(8,128)}, u32[]{:S(2)}) copy-start(s32[32,16,128]{2,1,0:T(8,128)} %get-tuple-element.54) | copy-start | bytes 786436
  379.9 72.5 %copy-start.11 = (f32[12,128,128]{2,1,0:T(8,128)S(1)}, f32[12,128,128]{2,1,0:T(8,128)}, u32[]{:S(2)}) copy-start(f32[12,128,128]{2,1,0:T(8,128)} %get-tuple-element.80) | copy-start | bytes 2359300
  448.4 4.9 copy-start.3
  452.5 28.1 %copy-start.17 = (f32[32,12]{0,1:T(8,128)S(1)}, f32[32,12]{0,1:T(8,128)}, u32[]{:S(2)}) copy-start(f32[32,12]{0,1:T(8,128)} %param.50) | copy-start | bytes 4612
  452.5 28.1 %copy-start.18 = (f32[32,12]{0,1:T(8,128)S(1)}, f32[32,12]{0,1:T(8,128)}, u32[]{:S(2)}) copy-start(f32[32,12]{0,1:T(8,128)} %param.49) | copy-start | bytes 4612
  452.5 28.8 %copy-start.19 = (f32[3,24]{1,0:T(4,128)S(1)}, f32[3,24]{1,0:T(4,128)}, u32[]{:S(2)}) copy-start(f32[3,24]{1,0:T(4,128)} %param.36) | copy-start | bytes 868
  452.6 28.7 %copy-start.21 = (f32[3,24]{1,0:T(4,128)S(1)}, f32[3,24]{1,0:T(4,128)}, u32[]{:S(2)}) copy-start(f32[3,24]{1,0:T(4,128)} %param.48) | copy-start | bytes 868
  452.6 28.7 %copy-start.22 = (f32[3,24]{1,0:T(4,128)S(1)}, f32[3,24]{1,0:T(4,128)}, u32[]{:S(2)}) copy-start(f32[3,24]{1,0:T(4,128)} %param.47) | copy-start | bytes 868
  452.6 29.4 %copy-start.10 = (f32[192,384]{1,0:T(8,128)S(1)}, f32[192,384]{1,0:T(8,128)}, u32[]{:S(2)}) copy-start(f32[192,384]{1,0:T(8,128)} %get-tuple-element.83) | copy-start | bytes 884740
  453.2 31.0 %copy-start.9 = (f32[96,768]{1,0:T(8,128)S(1)}, f32[96,768]{1,0:T(8,128)}, u32[]{:S(2)}) copy-start(f32[96,768]{1,0:T(8,128)} %get-tuple-element.82) | copy-start | bytes 884740
  455.0 29.3 %copy-start.12 = (f32[96,768]{1,0:T(8,128)S(1)}, f32[96,768]{1,0:T(8,128)}, u32[]{:S(2)}) copy-start(f32[96,768]{1,0:T(8,128)} %param.44) | copy-start | bytes 884740
  455.0 31.4 %copy-start.5 = (f32[2,5,48,192]{3,2,1,0:T(8,128)S(1)}, f32[2,5,48,192]{3,2,1,0:T(8,128)}, u32[]{:S(2)}) copy-start(f32[2,5,48,192]{3,2,1,0:T(8,128)} %get-tuple-element.81) | copy-start | bytes 1105924
  480.4 6.1 %copy-start.6 = (f32[5,96,192]{2,1,0:T(8,128)S(1)}, f32[5,96,192]{2,1,0:T(8,128)}, u32[]{:S(2)}) copy-start(f32[5,96,192]{2,1,0:T(8,128)} %param.33) | copy-start | bytes 1105924
  482.0 7.2 %copy-start.4 = (f32[24,32128]{1,0:T(8,128)S(1)}, f32[24,32128]{1,0:T(8,128)}, u32[]{:S(2)}) copy-start(f32[24,32128]{1,0:T(8,128)} %param.40) | copy-start | bytes 9252868
  484.3 5.0 copy-start.1
  486.4 2.8 copy-start

commit v6 on v5

--- a/solution.py
+++ b/solution.py
@@ -169,7 +169,7 @@
         name="lookup",
     )(rows_idx, groups_idx, table)
 
-def scatter_kernel(fold, row_ref, group_ref, grad_ref, out_ref, total, rows):
+def scatter_kernel(fold, row_ref, group_ref, grad_ref, out_ref, squares_ref, total, rows):
     feats, vocab = out_ref.shape
     tokens = rows.shape[0]
     step = pl.program_id(0)
@@ -180,64 +180,77 @@
             return 0
         lax.fori_loop(0, fold // LANES, clear, 0)
         total[pl.ds(fold, 8), :] = jnp.zeros((8, LANES), jnp.float32)
-    block = grad_ref[0].astype(jnp.float32)
-    flat = jnp.concatenate([block[:feats], block[feats:]], axis=1)
+    flat = []
+    for half in range(2):
+        block = grad_ref[half, 0].astype(jnp.float32)
+        flat += [block[:feats], block[feats:]]
+    flat = jnp.concatenate(flat, axis=1)
     group = group_ref[0]
     pad = jnp.zeros((SLOT - feats, tokens), jnp.float32)
     parts = []
     for j in range(GROUPS):
         parts += [jnp.where(group == j, flat, 0.0), pad]
-    spread = jnp.concatenate(parts, axis=0).astype(jnp.bfloat16)
-    rows[...] = lax.dot_general(spread, eye(), (((0,), (0,)), ((), ())), preferred_element_type=jnp.float32)
-    LN = 16
-    stride = tokens // LN
-    def add(i, _):
-        at = [row_ref[0, 0, i + stride * k] for k in range(LN)]
-        new = [total[pl.ds(at[k], 1), :] + rows[pl.ds(i + stride * k, 1), :] for k in range(LN)]
-        for k in range(LN):
-            total[pl.ds(at[k], 1), :] = new[k]
-        return 0
-    lax.fori_loop(0, stride, add, 0, unroll=2)
+    rows[...] = jnp.concatenate(parts, axis=0).T
+    lines = tokens // LANES
+    ways = 32 // lines
+    per = LANES // ways
+    for half in range(2):
+        for l in range(per):
+            spots = [(r, l + per * w) for r in range(half * lines // 2, (half + 1) * lines // 2) for w in range(ways)]
+            at = [row_ref[r, c] for r, c in spots]
+            new = [
+                total[pl.ds(at[n], 1), :] + rows[pl.ds(r * LANES + c, 1), :] for n, (r, c) in enumerate(spots)
+            ]
+            for n in range(len(spots)):
+                total[pl.ds(at[n], 1), :] = new[n]
+
     @pl.when(step == pl.num_programs(0) - 1)
     def _():
         whole = (vocab - (GROUPS - 1) * fold) // LANES
-        def turn(b, _):
+        def turn(b, squares):
             tile = total[pl.ds(pl.multiple_of(b * LANES, LANES), LANES), :].T
             for j in range(GROUPS):
-                out_ref[:, pl.ds(pl.multiple_of(j * fold + b * LANES, LANES), LANES)] = tile[j * SLOT:j * SLOT + feats]
-            return 0
-        lax.fori_loop(0, whole, turn, 0)
+                out_ref[:, pl.ds(pl.multiple_of(j * fold + b * LANES, LANES), LANES)] = tile[j * SLOT : j * SLOT + feats]
+            return squares + tile * tile
+
+        squares = lax.fori_loop(0, whole, turn, jnp.zeros((LANES, LANES), jnp.float32))
         for b in range(whole, fold // LANES):
             tile = total[pl.ds(b * LANES, LANES), :].T
             for j in range(GROUPS - 1):
-                out_ref[:, pl.ds(j * fold + b * LANES, LANES)] = tile[j * SLOT:j * SLOT + feats]
+                out_ref[:, pl.ds(j * fold + b * LANES, LANES)] = tile[j * SLOT : j * SLOT + feats]
+            squares = squares + tile * tile
+        squares_ref[...] = jnp.sum(squares.reshape(LANES // 8, 8, LANES), axis=0)
+
 
 def scatter(grads, rows_idx, groups_idx, vocab):
     n, tokens = rows_idx.shape[0], rows_idx.shape[2]
-    feats = grads.shape[1] // 2
+    feats = grads.shape[2] // 2
     fold = fold_rows(vocab)
     return pl.pallas_call(
         functools.partial(scatter_kernel, fold),
         grid=(n,),
-        out_shape=jax.ShapeDtypeStruct((feats, vocab), jnp.float32),
+        out_shape=[jax.ShapeDtypeStruct((feats, vocab), jnp.float32), jax.ShapeDtypeStruct((8, LANES), jnp.float32)],
         in_specs=[
-            pl.BlockSpec((1, 1, tokens), lambda s: (s, 0, 0), memory_space=pltpu.SMEM),
+            pl.BlockSpec((tokens // LANES, LANES), lambda s: (s, 0), memory_space=pltpu.SMEM),
             pl.BlockSpec((1, 1, tokens), lambda s: (s, 0, 0)),
-            pl.BlockSpec((1, 2 * feats, tokens // 2), lambda s: (s, 0, 0)),
+            pl.BlockSpec((2, 1, 2 * feats, tokens // 4), lambda s: (0, s, 0, 0)),
         ],
-        out_specs=pl.BlockSpec((feats, vocab), lambda s: (0, 0)),
+        out_specs=[pl.BlockSpec((feats, vocab), lambda s: (0, 0)), pl.BlockSpec((8, LANES), lambda s: (0, 0))],
         scratch_shapes=[pltpu.VMEM((fold + 8, LANES), jnp.float32), pltpu.VMEM((tokens, LANES), jnp.float32)],
         compiler_params=pltpu.CompilerParams(vmem_limit_bytes=VMEM_CAP),
         name="scatter",
-    )(rows_idx, groups_idx, grads)
+    )(rows_idx.reshape(-1, LANES), groups_idx, grads)
 
 def token_keys(tokens, fold):
     count = tokens.shape[0]
     key = (tokens % fold) * GROUPS + tokens // fold
     places = jnp.arange(count, dtype=jnp.int32)
-    same_before = (key[:, None] == key[None, :]) & (places[:, None] < places[None, :])
+    half = count // 2
+    together = (places[:, None] < half) == (places[None, :] < half)
+    same_before = together & (key[:, None] == key[None, :]) & (places[:, None] < places[None, :])
     first = ~jnp.any(same_before, axis=0)
-    rank = jnp.sum(((key[None, :] < key[:, None]) & first[None, :]).astype(jnp.int32), axis=1)
+    rank = jnp.sum((together & (key[None, :] < key[:, None]) & first[None, :]).astype(jnp.int32), axis=1)
+    rank = rank + jnp.where(places < half, 0, half)
     hit = (rank[:, None] == places[None, :]) & first[:, None]
     packed = GROUPS * fold + jnp.sum(jnp.where(hit, key[:, None] - GROUPS * fold, 0), axis=0)
     return packed, rank
@@ -317,18 +330,18 @@
     )(blocks)
 
 
-SQUARE, EXPAND, REDUCE = range(3)
-KINDS = 3
-STEPS = (5, 6, 4)
-FIRST = (3, 3, 2)
+SQUARE, EXPAND, REDUCE, EARLY, LATE = range(5)
+STEPS = (5, 6, 4, 2, 3)
+FIRST = (3, 3, 2, 1, 2)
+SPANS = {SQUARE: (0, 5), EARLY: (3, 2), LATE: (0, 3)}
 
 
 def spot(refs, kind, z, x, y, core):
     dp = z * 2 + x
     column = y * 2 + core
-    if kind == SQUARE:
-        return refs[kind].at[
-            :,
+    if kind in SPANS:
+        return refs[SQUARE].at[
+            pl.ds(*SPANS[kind]),
             pl.ds(pl.multiple_of(dp * 96 + core * 48, 16), 48),
             pl.ds(pl.multiple_of(y * 384, 128), 384),
         ]
@@ -361,21 +374,14 @@
     ]
 
 
-def block_part(ref, kind, part):
-    if kind == SQUARE:
-        return ref.at[pl.ds(0, 3) if part == 0 else pl.ds(3, 2)]
-    half = 48 if kind == EXPAND else 96
-    return ref.at[pl.ds(part * half, half)]
-
-
 def block_step(ref, kind, k):
-    if kind == SQUARE:
+    if kind in SPANS:
         return ref.at[k]
     rows = 16 if kind == EXPAND else 48
     return ref.at[pl.ds(pl.multiple_of(k * rows, 16), rows)]
 
 
-BLOCKS = ((5, 48, 384), (96, 768), (192, 384))
+BLOCKS = ((5, 48, 384), (96, 768), (192, 384), (2, 48, 384), (3, 48, 384))
 
 
 def place():
@@ -448,9 +454,9 @@
             self.sources[a], spot(self.outs, a, self.z, self.x, self.y, self.core), self.own_sem.at[self.number[a]]
         )
 
-    def begin(self):
+    def begin(self, kinds):
         z, x, y, core = self.z, self.x, self.y, self.core
-        for a in self.kinds:
+        for a in kinds:
             source = self.sources[a]
             self.own_copy(a).start()
 
@@ -583,12 +589,16 @@
     ]
 
 
-FEED_KINDS = (EXPAND, REDUCE)
-SQUARE_KINDS = (SQUARE,)
-
-
-def front_kernel(fold, depth, keys_ref, gains_ref, table_ref, square_in, *refs):
-    found, square_out, keys_all, gains_all = refs[:4]
+BY_Y = (EXPAND, EARLY)
+FIRST_KINDS = (EXPAND, REDUCE, EARLY)
+LAST_KINDS = (LATE,)
+FRONT_KINDS = (SQUARE, EXPAND)
+LATER_KINDS = (REDUCE,)
+
+
+def front_kernel(fold, depth, keys_ref, gains_ref, table_ref, square_in, expand_in, *refs):
+    found, square_out, expand_out, keys_all, gains_all = refs[:5]
+    refs = refs[1:]
     theirs, own, turned, rows, blocks, row_low, row_all = refs[4:11]
     gather_sem, refs = refs[11:17], refs[17:]
     pair_send, pair_recv, part_send, part_got, part_own, keys_send, keys_got, gains_send, gains_got, near_sem = refs
@@ -617,7 +627,10 @@
     gains_all[me] = gains_ref[...]
     pair = remote(square_in.at[1 - core], theirs, pair_send, pair_recv, sibling)
     pair.start()
-    gather = Gather(SQUARE_KINDS, depth, {SQUARE: own}, {SQUARE: square_out}, gather_sem)
+    gather = Gather(
+        FRONT_KINDS, depth, {SQUARE: own, EXPAND: expand_in}, {SQUARE: square_out, EXPAND: expand_out}, gather_sem
+    )
+    gather.begin((EXPAND,))
     row = lax.broadcasted_iota(jnp.int32, (192, 384), 0)
     col = lax.broadcasted_iota(jnp.int32, (192, 384), 1)
     here = (row + core * 192 == col).astype(jnp.float32).astype(jnp.bfloat16)
@@ -628,7 +641,7 @@
             theirs[k], there, preferred_element_type=jnp.float32
         )
         own[k] = block.astype(jnp.bfloat16)
-    gather.begin()
+    gather.begin((SQUARE,))
     turn_table(fold, table_ref, turned)
 
     def end_info(k, carry):
@@ -695,7 +708,7 @@
     lax.fori_loop(1, count, end_part, 0)
 
 
-def run_front(keys, gains, tokens, table, square, call_id):
+def run_front(keys, gains, tokens, table, square, expand, call_id):
     depth = lax.axis_size("dp") // 2
     count = lax.axis_size("dp") * lax.axis_size("fsdp")
     feats, vocab = table.shape
@@ -709,11 +722,12 @@
         out_shape=[
             jax.ShapeDtypeStruct(blocks, jnp.bfloat16),
             jax.ShapeDtypeStruct((5, 768, 768), jnp.bfloat16),
+            jax.ShapeDtypeStruct((768, 3072), jnp.bfloat16),
             jax.ShapeDtypeStruct((count,) + keys.shape, keys.dtype),
             jax.ShapeDtypeStruct((count,) + gains.shape, gains.dtype),
         ],
-        in_specs=[whole] * 4,
-        out_specs=[anywhere] * 2 + [whole] * 2,
+        in_specs=[whole] * 5,
+        out_specs=[anywhere] * 3 + [whole] * 2,
         scratch_shapes=[
             pltpu.VMEM((5, 48, 192), jnp.bfloat16),
             pltpu.VMEM((5, 48, 384), jnp.bfloat16),
@@ -723,7 +737,7 @@
             pltpu.VMEM((count * tokens // LANES, LANES), jnp.int32),
             pltpu.SMEM((count * tokens // LANES, LANES), jnp.int32),
         ]
-        + gather_sems(SQUARE_KINDS, depth)
+        + gather_sems(FRONT_KINDS, depth)
         + [pltpu.SemaphoreType.DMA, pltpu.SemaphoreType.DMA]
         + [many, many, pltpu.SemaphoreType.DMA]
         + [many] * 4
@@ -732,7 +746,7 @@
             collective_id=call_id, has_side_effects=True, vmem_limit_bytes=VMEM_CAP
         ),
         name="front",
-    )(keys, gains, table, square)
+    )(keys, gains, table, square, expand)
 
 
 class Reduction:
@@ -750,27 +764,51 @@
         self.sibling = device_at(z, x, y, 1 - core)
         self.x_next, self.y_next = device_at(z, 1 - x, y, core), device_at(z, x, 1 - y, core)
 
+    def piece(self, ref, a, z_at, x_at, y_at):
+        i = z_at * 2 + x_at
+        if a == EXPAND:
+            return ref.at[y_at, pl.ds(pl.multiple_of(i * 96, 16), 96)]
+        if a == REDUCE:
+            return ref.at[y_at, :, pl.ds(pl.multiple_of(i * 384, 128), 384)]
+        return ref.at[i, :, :, pl.ds(pl.multiple_of(y_at * 384, 128), 384)]
+
     def work(self, a, z_at, x_at, y_at):
-        if self.own_work is None:
+        if a in SPANS:
             return spot(self.grads, a, z_at, x_at, y_at, self.core)
-        return self.own_work[a].at[z_at * 2 + x_at, y_at]
-
-    def load(self, a, z_at, x_at, y_at):
+        return self.piece(self.own_work[a], a, z_at, x_at, y_at)
+
+    def half(self, a, y_at, core):
+        column = y_at * 2 + core
+        if a == EXPAND:
+            return self.grads[a].at[:, pl.ds(pl.multiple_of(column * 768, 128), 768)]
+        return self.grads[a].at[pl.ds(pl.multiple_of(column * 192, 16), 192)]
+
+    def load(self, a, y_at):
         return pltpu.make_async_copy(
-            spot(self.grads, a, z_at, x_at, y_at, self.core),
-            self.work(a, z_at, x_at, y_at),
-            self.load_sem.at[self.number[a], z_at * 2 + x_at, y_at],
-        )
-
-    def pair(self, a, z_at, x_at, y_at):
-        n, i = self.number[a], z_at * 2 + x_at
-        return remote(
-            spot(self.grads, a, z_at, x_at, y_at, 1 - self.core),
-            self.paired[a].at[i, y_at],
-            self.pair_send.at[n, i, y_at],
-            self.pair_got.at[n, i, y_at],
-            self.sibling,
-        )
+            self.half(a, y_at, self.core), self.own_work[a].at[y_at], self.load_sem.at[self.number[a], y_at]
+        )
+
+    def pair(self, a, at):
+        n = self.number[a]
+        if a in SPANS:
+            source = self.grads[SQUARE].at[
+                pl.ds(*SPANS[a]), pl.ds(pl.multiple_of(at * 96 + (1 - self.core) * 48, 16), 48)
+            ]
+        else:
+            source = self.half(a, at, 1 - self.core)
+        return remote(source, self.paired[a].at[at], self.pair_send.at[n, at], self.pair_got.at[n, at], self.sibling)
+
+    def each_pair(self, a, act):
+        if a not in SPANS:
+            act(1 - self.y)
+            act(self.y)
+            return
+
+        def one(i, carry):
+            act(i)
+            return carry
+
+        lax.fori_loop(0, 2 * self.depth, one, 0)
 
     def sides(self, step, act):
         if step == 0:
@@ -783,56 +821,53 @@
             def _():
                 act(z_at)
 
-    def begin(self):
-        x, y = self.x, self.y
-        for x_at, y_at in ((1 - x, 1 - y), (1 - x, y), (x, 1 - y), (x, y)):
-            for step in range(self.depth - 1, -1, -1):
-
-                def start(z_at):
-                    for a in self.kinds:
-                        if self.own_work is not None:
-                            self.load(a, z_at, x_at, y_at).start()
-                        self.pair(a, z_at, x_at, y_at).start()
-
-                self.sides(step, start)
-
-    def ready(self, a, z_at, x_at, y_at):
-        if self.own_work is not None:
-            self.load(a, z_at, x_at, y_at).wait()
-        self.pair(a, z_at, x_at, y_at).wait_recv()
-
-    def total(self, a, z_at, x_at, y_at, first, last, extra=()):
+    def begin(self, kinds):
+        for a in kinds:
+
+            def start(at):
+                if a not in SPANS:
+                    self.load(a, at).start()
+                self.pair(a, at).start()
+
+            self.each_pair(a, start)
+
+    def ready(self, last):
+        for a in self.kinds:
+            if a in SPANS:
+                if not last:
+                    self.each_pair(a, lambda at: self.pair(a, at).wait_recv())
+            else:
+                y_at = self.y if last else 1 - self.y
+                self.load(a, y_at).wait()
+                self.pair(a, y_at).wait_recv()
+
+    def total(self, a, z_at, x_at, y_at, extra=()):
         here = self.work(a, z_at, x_at, y_at)
-        paired = self.paired[a].at[z_at * 2 + x_at, y_at]
-
-        def add(k, carry):
-            step = block_step(here, a, k)
-            value = step[...].astype(jnp.float32) + block_step(paired, a, k)[...].astype(jnp.float32)
-            for buffer in extra:
-                value = value + block_step(buffer, a, k)[...].astype(jnp.float32)
-            step[...] = value.astype(jnp.bfloat16)
-            return carry
-
-        lax.fori_loop(first, last, add, 0)
-
-    def diag_copy(self, a, z_at, part):
+        paired = self.piece(self.paired[a], a, z_at, x_at, y_at)
+
+        value = here[...] + paired[...]
+        for buffer in extra:
+            value = value + buffer[...]
+        here[...] = value
+
+    def diag_copy(self, a, z_at):
         n = self.number[a]
         return remote(
-            block_part(self.work(a, z_at, 1 - self.x, 1 - self.y), a, part),
-            block_part(self.step_one[a].at[z_at], a, part),
-            self.send.at[part, n, z_at],
-            self.one_got.at[n, part, z_at],
-            self.y_next if part == 0 else self.x_next,
+            self.work(a, z_at, 1 - self.x, 1 - self.y),
+            self.step_one[a].at[z_at],
+            self.send.at[0, n, z_at],
+            self.one_got.at[n, z_at],
+            self.y_next if a in BY_Y else self.x_next,
         )
 
     def diag(self, step):
         def act(z_at):
             for a in self.kinds:
-                self.ready(a, z_at, 1 - self.x, 1 - self.y)
-                self.total(a, z_at, 1 - self.x, 1 - self.y, 0, STEPS[a])
-                for part in range(2):
-                    self.diag_copy(a, z_at, part).start()
-
+                self.total(a, z_at, 1 - self.x, 1 - self.y)
+                self.diag_copy(a, z_at).start()
+
+        if step == self.depth - 1:
+            self.ready(False)
         self.sides(step, act)
 
     def x_copy(self, a, z_at):
@@ -860,18 +895,15 @@
 
         def act(z_at):
             for a in self.kinds:
-                middle, last = FIRST[a], STEPS[a]
-                self.ready(a, z_at, 1 - x, y)
-                self.diag_copy(a, z_at, 0).wait_recv()
-                self.total(a, z_at, 1 - x, y, 0, middle, [self.step_one[a].at[z_at]])
-                self.total(a, z_at, 1 - x, y, middle, last)
+                received = [self.step_one[a].at[z_at]]
+                self.diag_copy(a, z_at).wait_recv()
+                self.total(a, z_at, 1 - x, y, received if a in BY_Y else ())
                 self.x_copy(a, z_at).start()
-                self.ready(a, z_at, x, 1 - y)
-                self.diag_copy(a, z_at, 1).wait_recv()
-                self.total(a, z_at, x, 1 - y, 0, middle)
-                self.total(a, z_at, x, 1 - y, middle, last, [self.step_one[a].at[z_at]])
+                self.total(a, z_at, x, 1 - y, () if a in BY_Y else received)
                 self.y_copy(a, z_at).start()
 
+        if step == self.depth - 1:
+            self.ready(True)
         self.sides(step, act)
 
     def z_copy(self, a, z_at, side, target):
@@ -889,7 +921,6 @@
 
         def act(z_at):
             for a in self.kinds:
-                self.ready(a, z_at, x, y)
                 self.x_copy(a, z_at).wait_recv()
                 self.y_copy(a, z_at).wait_recv()
                 across = [self.from_x[a].at[z_at], self.from_y[a].at[z_at]]
@@ -901,11 +932,11 @@
                     @pl.when(before)
                     def _():
                         self.z_copy(a, z_at, side, self.sibling).wait_recv()
-                        self.total(a, z_at, x, y, 0, STEPS[a], across + [self.from_z[a].at[side, z_at]])
+                        self.total(a, z_at, x, y, across + [self.from_z[a].at[side, z_at]])
 
                     @pl.when(jnp.logical_not(before))
                     def _():
-                        self.total(a, z_at, x, y, 0, STEPS[a], across)
+                        self.total(a, z_at, x, y, across)
 
                     @pl.when(upward)
                     def _():
@@ -926,17 +957,17 @@
                         def _():
                             self.from_z[a][side, z] = jnp.zeros(BLOCKS[a], jnp.bfloat16)
 
-                    here, paired = self.work(a, z, x, y), self.paired[a].at[z * 2 + x, y]
+                    here, paired = self.work(a, z, x, y), self.piece(self.paired[a], a, z, x, y)
 
                     def finish(k, carry):
                         value = block_step(here, a, k)[...].astype(jnp.float32)
                         for buffer in [paired] + across + [self.from_z[a].at[0, z], self.from_z[a].at[1, z]]:
                             value = value + block_step(buffer, a, k)[...].astype(jnp.float32)
-                        if a == SQUARE:
-                            spare = self.outs[3]
+                        if a in SPANS:
+                            spare, at = self.outs[3], k + SPANS[a][0]
                             low, high = value[:, :192], pltpu.roll(value, 192, 1)[:, :192]
-                            self.outs[SQUARE][core, k] = jnp.where(core == 0, low, high)
-                            spare[k] = jnp.where(core == 0, high, low)
+                            self.outs[SQUARE][core, at] = jnp.where(core == 0, low, high)
+                            spare[at] = jnp.where(core == 0, high, low)
                         else:
                             block_step(self.outs[a], a, k)[...] = value
                         return carry
@@ -960,11 +991,7 @@
     def finish(self):
         def wait(z_at, carry):
             for a in self.kinds:
-                for x_at in range(2):
-                    for y_at in range(2):
-                        self.pair(a, z_at, x_at, y_at).wait_send()
-                for part in range(2):
-                    self.diag_copy(a, z_at, part).wait_send()
+                self.diag_copy(a, z_at).wait_send()
                 self.x_copy(a, z_at).wait_send()
                 self.y_copy(a, z_at).wait_send()
 
@@ -974,6 +1001,16 @@
             return carry
 
         lax.fori_loop(0, self.depth, wait, 0)
+        for a in self.kinds:
+            self.each_pair(a, lambda at: self.pair(a, at).wait_send())
+
+
+def pair_shape(a, depth):
+    if a == EXPAND:
+        return (2, depth * 192, 768)
+    if a == REDUCE:
+        return (2, 192, depth * 768)
+    return (2 * depth, SPANS[a][1], 48, 768)
 
 
 def reduction_scratch(kinds, depth):
@@ -981,15 +1018,16 @@
         return [pltpu.VMEM(lead + BLOCKS[a], jnp.bfloat16) for a in kinds]
 
     count = len(kinds)
-    spots = pltpu.SemaphoreType.DMA((count, 2 * depth, 2))
+    spots = pltpu.SemaphoreType.DMA((count, 2 * depth))
     return (
-        buffers(2 * depth, 2) + buffers(depth) + buffers(depth) + buffers(depth) + buffers(2, depth),
+        [pltpu.VMEM(pair_shape(a, depth), jnp.bfloat16) for a in kinds]
+        + buffers(depth) + buffers(depth) + buffers(depth) + buffers(2, depth),
         [
             spots,
             spots,
             spots,
             pltpu.SemaphoreType.DMA((5, count, depth)),
-            pltpu.SemaphoreType.DMA((count, 2, depth)),
+            pltpu.SemaphoreType.DMA((count, depth)),
             pltpu.SemaphoreType.DMA((count, depth)),
             pltpu.SemaphoreType.DMA((count, depth)),
             pltpu.SemaphoreType.DMA((count, 2, depth)),
@@ -1046,8 +1084,8 @@
     return jnp.concatenate([mask, mask], axis=0)
 
 
-def hot_rows(rank_ref, rows, tokens):
-    place = lax.broadcasted_iota(jnp.int32, (rows.size, tokens), 1)
+def hot_rows(rank_ref, rows, slots, first=0):
+    place = lax.broadcasted_iota(jnp.int32, (rows.size, slots), 1) + first
     return (rank_ref[rows, :1] == place).astype(jnp.float32).astype(jnp.bfloat16)
 
 
@@ -1176,31 +1214,22 @@
 
 
 def relayed_forward_kernel(depth, *refs):
-    ins, expand_in, reduce_in = refs[:8], refs[8], refs[9]
-    outs, expand_out, reduce_out = refs[10:21], refs[21], refs[22]
-    steps, expand_all, reduce_all = refs[23:27], refs[27], refs[28]
-    sems, save = refs[29:35], refs[35]
+    ins, expand_ref, reduce_in = refs[:8], refs[8], refs[9]
+    outs, reduce_out = refs[10:21], refs[21]
+    steps, reduce_all = refs[22:26], refs[26]
+    sems, save_sem = refs[27:33], refs[33]
     greet_neighbours(depth)
-    gather = Gather(
-        FEED_KINDS, depth, {EXPAND: expand_in, REDUCE: reduce_in}, {EXPAND: expand_all, REDUCE: reduce_all}, sems
-    )
-    gather.begin()
-
-    def saves():
-        return (
-            pltpu.make_async_copy(expand_all, expand_out, save.at[0]),
-            pltpu.make_async_copy(reduce_all, reduce_out, save.at[1]),
-        )
+    gather = Gather(LATER_KINDS, depth, {REDUCE: reduce_in}, {REDUCE: reduce_all}, sems)
+    gather.begin(LATER_KINDS)
+    save = pltpu.make_async_copy(reduce_all, reduce_out, save_sem)
 
     def before_feed():
         gather.arrive()
-        for copy in saves():
-            copy.start()
-
-    forward_steps(*ins, *outs, *steps, expand_all, reduce_all, gather.relays(), before_feed)
+        save.start()
+
+    forward_steps(*ins, *outs, *steps, expand_ref, reduce_all, gather.relays(), before_feed)
     gather.finish()
-    for copy in saves():
-        copy.wait()
+    save.wait()
 
 
 def forward_outs(tokens, seqs):
@@ -1234,7 +1263,7 @@
     )(*ins, expand, reduce_turned)
 
 
-def run_relayed_forward(ins, expand_piece, reduce_piece, call_id):
+def run_relayed_forward(ins, expand, reduce_piece, call_id):
     depth = lax.axis_size("dp") // 2
     tokens, seqs = ins[1].shape[0], ins[6].shape[0]
     weight = (768, 3072)
@@ -1243,18 +1272,18 @@
     anywhere = pl.BlockSpec(memory_space=pl.ANY)
     return pl.pallas_call(
         functools.partial(relayed_forward_kernel, depth),
-        out_shape=outs + [jax.ShapeDtypeStruct(weight, jnp.bfloat16)] * 2,
+        out_shape=outs + [jax.ShapeDtypeStruct(weight, jnp.bfloat16)],
         in_specs=[whole] * (len(ins) + 2),
-        out_specs=[whole] * len(outs) + [anywhere] * 2,
+        out_specs=[whole] * len(outs) + [anywhere],
         scratch_shapes=forward_scratch(tokens, seqs)
-        + [pltpu.VMEM(weight, jnp.bfloat16)] * 2
-        + gather_sems(FEED_KINDS, depth)
-        + [pltpu.SemaphoreType.DMA((2,))],
+        + [pltpu.VMEM(weight, jnp.bfloat16)]
+        + gather_sems(LATER_KINDS, depth)
+        + [pltpu.SemaphoreType.DMA],
         compiler_params=pltpu.CompilerParams(
             collective_id=call_id, has_side_effects=True, vmem_limit_bytes=VMEM_CAP
         ),
         name="layer_forward",
-    )(*ins, expand_piece, reduce_piece)
+    )(*ins, expand, reduce_piece)
 
 
 def norm_back_rows(values, gain, grad):
@@ -1268,7 +1297,7 @@
 def feed_back_kernel(
     grad_embed_ref, embed_ref, inverse_ref, pool_ref, length_ref, last_ref, middle_ref, ending_ref, expand_ref,
     reduce_ref, gains_ref,
-    grad_expand_ref, grad_reduce_ref, grad_middle_ref, grad_low_ref, grad_proj_ref, grad_gains_ref,
+    grad_expand_ref, grad_reduce_ref, grad_middle_ref, grad_proj_ref, grad_gains_ref,
     normed, normed_turned, end_low, end_turned, back,
 ):
     tokens = middle_ref.shape[0]
@@ -1319,9 +1348,7 @@
         rows = rows_at(r, 256)
         through, gain = norm_back_rows(middle_ref[rows, :], gains_ref[1:2], back[rows, :])
         grad_gains_ref[1:2] += gain
-        grad_middle = grad_middle_ref[rows, :] + through
-        grad_middle_ref[rows, :] = grad_middle
-        grad_low_ref[rows, :] = grad_middle.astype(jnp.bfloat16)
+        grad_middle_ref[rows, :] += through
         return carry
 
     lax.fori_loop(0, tokens // 256, end, 0)
@@ -1339,14 +1366,13 @@
             jax.ShapeDtypeStruct(expand.shape, low),
             jax.ShapeDtypeStruct(reduce_turned.shape, low),
             jax.ShapeDtypeStruct((tokens, D), jnp.float32),
-            jax.ShapeDtypeStruct((tokens, D), low),
             jax.ShapeDtypeStruct((seqs, D), low),
             jax.ShapeDtypeStruct((8, D), jnp.float32),
         ],
         in_specs=[whole] * 5
         + [pl.BlockSpec((1, D, D), lambda i: (4, 0, 0))]
         + [whole] * 5,
-        out_specs=[whole] * 6,
+        out_specs=[whole] * 5,
         scratch_shapes=[
             pltpu.VMEM((tokens, D), low),
             pltpu.VMEM((D, tokens), low),
@@ -1360,10 +1386,10 @@
 
 
 def attend_back_steps(
-    grad_middle_ref, grad_low_ref, grad_proj_ref, pooled_ref, start_ref, query_ref, key_ref, value_ref, mixed_ref,
+    grad_middle_ref, grad_proj_ref, pooled_ref, start_ref, query_ref, key_ref, value_ref, mixed_ref,
     square_ref, gains_ref, bias_ref, mask_ref, rank_ref,
     grad_square_ref, grad_score_ref, grad_gain_ref, grad_mixed, turned, grad_query, grad_key, grad_value,
-    between, squares_done, put,
+    turned_half, between, early_done, squares_done, put,
 ):
     tokens = start_ref.shape[0]
     big = 512
@@ -1371,7 +1397,9 @@
 
     def begin(r, carry):
         rows = rows_at(r, big)
-        grad_mixed[rows, :] = dot_nt(grad_low_ref[rows, :], square_ref[3]).astype(jnp.bfloat16)
+        grad_mixed[rows, :] = dot_nt(grad_middle_ref[rows, :].astype(jnp.bfloat16), square_ref[3]).astype(
+            jnp.bfloat16
+        )
         turned[:, rows] = mixed_ref[rows, :].astype(jnp.float32).T.astype(jnp.bfloat16)
         return carry
 
@@ -1380,12 +1408,15 @@
     def outer(target, right_ref):
         def part(r, carry):
             rows = rows_at(r, 384)
-            grad_square_ref[target, rows, :] = dot_nn(turned[rows, :], right_ref[...]).astype(jnp.bfloat16)
+            grad_square_ref[target, rows, :] = dot_nn(turned[rows, :], right_ref[...].astype(jnp.bfloat16)).astype(
+                jnp.bfloat16
+            )
             return carry
 
         lax.fori_loop(0, D // 384, part, 0)
 
-    outer(3, grad_low_ref)
+    outer(3, grad_middle_ref)
+    early_done()
     grad_score_ref[...] = jnp.zeros_like(grad_score_ref)
 
     def attend(t, carry):
@@ -1410,14 +1441,52 @@
         return carry
 
     tiles = tokens // TILE
-    done = 0
-    for n, act in enumerate(between):
-        until = ((n + 1) * tiles) // (len(between) + 1)
-        if until > done:
-            lax.fori_loop(done, until, attend, 0)
-        done = until
-        act()
-    lax.fori_loop(done, tiles, attend, 0)
+    between = list(between)
+    part = tokens // 2
+
+    def relay(place, number):
+        for spot_name, spot_number, act in between:
+            if (spot_name, spot_number) == (place, number):
+                act()
+
+    grad_gain_ref[...] = jnp.zeros_like(grad_gain_ref)
+
+    def attend_half(half):
+        for t in range(half * tiles // 2, (half + 1) * tiles // 2):
+            lax.fori_loop(t, t + 1, attend, 0)
+            relay("tile", t)
+
+    def end_half(half):
+        def end(r, carry):
+            rows = pl.ds(pl.multiple_of(half * part + r * 256, 256), 256)
+            grad_normed = (
+                dot_nt(grad_query[rows, :], square_ref[0])
+                + dot_nt(grad_key[rows, :], square_ref[1])
+                + dot_nt(grad_value[rows, :], square_ref[2])
+            )
+            through, gain = norm_back_rows(start_ref[rows, :].astype(jnp.float32), gains_ref[0:1], grad_normed)
+            grad_gain_ref[0:1] += gain
+            turned_half[:, rows_at(r, 256)] = (grad_middle_ref[rows, :] + through).T.astype(jnp.bfloat16)
+            return carry
+
+        lax.fori_loop(0, part // 256, end, 0)
+
+        def merge(r, carry):
+            rows = rows_at(r, 384)
+            total = jnp.zeros((384, part), jnp.float32)
+            for c in range(part // 256):
+                hot = hot_rows(rank_ref, pl.ds(half * part + c * 256, 256), part, half * part)
+                total = total + dot_nn(turned_half[rows, c * 256 : (c + 1) * 256], hot)
+            put(half, r, total)
+            return carry
+
+        lax.fori_loop(0, D // 384, merge, 0)
+        put(half, None, None)
+
+    attend_half(0)
+    end_half(0)
+    relay("end", 0)
+    attend_half(1)
 
     def renorm(r, carry):
         rows = rows_at(r, 256)
@@ -1426,46 +1495,31 @@
         return carry
 
     lax.fori_loop(0, tokens // 256, renorm, 0)
+    relay("norm", 0)
     outer(0, grad_query)
+    relay("outer", 0)
     outer(1, grad_key)
+    relay("outer", 1)
     outer(2, grad_value)
     squares_done()
-    grad_gain_ref[...] = jnp.zeros_like(grad_gain_ref)
-
-    def end(r, carry):
-        rows = rows_at(r, 256)
-        grad_normed = (
-            dot_nt(grad_query[rows, :], square_ref[0])
-            + dot_nt(grad_key[rows, :], square_ref[1])
-            + dot_nt(grad_value[rows, :], square_ref[2])
-        )
-        through, gain = norm_back_rows(start_ref[rows, :].astype(jnp.float32), gains_ref[0:1], grad_normed)
-        grad_gain_ref[0:1] += gain
-        turned[:, rows] = (grad_middle_ref[rows, :] + through).T.astype(jnp.bfloat16)
-        return carry
-
-    lax.fori_loop(0, tokens // 256, end, 0)
-
-    def merge(r, carry):
-        rows = rows_at(r, 384)
-        total = jnp.zeros((384, tokens), jnp.float32)
-        for c in range(tokens // 256):
-            at = pl.ds(c * 256, 256)
-            total = total + dot_nn(turned[rows, at], hot_rows(rank_ref, at, tokens))
-        put(r, total)
-        return carry
-
-    lax.fori_loop(0, D // 384, merge, 0)
+    relay("outer", 2)
+    end_half(1)
+    relay("end", 1)
 
 
 def attend_back_kernel(*refs):
-    ins, rest = refs[:14], refs[14:]
+    ins, rest = refs[:13], refs[13:]
     grad_square_ref, grad_score_ref, grad_gain_ref, send_ref = rest[:4]
 
-    def put(r, total):
-        send_ref[rows_at(r, 384), :] = total.astype(jnp.bfloat16)
-
-    attend_back_steps(*ins, grad_square_ref, grad_score_ref, grad_gain_ref, *rest[4:], [], lambda: None, put)
+    def put(half, r, total):
+        if r is not None:
+            part = total.shape[1]
+            send_ref[rows_at(r, 384), half * part : (half + 1) * part] = total.astype(jnp.bfloat16)
+
+    nothing = lambda: None
+    attend_back_steps(
+        *ins, grad_square_ref, grad_score_ref, grad_gain_ref, *rest[4:], [], nothing, nothing, put
+    )
 
 
 def attend_scratch(tokens):
@@ -1476,6 +1530,7 @@
         pltpu.VMEM((tokens, D), low),
         pltpu.VMEM((tokens, D), low),
         pltpu.VMEM((tokens, D), low),
+        pltpu.VMEM((D, tokens // 2), low),
     ]
 
 
@@ -1496,20 +1551,28 @@
     )(*ins)
 
 
-BACK_CAP = 62 * 1024 * 1024
+BACK_CAP = 64 * 1024 * 1024 - 128 * 1024
+
+
+HIGH = 32
+SEGMENTS = 8
+EARLY_PLAN = (("tile", 3), ("outer", 0), ("end", 1), ("dense", 1), ("dense", 3), ("dense", 5))
+LATE_PLAN = (("dense", 6), ("dense", 7), ("dense", 9), ("dense", 11), ("dense", 13), ("dense", 15))
 
 
 def back_kernel(depth, *refs):
-    ins, refs = refs[:14], refs[14:]
-    grad_expand, grad_reduce = refs[:2]
-    square_sum, expand_sum, reduce_sum, grad_score_ref, grad_gain_ref, returned = refs[2:8]
-    grad_square, *steps = refs[8:14]
-    blocks, spare, work_expand, work_reduce = refs[14:18]
-    refs = refs[18:]
-    feed_buffers, refs = refs[:10], refs[10:]
-    feed_sems, refs = refs[:8], refs[8:]
-    square_buffers, refs = refs[:5], refs[5:]
-    square_sems, refs = refs[:8], refs[8:]
+    ins, refs = refs[:13], refs[13:]
+    keys_ref, grad_expand, grad_reduce = refs[:3]
+    square_sum, expand_sum, reduce_sum, grad_score_ref, grad_gain_ref, squares_ref, table_ref = refs[3:10]
+    grad_square, *steps = refs[10:17]
+    blocks, spare, work_expand, work_reduce, returned, places = refs[17:23]
+    refs = refs[23:]
+    turned = steps[1]
+    count_first, count_last = 5 * len(FIRST_KINDS), 5 * len(LAST_KINDS)
+    first_buffers, refs = refs[:count_first], refs[count_first:]
+    first_sems, refs = refs[:8], refs[8:]
+    last_buffers, refs = refs[:count_last], refs[count_last:]
+    last_sems, refs = refs[:8], refs[8:]
     part_send, part_got, part_own, end_send, end_got = refs
     dp_size, fsdp_size = lax.axis_size("dp"), lax.axis_size("fsdp")
     count = dp_size * fsdp_size
@@ -1517,11 +1580,11 @@
     greet_all(count, fsdp_size, me)
     grads = (grad_square, grad_expand, grad_reduce)
     outs = (square_sum, expand_sum, reduce_sum, spare)
-    feed = Reduction(
-        FEED_KINDS, depth, grads, outs, {EXPAND: work_expand, REDUCE: work_reduce}, feed_buffers, feed_sems
-    )
-    square = Reduction(SQUARE_KINDS, depth, grads, outs, None, square_buffers, square_sems)
-    feed.begin()
+    work = {EXPAND: work_expand, REDUCE: work_reduce}
+    early = Reduction(FIRST_KINDS, depth, grads, outs, work, first_buffers, first_sems)
+    late = Reduction(LAST_KINDS, depth, grads, outs, work, last_buffers, last_sems)
+    early.begin((EXPAND, REDUCE))
+    early_groups, late_groups = list(early.groups()), list(late.groups())
 
     def relay(group):
         def act():
@@ -1530,63 +1593,135 @@
 
         return act
 
-    feats, half = blocks.shape[1] // 2, blocks.shape[2]
-
-    def put(r, total):
+    feats, quarter = blocks.shape[2] // 2, blocks.shape[3]
+
+    def part_copy(half, k):
+        target = lax.rem(me + k, count)
+        device = (target // fsdp_size, lax.rem(target, fsdp_size))
+        return remote(
+            blocks.at[half, target], returned.at[half, me], part_send.at[half, k], part_got.at[half, k], device
+        )
+
+    def own_part(half):
+        return pltpu.make_async_copy(blocks.at[half, me], returned.at[half, me], part_own.at[half])
+
+    def put(half, r, total):
+        if r is None:
+
+            def start_part(k, carry):
+                part_copy(half, k).start()
+                return carry
+
+            lax.fori_loop(1, count, start_part, 0)
+            own_part(half).start()
+            return
         each = 384 // feats
         for p in range(each):
             part = total[p * feats : (p + 1) * feats]
-            blocks[r * each + p] = jnp.concatenate([part[:, :half], part[:, half:]], axis=0).astype(jnp.bfloat16)
+            blocks[half, r * each + p] = jnp.concatenate(
+                [part[:, :quarter], part[:, quarter:]], axis=0
+            ).astype(jnp.bfloat16)
 
     attend_back_steps(
         *ins, grad_square, grad_score_ref, grad_gain_ref, *steps,
-        [relay(group) for group in feed.groups()], square.begin, put,
+        [(*place_at, relay(group)) for place_at, group in zip(EARLY_PLAN, early_groups)],
+        lambda: early.begin((EARLY,)),
+        lambda: late.begin((LATE,)),
+        put,
     )
 
-    def part_copy(k):
-        target = lax.rem(me + k, count)
-        return pltpu.make_async_remote_copy(
-            src_ref=blocks.at[target],
-            dst_ref=returned.at[me],
-            send_sem=part_send.at[k],
-            recv_sem=part_got.at[k],
-            device_id=(target // fsdp_size, lax.rem(target, fsdp_size)),
-            device_id_type=MESH,
-        )
-
-    def start_part(k, carry):
-        part_copy(k).start()
-        return carry
-
-    lax.fori_loop(1, count, start_part, 0)
-    own_part = pltpu.make_async_copy(blocks.at[me], returned.at[me], part_own)
-    own_part.start()
-    for group in square.groups():
-        relay(group)()
-    end_copy = remote(spare, square_sum.at[square.core], end_send, end_got, square.sibling)
-    end_copy.start()
-    feed.finish()
-    square.finish()
-    end_copy.wait_send()
-    remote(spare, square_sum.at[1 - square.core], end_send, end_got, square.sibling).wait_recv()
-    own_part.wait()
-
-    def end_part(k, carry):
-        part_copy(k).wait()
-        return carry
-
-    lax.fori_loop(1, count, end_part, 0)
-
-
-def run_back(ins, grad_expand, grad_reduce, count, feats, call_id):
+    def end_copy(number, kind, of):
+        span = pl.ds(*SPANS[kind])
+        return remote(
+            spare.at[span], square_sum.at[of, span], end_send.at[number], end_got.at[number], early.sibling
+        )
+
+    core = early.core
+    table_ref[...] = jnp.zeros_like(table_ref)
+    vocab = table_ref.shape[1]
+    batch = 2
+    segments = 4
+    slots = 2 * quarter
+    lines = slots // LANES
+
+    def add_rows(half, n, carry):
+        for b in range(batch):
+            k = n * batch + b
+
+            @pl.when(k > 0)
+            def _():
+                part_copy(half, k).wait_recv()
+
+            source = lax.rem(me + count - k, count)
+            block = returned[half, source].astype(jnp.float32)
+            keys = keys_ref[source]
+            for c in range(lines):
+                key = keys[half * lines + c : half * lines + c + 1]
+                number = (key >> 2) + (key & 3) * fold_rows(vocab)
+                at = pl.ds(b * slots + c * LANES, LANES)
+                places[0:1, at] = number & 1023
+                first = 0 if c < lines // 2 else feats
+                low = (c % (lines // 2)) * LANES
+                piece = block[first : first + feats, low : low + LANES]
+                high = number >> 10
+                spread = [jnp.where(high == g, piece, 0.0) for g in range(HIGH)]
+                turned[:, at] = jnp.concatenate(spread, axis=0).astype(jnp.bfloat16)
+        for w in range(4):
+            window = 256
+            row = lax.broadcasted_iota(jnp.int32, (window, batch * slots), 0) + w * window
+            hot = (row == places[0:1]).astype(jnp.float32).astype(jnp.bfloat16)
+            total = dot_nt(turned[...], hot)
+            for g in range(HIGH):
+                start = g * 1024 + w * window
+                width = min(window, vocab - start)
+                if width > 0:
+                    table_ref[:, start : start + width] += total[g * feats : (g + 1) * feats, :width]
+        return carry
+
+    plan = list(zip(EARLY_PLAN, early_groups)) + list(zip(LATE_PLAN, late_groups))
+    for half in range(2):
+        own_part(half).wait()
+        each = count // batch // SEGMENTS
+        for segment in range(SEGMENTS):
+            lax.fori_loop(segment * each, (segment + 1) * each, functools.partial(add_rows, half), 0)
+            for place_at, group in plan:
+                if place_at == ("dense", half * SEGMENTS + segment):
+                    relay(group)()
+                    if group is early_groups[-1]:
+                        end_copy(0, EARLY, core).start()
+    end_copy(1, LATE, core).start()
+    early.finish()
+    late.finish()
+    for number, kind in enumerate((EARLY, LATE)):
+        end_copy(number, kind, core).wait_send()
+        end_copy(number, kind, 1 - core).wait_recv()
+    squares = jnp.zeros((1, 1), jnp.float32)
+    for sums in (square_sum, expand_sum, reduce_sum):
+        value = sums[...].reshape(-1, sums.shape[-1])
+        squares = squares + jnp.sum(value * value, keepdims=True)
+    for g in range(HIGH):
+        value = table_ref[:, g * 1024 : min(vocab, (g + 1) * 1024)]
+        squares = squares + jnp.sum(value * value, keepdims=True)
+    squares_ref[...] = jnp.broadcast_to(squares, squares_ref.shape)
+    for half in range(2):
+
+        def end_part(k, carry):
+            part_copy(half, k).wait_send()
+            return carry
+
+        lax.fori_loop(1, count, end_part, 0)
+
+
+def run_back(ins, keys, grad_expand, grad_reduce, feats, vocab, call_id):
     depth = lax.axis_size("dp") // 2
     tokens = ins[0].shape[0]
     low = jnp.bfloat16
-    blocks = (count, 2 * feats, tokens // 2)
+    count = keys.shape[0]
+    blocks = (2, count, 2 * feats, tokens // 4)
     whole = pl.BlockSpec(memory_space=pltpu.VMEM)
     anywhere = pl.BlockSpec(memory_space=pl.ANY)
-    feed_buffers, feed_sems = reduction_scratch(FEED_KINDS, depth)
-    square_buffers, square_sems = reduction_scratch(SQUARE_KINDS, depth)
+    first_buffers, first_sems = reduction_scratch(FIRST_KINDS, depth)
+    last_buffers, last_sems = reduction_scratch(LAST_KINDS, depth)
     return pl.pallas_call(
         functools.partial(back_kernel, depth),
         out_shape=[
@@ -1595,44 +1730,43 @@
             jax.ShapeDtypeStruct((192, 384), jnp.float32),
             jax.ShapeDtypeStruct((HEADS, TILE, TILE), jnp.float32),
             jax.ShapeDtypeStruct((8, D), jnp.float32),
-            jax.ShapeDtypeStruct(blocks, low),
+            jax.ShapeDtypeStruct((8, LANES), jnp.float32),
+            jax.ShapeDtypeStruct((feats, vocab), jnp.float32),
         ],
         in_specs=[whole] * 14 + [anywhere] * 2,
-        out_specs=[whole] * 5 + [anywhere],
+        out_specs=[whole] * 7,
         scratch_shapes=[pltpu.VMEM((5, D, D), low)]
         + attend_scratch(tokens)
         + [
             pltpu.VMEM(blocks, low),
             pltpu.VMEM((5, 48, 192), jnp.float32),
-            pltpu.VMEM((2 * depth, 2) + BLOCKS[EXPAND], low),
-            pltpu.VMEM((2 * depth, 2) + BLOCKS[REDUCE], low),
+            pltpu.VMEM(pair_shape(EXPAND, depth), low),
+            pltpu.VMEM(pair_shape(REDUCE, depth), low),
+            pltpu.VMEM(blocks, low),
+            pltpu.VMEM((8, tokens), jnp.int32),
         ]
-        + feed_buffers
-        + feed_sems
-        + square_buffers
-        + square_sems
+        + first_buffers
+        + first_sems
+        + last_buffers
+        + last_sems
         + [
-            pltpu.SemaphoreType.DMA((count,)),
-            pltpu.SemaphoreType.DMA((count,)),
-            pltpu.SemaphoreType.DMA,
-            pltpu.SemaphoreType.DMA,
-            pltpu.SemaphoreType.DMA,
+            pltpu.SemaphoreType.DMA((2, count)),
+            pltpu.SemaphoreType.DMA((2, count)),
+            pltpu.SemaphoreType.DMA((2,)),
+            pltpu.SemaphoreType.DMA((2,)),
+            pltpu.SemaphoreType.DMA((2,)),
         ],
         compiler_params=pltpu.CompilerParams(
             collective_id=call_id, has_side_effects=True, vmem_limit_bytes=BACK_CAP
         ),
         name="back",
-    )(*ins, grad_expand, grad_reduce)
-
-
-def loss_kernel(
-    query_rows, nli_rows, embeds_ref, negative_ref, scale_ref, grad_ref, stats_ref, everyone, grad_sims, turned_sims,
-    send, got, hand_send, hand_got,
-):
+    )(*ins, keys, grad_expand, grad_reduce)
+
+
+def share_chips(own_ref, everyone, send, got, hand_send, hand_got):
     dp_size, fsdp_size = lax.axis_size("dp"), lax.axis_size("fsdp")
     count = dp_size * fsdp_size
     chips = count // 2
-    slots = embeds_ref.shape[0]
     dp, fsdp = lax.axis_index("dp"), lax.axis_index("fsdp")
     me = dp * fsdp_size + fsdp
     core = lax.rem(fsdp, 2)
@@ -1645,7 +1779,7 @@
 
     def across(k):
         target = lax.rem(chip + k, chips) * 2 + core
-        return remote(embeds_ref, everyone.at[me], send.at[k], got.at[k], device(target))
+        return remote(own_ref, everyone.at[me], send.at[k], got.at[k], device(target))
 
     def hand(k, of):
         source = lax.rem(chip + chips - k, chips) * 2 + of
@@ -1666,15 +1800,67 @@
         hand(k, 1 - core).wait_recv()
         return carry
 
-    first = remote(embeds_ref, everyone.at[me], hand_send.at[0], hand_got.at[0], sibling)
+    first = remote(own_ref, everyone.at[me], hand_send.at[0], hand_got.at[0], sibling)
     first.start()
-    everyone[me] = embeds_ref[...]
+    everyone[me] = own_ref[...]
     lax.fori_loop(1, chips, start, 0)
     lax.fori_loop(1, chips, relay, 0)
     lax.fori_loop(1, chips, end, 0)
     first.wait_send()
     hand(0, 1 - core).wait_recv()
-
+    return me
+
+
+def total_kernel(
+    first_gain, late_gains, position_ref, table_squares, layer_squares, scale_ref, total_ref, norm_ref, tile,
+    everyone, send, got, hand_send, hand_got,
+):
+    gains = first_gain[...] + late_gains[...]
+    rows = [jnp.sum(table_squares[...], axis=0, keepdims=True), layer_squares[0:1]]
+    rows += [position_ref[k : k + 1] for k in range(3)]
+    for k in range(3):
+        rows += [gains[k : k + 1, c * LANES : (c + 1) * LANES] for c in range(D // LANES)]
+    rows.append(jnp.zeros((tile.shape[0] - len(rows), LANES), jnp.float32))
+    tile[...] = jnp.concatenate(rows, axis=0)
+    share_chips(tile, everyone, send, got, hand_send, hand_got)
+
+    def add(k, total):
+        return total + everyone[k]
+
+    total = lax.fori_loop(1, everyone.shape[0], add, everyone[0])
+    total_ref[...] = total
+    row = lax.broadcasted_iota(jnp.int32, total.shape, 0)
+    lane = lax.broadcasted_iota(jnp.int32, total.shape, 1)
+    squares = jnp.where(row == 0, total, jnp.where(row == 1, jnp.where(lane == 0, total, 0.0), total * total))
+    norm = jnp.sqrt(jnp.sum(squares, keepdims=True) + scale_ref[...] * scale_ref[...])
+    norm_ref[...] = jnp.broadcast_to(norm, norm_ref.shape)
+
+
+def run_total(first_gain, late_gains, position, table_squares, layer_squares, grad_scale, call_id):
+    count = lax.axis_size("dp") * lax.axis_size("fsdp")
+    few = pltpu.SemaphoreType.DMA((count // 2,))
+    return pl.pallas_call(
+        total_kernel,
+        out_shape=[jax.ShapeDtypeStruct((24, LANES), jnp.float32), jax.ShapeDtypeStruct((8, LANES), jnp.float32)],
+        scratch_shapes=[
+            pltpu.VMEM((24, LANES), jnp.float32),
+            pltpu.VMEM((count, 24, LANES), jnp.float32),
+            few, few, few, few,
+        ],
+        compiler_params=pltpu.CompilerParams(
+            collective_id=call_id, has_side_effects=True, vmem_limit_bytes=VMEM_CAP
+        ),
+        name="total",
+    )(first_gain, late_gains, position, table_squares, layer_squares, grad_scale)
+
+
+def loss_kernel(
+    query_rows, nli_rows, embeds_ref, negative_ref, scale_ref, grad_ref, stats_ref, everyone, grad_sims, turned_sims,
+    send, got, hand_send, hand_got,
+):
+    count = everyone.shape[0]
+    slots = embeds_ref.shape[0]
+    me = share_chips(embeds_ref, everyone, send, got, hand_send, hand_got)
     total_rows = count * slots
     embeds = everyone[...].reshape(total_rows, D)
     scale = jnp.exp(scale_ref[...])
@@ -1809,8 +1995,8 @@
     half = token_count // 2
     if direct:
         square_pieces = square_low.reshape(5, 2, 48, 192).transpose(1, 0, 2, 3)
-        found, square_all, info_all, gains_all = run_front(
-            info, own_gains, token_count, embed_table, square_pieces, 1
+        found, square_all, expand_all, info_all, gains_all = run_front(
+            info, own_gains, token_count, embed_table, square_pieces, expand_low, 1
         )
     else:
         info_all = exchange(info[None], True, 0, "share_keys")
@@ -1860,7 +2046,7 @@
 
     forward_ins = (found, rank_rows, square_all, gains, bias, mask, pool, length_rows)
     if direct:
-        *forward_all, expand_all, reduce_all = run_relayed_forward(forward_ins, expand_low, reduce_low, 2)
+        *forward_all, reduce_all = run_relayed_forward(forward_ins, expand_all, reduce_low, 2)
     else:
         forward_all = run_forward(forward_ins, expand_all, reduce_all)
     (start, queries, keys_here, values_here, mixed, middle, ending, embeds_low, pooled, embeds, inverse) = forward_all
@@ -1919,17 +2105,18 @@
         )
         losses = jnp.stack([first_loss, second_loss])
         grad_scale = ((first_dscale + second_dscale) * scale).reshape(1)
-    (grad_expand, grad_reduce, grad_middle, grad_middle_low, grad_proj, late_gains) = run_feed_back(
+    (grad_expand, grad_reduce, grad_middle, grad_proj, late_gains) = run_feed_back(
         grad_embeds, embeds, inverse, pool, length_rows, square_all, middle, ending, expand_all, reduce_all, gains
     )
     back_ins = (
-        grad_middle, grad_middle_low, grad_proj, pooled, start, queries, keys_here, values_here, mixed, square_all,
+        grad_middle, grad_proj, pooled, start, queries, keys_here, values_here, mixed, square_all,
         gains, bias, mask, rank_rows,
     )
     if direct:
-        (square_sum, expand_sum, reduce_sum, grad_scores, first_gain, returned) = run_back(
-            back_ins, grad_expand, grad_reduce, count, feats, 5
-        )
+        (square_sum, expand_sum, reduce_sum, grad_scores, first_gain, layer_squares, grad_table) = run_back(
+            back_ins, info_all, grad_expand, grad_reduce, feats, vocab_size, 5
+        )
+        table_squares = jnp.zeros((8, LANES), jnp.float32)
         square_sum = square_sum.transpose(1, 0, 2, 3).reshape(5, 96, 192)
     else:
 
@@ -1944,37 +2131,36 @@
         square_sum = shard(grad_square, "dp", "fsdp")
         expand_sum = shard(grad_expand, "dp", "fsdp")
         reduce_sum = shard(grad_reduce, "fsdp", "dp")
-        merged = merged.reshape(count, feats, 2, half).transpose(0, 2, 1, 3)
+        layer_squares = jnp.full(
+            (8, LANES), sum(jnp.sum(part * part) for part in (square_sum, expand_sum, reduce_sum)), jnp.float32
+        )
+        merged = merged.reshape(count, feats, 2, 2, half // 2).transpose(2, 0, 3, 1, 4)
         if feats_pad > feats:
-            merged = jnp.pad(merged, ((0, 0), (0, 0), (0, feats_pad - feats), (0, 0)))
-        returned = exchange(merged.reshape(count, 2 * feats_pad, half), False, 4, "send_gradients")
-    grad_table = scatter(returned, row_all, group_all, vocab_size)[:feats]
-    grad_gains = jnp.concatenate([first_gain[:1], late_gains[1:3]], axis=0)
+            merged = jnp.pad(merged, ((0, 0), (0, 0), (0, 0), (0, feats_pad - feats), (0, 0)))
+        merged = merged.reshape(2, count, 2 * feats_pad, half // 2)
+        returned = jnp.stack(
+            [exchange(merged[n], False, 9 + n, ("send_early", "send_late")[n]) for n in range(2)]
+        )
+        grad_table, table_squares = scatter(returned, row_all, group_all, vocab_size)
+        grad_table = grad_table[:feats]
     grad_position = lax.dot_general(
         onehot, grad_scores.reshape(HEADS, TILE * TILE), (((0,), (1,)), ((), ())), precision=HIGHEST
     )
     reduced = (square_sum, expand_sum, reduce_sum.T)
-    local_square = (
-        jnp.sum(reduced[0] * reduced[0])
-        + jnp.sum(reduced[1] * reduced[1])
-        + jnp.sum(reduce_sum * reduce_sum)
-        + jnp.sum(grad_table * grad_table)
+    total, norm = run_total(
+        first_gain,
+        late_gains,
+        grad_position.reshape(-1, LANES),
+        table_squares,
+        layer_squares,
+        grad_scale.reshape(1, 1),
+        7,
     )
-    small = jnp.concatenate([grad_gains.reshape(-1), grad_position.reshape(-1), local_square.reshape(1)])
-    small_rows = -(-small.shape[0] // (8 * LANES)) * 8
-    small = jnp.pad(small, (0, small_rows * LANES - small.shape[0])).reshape(1, small_rows, LANES)
-    summed = jnp.sum(exchange(small, True, 7, "share_small"), axis=0).reshape(-1)
-    gains_total = summed[: 3 * D].reshape(3, D)
-    position_total = summed[3 * D : 3 * D + BUCKETS * HEADS].reshape(BUCKETS, HEADS)
-    square_total = summed[3 * D + BUCKETS * HEADS]
+    position_total = total[2:5].reshape(BUCKETS, HEADS)
+    gains_total = total[5:23].reshape(3, D)
     scale_total = grad_scale
+    gradient_norm = norm[0, 0]
     grad_gain_shard = lax.dynamic_slice_in_dim(gains_total, position * feats, feats, 1)
-    gradient_norm = jnp.sqrt(
-        square_total
-        + jnp.sum(gains_total * gains_total)
-        + jnp.sum(position_total * position_total)
-        + jnp.sum(scale_total * scale_total)
-    )
     factor = jnp.minimum(1.0, CLIP_NORM / gradient_norm)
     table_out = adam_update(embed_table, table_moment, table_second, grad_table, factor, TABLE_RATE)
     square_out = adam_update(

time: 511 us -> 450 us (0.88)
  the two profiles are of different devices: /device:TPU:15 before, /device:TPU:0 now
where the time goes in v6:
time: 450 us; the launch traced here: 441 us
  Pallas kernels  385 us (86%)
  other arithmetic  27.7 us (6%)
  local copies, waits for them, and re-layouts  16.6 us (4%)
  between operations  8.23 us (2%)
    pallas_call x1, Pallas kernels, run_back(): pl.pallas_call(functools.partial(back_kernel, depth), out_shape=[jax.Shap...  158 us
    pallas_call x1, Pallas kernels, run_front(): pl.pallas_call(functools.partial(front_kernel, fold, depth), out_shape=[j...  84.2 us
    pallas_call x1, Pallas kernels, run_relayed_forward(): pl.pallas_call(functools.partial(relayed_forward_kernel, depth), out_shap...  61.3 us
    pallas_call x1, Pallas kernels, run_feed_back(): pl.pallas_call(feed_back_kernel, grid=(1,), out_shape=[jax.ShapeDtypeStru...  51.9 us
    pallas_call x1, Pallas kernels, run_total(): pl.pallas_call(total_kernel, out_shape=[jax.ShapeDtypeStruct((24, LANES),...  15.4 us
    pallas_call x1, Pallas kernels, run_loss(): pl.pallas_call(functools.partial(loss_kernel, query_rows, nli_rows), out_...  14.2 us
    sub x6, other arithmetic, adam_update(): weight - rate * (moment_hat / (jnp.sqrt(second_hat) + ADAM_EPS) + WEIGHT_...  13.6 us

profile of v6, /device:TPU:0, one launch (start us, length us, event | category | flops | bytes accessed | tf_op | source)
XLA Modules:
  0.0 440.6 jit_solution(9877294654226230679)
XLA Ops:
  0.7 0.8 pad_add_fusion
  2.3 1.9 fusion.1
  4.1 1.4 convert_reduce_fusion
  5.5 1.1 select_reduce_fusion
  8.1 1.1 convert_element_type.33
  9.1 0.7 copy.101
  9.9 1.6 convert_element_type.34.expand_in
  11.5 1.3 pad.23.gains_ref
  12.8 84.2 %front.1 = (bf16[32,48,512]{2,1,0:T(8,128)(2,1)}, bf16[5,768,768]{2,1,0:T(8,128)(2,1)}, bf16[768,3072]{1,0:T(8,128)(2,1)}, s32[32,16,128]{2,1,0:T(8,128)}, f32[32,8,128]{2,1,0:T(8,128)}) custom-call(s32[16,128]{1,0:T(8,128)} %add_add_fusion.keys_ref, f32[8,128]{1,0:T(8,128)} %pad.23.gains_ref, f32[24,32128]{1,0:T(8,128)} %table_ref.1, ...), custom_call_target="tpu_custom_call" | custom-call | tf_op jit(solution)/shard_map/front/pallas_call | solution.py:720
  97.0 0.9 fusion.12
  98.6 1.0 broadcast_in_dim.39.refs_1_.refs_12_
  99.7 0.7 fusion.10
  100.4 0.9 and_select_fusion.refs_5_.refs_11_
  102.0 1.2 fusion.28
  103.4 0.9 bitcast_bitcast_fusion.refs_4_.refs_10_
  105.0 61.3 %layer_forward.1 = (bf16[1024,768]{1,0:T(8,128)(2,1)}, bf16[1024,768]{1,0:T(8,128)(2,1)}, bf16[1024,768]{1,0:T(8,128)(2,1)}, bf16[1024,768]{1,0:T(8,128)(2,1)}, ...) custom-call(bf16[32,48,512]{2,1,0:T(8,128)(2,1)} %get-tuple-element., ...), custom_call_target="tpu_custom_call" | custom-call | tf_op jit(solution)/shard_map/layer_forward/pallas_call | solution.py:1273
  166.3 0.9 slice.23
  167.6 0.8 broadcast_in_dim.71.negative_ref
  169.1 14.2 %loss.1 = (f32[16,768]{1,0:T(8,128)}, f32[8,128]{1,0:T(8,128)}) custom-call(bf16[16,768]{1,0:T(8,128)(2,1)} %get-tuple-element.60.embeds_ref, s32[512,128]{1,0:T(8,128)} %broadcast_in_dim.71.negative_ref, f32[1,1]{1,0:T(1,128)} %bitcast.65.scale_ref), custom_call_target="tpu_custom_call" | custom-call | tf_op jit(solution)/shard_map/loss/pallas_call | solution.py:1908
  183.3 51.9 %feed_backward.1 = (bf16[768,3072]{1,0:T(8,128)(2,1)}, bf16[768,3072]{1,0:T(8,128)(2,1)}, f32[1024,768]{1,0:T(8,128)}, bf16[16,768]{1,0:T(8,128)(2,1)}, f32[8,768]{1,0:T(8,128)}) custom-call(f32[16,768]{1,0:T(8,128)} %get-tuple-element.62.grad_embed_ref, f32[16,768]{1,0:T(8,128)} %get-tuple-element.63.embed_ref, f32[16,128]{1,0:T(8,128)} %get-tuple-element.64.inverse_ref, ...), custom_call_target="tpu_custom_call" | custom-call | tf_op jit(solution)/shard_map/feed_backward/pallas_call | solution.py:1362
  235.2 158.1 %back.1 = (f32[2,5,48,192]{3,2,1,0:T(8,128)}, f32[96,768]{1,0:T(8,128)}, f32[192,384]{1,0:T(8,128)}, f32[12,128,128]{2,1,0:T(8,128)}, f32[8,768]{1,0:T(8,128)}, /*index=5*/f32[8,128]{1,0:T(8,128)}, f32[24,32128]{1,0:T(8,128)}) custom-call(f32[1024,768]{1,0:T(8,128)} %get-tuple-element.68.refs_0_, bf16[16,768]{1,0:T(8,128)(2,1)} %get-tuple-element.69.refs_1_, ...), custom_call_target="tpu_custom_call" | custom-call | tf_op jit(solution)/shard_map/back/pallas_call | solution.py:1725
  393.3 1.4 pad.39
  395.4 1.8 fusion.29
  397.9 1.3 slice.24.scale_ref
  399.7 15.4 %total.1 = (f32[24,128]{1,0:T(8,128)}, f32[8,128]{1,0:T(8,128)}) custom-call(f32[8,768]{1,0:T(8,128)} %get-tuple-element.79.first_gain, f32[8,768]{1,0:T(8,128)} %get-tuple-element.80.late_gains, f32[3,128]{1,0:T(4,128)} %reshape.254.position_ref, f32[8,128]{1,0:T(8,128)} %broadcast_in_dim.72.table_squares, f32[8,128]{1,0:T(8,128)} %get-tuple-element.82.layer_squares, ...), custom_call_target="tpu_custom_call" | custom-call | tf_op jit(solution)/shard_map/total/pallas_call | solution.py:1842
  415.1 1.2 slice.25
  422.0 2.3 multiply_subtract_fusion.2
  424.4 2.4 multiply_subtract_fusion.3
  426.8 1.2 multiply_bitcast_fusion
  428.0 2.7 multiply_subtract_fusion.1
  430.8 4.8 %multiply_subtract_fusion = (f32[24,32128]{1,0:T(8,128)}, f32[24,32128]{1,0:T(8,128)}, f32[24,32128]{1,0:T(8,128)}) fusion(f32[24,32128]{1,0:T(8,128)S(1)} %copy-done, f32[24,32128]{1,0:T(8,128)S(1)} %copy-done.5, f32[]{:T(128)} %min_shard_map.3, f32[24,32128]{1,0:T(8,128)S(1)} %copy-done.3, f32[24,32128]{1,0:T(8,128)S(1)} %copy-done.4), kind=kLoop, calls=%fused_computation.12 | loop fusion | flops 12337152 | bytes 21590020 | tf_op jit(solution)/shard_map/sub | solution.py:80
  435.6 1.2 slice_bitcast_fusion
  (73 shorter events, 9.8 us)
Async XLA Ops:
  0.7 99.1 %copy-start.14 = (s32[1024]{0:T(1024)S(1)}, s32[1024]{0:T(1024)}, u32[]{:S(2)}) copy-start(s32[1024]{0:T(1024)} %constant.224) | copy-start | bytes 12292
  0.7 99.1 %copy-start.10 = (pred[16,1024]{1,0:T(8,128)(4,1)S(1)}, pred[16,1024]{1,0:T(8,128)(4,1)}, u32[]{:S(2)}) copy-start(pred[16,1024]{1,0:T(8,128)(4,1)} %constant.93.clone) | copy-start | bytes 49156
  0.7 99.8 %copy-start.8 = (pred[8,128,128]{2,1,0:T(32,128)(4,1)S(1)}, pred[8,128,128]{2,1,0:T(32,128)(4,1)}, u32[]{:S(2)}) copy-start(pred[8,128,128]{2,1,0:T(32,128)(4,1)} %constant.94.clone) | copy-start | bytes 393220
  0.7 98.9 %copy-start.18 = (s32[4]{0:T(128)S(1)}, s32[4]{0:T(128)}, u32[]{:S(2)}) copy-start(s32[4]{0:T(128)} %param.55) | copy-start | bytes 52
  0.7 98.9 %copy-start.17 = (s32[4]{0:T(128)S(1)}, s32[4]{0:T(128)}, u32[]{:S(2)}) copy-start(s32[4]{0:T(128)} %param.56) | copy-start | bytes 52
  9.1 92.9 %copy-start.1 = (f32[16384,32]{0,1:T(8,128)S(1)}, f32[16384,32]{0,1:T(8,128)}, u32[]{:S(2)}) copy-start(f32[16384,32]{0,1:T(8,128)} %constant.95.clone) | copy-start | bytes 6291460
  9.1 92.9 %copy-start.9 = (f32[32,12]{0,1:T(8,128)S(1)}, f32[32,12]{0,1:T(8,128)}, u32[]{:S(2)}) copy-start(f32[32,12]{0,1:T(8,128)} %param.37) | copy-start | bytes 4612
  102.0 2.4 copy-start.6
  393.3 2.1 copy-start.2
  394.7 25.2 %copy-start.11 = (f32[32,12]{0,1:T(8,128)S(1)}, f32[32,12]{0,1:T(8,128)}, u32[]{:S(2)}) copy-start(f32[32,12]{0,1:T(8,128)} %param.50) | copy-start | bytes 4612
  394.7 25.2 %copy-start.12 = (f32[32,12]{0,1:T(8,128)S(1)}, f32[32,12]{0,1:T(8,128)}, u32[]{:S(2)}) copy-start(f32[32,12]{0,1:T(8,128)} %param.49) | copy-start | bytes 4612
  394.7 26.6 %copy-start.13 = (f32[3,24]{1,0:T(4,128)S(1)}, f32[3,24]{1,0:T(4,128)}, u32[]{:S(2)}) copy-start(f32[3,24]{1,0:T(4,128)} %param.36) | copy-start | bytes 868
  394.7 26.6 %copy-start.15 = (f32[3,24]{1,0:T(4,128)S(1)}, f32[3,24]{1,0:T(4,128)}, u32[]{:S(2)}) copy-start(f32[3,24]{1,0:T(4,128)} %param.48) | copy-start | bytes 868
  394.7 26.6 %copy-start.16 = (f32[3,24]{1,0:T(4,128)S(1)}, f32[3,24]{1,0:T(4,128)}, u32[]{:S(2)}) copy-start(f32[3,24]{1,0:T(4,128)} %param.47) | copy-start | bytes 868
  394.8 27.3 %copy-start.7 = (f32[384,192]{0,1:T(8,128)S(1)}, f32[384,192]{0,1:T(8,128)}, u32[]{:S(2)}) copy-start(f32[384,192]{0,1:T(8,128)} %param.35) | copy-start | bytes 884740
  395.4 35.3 %copy-start.5 = (f32[24,32128]{1,0:T(8,128)S(1)}, f32[24,32128]{1,0:T(8,128)}, u32[]{:S(2)}) copy-start(f32[24,32128]{1,0:T(8,128)} %get-tuple-element.78) | copy-start | bytes 9252868
  422.0 8.7 %copy-start.4 = (f32[24,32128]{1,0:T(8,128)S(1)}, f32[24,32128]{1,0:T(8,128)}, u32[]{:S(2)}) copy-start(f32[24,32128]{1,0:T(8,128)} %param.39) | copy-start | bytes 9252868
  424.4 6.4 %copy-start.3 = (f32[24,32128]{1,0:T(8,128)S(1)}, f32[24,32128]{1,0:T(8,128)}, u32[]{:S(2)}) copy-start(f32[24,32128]{1,0:T(8,128)} %param.40) | copy-start | bytes 9252868
  426.8 4.0 copy-start
